TPU v7x, 32 devices: a whole 2x2x4 slice. The times are simulated.
32 devices in a mesh: px: 4 (over x, core), py: 8 (over z, y).
Axes of the slice: x: 2, y: 2, z: 4, core: 2. Of those that a mesh axis runs over, the one named last changes fastest.
Arguments:
- field: float32 [5, 32, 128, 128], P(None, 'px', 'py'), may hold values from -6 to 6
- forcing: float32 [5, 32, 128, 128], P(None, 'px', 'py'), may hold values from -6 to 6
- x_inverse: float32 [5, 5, 32, 128, 128], P(None, None, 'px', 'py'), may hold values from -1 to 1
- x_lower: float32 [5, 5, 32, 128, 128], P(None, None, 'px', 'py'), may hold values from -1 to 1
- x_upper: float32 [5, 5, 32, 128, 128], P(None, None, 'px', 'py'), may hold values from -1 to 1
- y_inverse: float32 [5, 5, 32, 128, 128], P(None, None, 'px', 'py'), may hold values from -1 to 1
- y_lower: float32 [5, 5, 32, 128, 128], P(None, None, 'px', 'py'), may hold values from -1 to 1
- y_upper: float32 [5, 5, 32, 128, 128], P(None, None, 'px', 'py'), may hold values from -1 to 1
Outputs:
- update: float32 [5, 32, 128, 128], P(None, 'px', 'py')
All inputs are finite; a program needn't handle non-finite values.
Results may differ from a plain program's by a relative error of at most 0.00014.
Values sent between devices are 32-bit elements; how exact they have to be, the bound alone decides.
No kernel may reach another device: no remote copies, remote signals or barrier semaphores. Data moves between devices by JAX's collectives and lax.ppermute only.
A program may use at most 64 MiB of HBM per device.

v0:
```python
import jax
import jax.numpy as jnp
from jax import lax
from jax.sharding import PartitionSpec as P

DISSIPATION = 0.1


def from_behind(value, axis, steps):
    count = lax.axis_size(axis)
    first, last = (max(0, -steps), min(count, count - steps))
    return lax.ppermute(value, axis, [(source, source + steps) for source in range(first, last)])


def extended(shard, sides, width):
    for axis, dim in sides:
        devices, length = (lax.axis_size(axis), shard.shape[dim])
        up = [(i, (i + 1) % devices) for i in range(devices - 1)]
        down = [(j, i) for i, j in up]
        last = lax.slice_in_dim(shard, length - width, length, axis=dim)
        first = lax.slice_in_dim(shard, 0, width, axis=dim)
        before = lax.ppermute(last, axis, up)
        after = lax.ppermute(first, axis, down)
        shard = jnp.concatenate([before, shard, after], axis=dim)
    return shard


def apply_block(blocks, vector):
    return jnp.sum(blocks * vector[None], axis=1)


def block_product(later, earlier):
    return jnp.sum(later[:, :, None] * earlier[None, :, :], axis=1)


def compose_cells(source, coupling, line_axis, backward):
    length = source.shape[line_axis]
    start = jnp.zeros(source.shape[:line_axis] + source.shape[line_axis + 1 :], jnp.float32)
    unit_matrix = jnp.eye(source.shape[0], dtype=jnp.float32)[:, :, None, None]
    start_matrix = jnp.broadcast_to(
        unit_matrix, (source.shape[0], source.shape[0]) + start.shape[1:]
    )

    def compose_advance(i, carried):
        matrix, vector = carried
        k = length - 1 - i if backward else i
        here = lax.dynamic_index_in_dim(coupling, k, line_axis + 1, keepdims=False)
        inflow = lax.dynamic_index_in_dim(source, k, line_axis, keepdims=False)
        return (-block_product(here, matrix), inflow - apply_block(here, vector))

    return lax.fori_loop(0, length, compose_advance, (start_matrix, start))


def run_cells(source, coupling, inflow, line_axis, backward):
    length = source.shape[line_axis]

    def run_advance(i, carried):
        before, result = carried
        k = length - 1 - i if backward else i
        here = lax.dynamic_index_in_dim(coupling, k, line_axis + 1, keepdims=False)
        current = lax.dynamic_index_in_dim(source, k, line_axis, keepdims=False) - apply_block(
            here, before
        )
        return (current, lax.dynamic_update_index_in_dim(result, current, k, line_axis))

    return lax.fori_loop(0, length, run_advance, (inflow, jnp.zeros_like(source)))[1]


def carry_x_forward(matrix, vector):

    def relay_step(i, inflow):
        return from_behind(apply_block(matrix, inflow) + vector, "px", 1)

    return lax.fori_loop(0, lax.axis_size("px") - 1, relay_step, jnp.zeros_like(vector))


def carry_x_backward(matrix, vector):

    def relay_step(i, inflow):
        return from_behind(apply_block(matrix, inflow) + vector, "px", -1)

    return lax.fori_loop(0, lax.axis_size("px") - 1, relay_step, jnp.zeros_like(vector))


def carry_y_forward(matrix, vector):

    def relay_step(i, inflow):
        return from_behind(apply_block(matrix, inflow) + vector, "py", 1)

    return lax.fori_loop(0, lax.axis_size("py") - 1, relay_step, jnp.zeros_like(vector))


def carry_y_backward(matrix, vector):

    def relay_step(i, inflow):
        return from_behind(apply_block(matrix, inflow) + vector, "py", -1)

    return lax.fori_loop(0, lax.axis_size("py") - 1, relay_step, jnp.zeros_like(vector))


def per_device(field, forcing, x_inverse, x_lower, x_upper, y_inverse, y_lower, y_upper):
    cells_x = field.shape[1]
    cells_y = field.shape[2]
    padded = extended(field, (("px", 1), ("py", 2)), 2)

    def window_x(k):
        return padded[:, k : k + cells_x, 2 : 2 + cells_y]

    def window_y(k):
        return padded[:, 2 : 2 + cells_x, k : k + cells_y]

    along_x = window_x(0) - 4.0 * window_x(1) + 6.0 * window_x(2) - 4.0 * window_x(3) + window_x(4)
    along_y = window_y(0) - 4.0 * window_y(1) + 6.0 * window_y(2) - 4.0 * window_y(3) + window_y(4)
    rhs = forcing - DISSIPATION * (along_x + along_y)
    source = apply_block(x_inverse, rhs)
    matrix, vector = compose_cells(source, x_lower, 1, False)
    inflow = carry_x_forward(matrix, vector)
    forward = run_cells(source, x_lower, inflow, 1, False)
    matrix, vector = compose_cells(forward, x_upper, 1, True)
    inflow = carry_x_backward(matrix, vector)
    x_result = run_cells(forward, x_upper, inflow, 1, True)
    source = apply_block(y_inverse, x_result)
    matrix, vector = compose_cells(source, y_lower, 2, False)
    inflow = carry_y_forward(matrix, vector)
    forward = run_cells(source, y_lower, inflow, 2, False)
    matrix, vector = compose_cells(forward, y_upper, 2, True)
    inflow = carry_y_backward(matrix, vector)
    return run_cells(forward, y_upper, inflow, 2, True)


def solution(mesh):
    in_specs = (
        P(None, "px", "py", None),
        P(None, "px", "py", None),
        P(None, None, "px", "py", None),
        P(None, None, "px", "py", None),
        P(None, None, "px", "py", None),
        P(None, None, "px", "py", None),
        P(None, None, "px", "py", None),
        P(None, None, "px", "py", None),
    )
    out_specs = P(None, "px", "py", None)
    return jax.shard_map(
        per_device, mesh=mesh, in_specs=in_specs, out_specs=out_specs, check_vma=False
    )
```

profile of v0, /device:TPU:6, one launch (start us, length us, event | category | flops | bytes accessed | tf_op | source)
XLA Modules:
  0.0 268.6 jit_solution(1170099722776919934)
XLA Ops:
  15.6 4.3 %collective-permute-done.7 = f32[5,12,2,128]{3,2,1,0:T(2,128)S(1)} collective-permute-done((f32[5,12,2,128]{3,2,1,0:T(2,128)}, f32[5,12,2,128]{3,2,1,0:T(2,128)S(1)}, u32[]{:S(2)}, u32[]{:S(2)}) %collective-permute-start.7) | collective-permute-done | bytes 61472 | tf_op jit(solution)/shard_map/ppermute | solution.py:23
  21.6 9.0 %while.180 = (s32[]{:T(128)}, f32[5,5,16,128]{3,2,1,0:T(8,128)S(1)}, f32[5,16,128]{2,1,0:T(8,128)S(1)}, f32[5,5,8,16,128]{4,3,2,1,0:T(8,128)}, f32[5,8,16,128]{3,2,1,0:T(8,128)S(1)}, /*index=5*/s32[]{:T(128)}, s32[]{:T(128)}) while((s32[]{:T(128)}, f32[5,5,16,128]{3,2,1,0:T(8,128)S(1)}, f32[5,16,128]{2,1,0:T(8,128)S(1)}, ...), condition=%wide.region_4.5_spmd.clone, body=%wide.region_1.4_spmd.clone.sunk | while | flops 624643 | bytes 1720415 | solution.py:51
  30.6 16.1 %while.172 = (s32[]{:T(128)}, f32[5,16,128]{2,1,0:T(8,128)S(1)}, f32[5,5,16,128]{3,2,1,0:T(8,128)S(1)}, f32[5,16,128]{2,1,0:T(8,128)S(1)}, s32[]{:T(128)}) while((s32[]{:T(128)}, f32[5,16,128]{2,1,0:T(8,128)S(1)}, f32[5,5,16,128]{3,2,1,0:T(8,128)S(1)}, f32[5,16,128]{2,1,0:T(8,128)S(1)}, s32[]{:T(128)}) %tuple.314), condition=%wide.region_7.8_spmd, body=%wide.region_5.7_spmd.sunk | while | flops 102402 | bytes 573541 | solution.py:74
  46.7 8.2 %while.173 = (s32[]{:T(128)}, f32[5,16,128]{2,1,0:T(8,128)S(1)}, f32[5,8,16,128]{3,2,1,0:T(8,128)S(1)}, f32[5,8,16,128]{3,2,1,0:T(8,128)S(1)}, f32[5,5,8,16,128]{4,3,2,1,0:T(8,128)}, /*index=5*/s32[]{:T(128)}) while((s32[]{:T(128)}, f32[5,16,128]{2,1,0:T(8,128)S(1)}, f32[5,8,16,128]{3,2,1,0:T(8,128)S(1)}, f32[5,8,16,128]{3,2,1,0:T(8,128)S(1)}, ...), condition=%wide.region_10.11_spmd, body=%wide.region_8.10_spmd.sunk | while | flops 112642 | bytes 532561 | solution.py:66
  55.0 9.2 %while.181 = (s32[]{:T(128)}, f32[5,5,16,128]{3,2,1,0:T(8,128)S(1)}, f32[5,16,128]{2,1,0:T(8,128)S(1)}, f32[5,5,8,16,128]{4,3,2,1,0:T(8,128)}, f32[5,8,16,128]{3...) while((s32[]{:T(128)}, f32[5,5,16,128]{3,2,1,0:T(8,128)S(1)}, ...), condition=%wide.region_14.15_spmd.clone, body=%wide.region_11.14_spmd.clone.sunk | while | flops 624647 | bytes 1720477 | solution.py:51
  64.2 14.4 %while.174 = (s32[]{:T(128)}, f32[5,16,128]{2,1,0:T(8,128)S(1)}, f32[5,5,16,128]{3,2,1,0:T(8,128)S(1)}, f32[5,16,128]{2,1,0:T(8,128)S(1)}, s32[]{:T(128)}) while((s32[]{:T(128)}, f32[5,16,128]{2,1,0:T(8,128)S(1)}, f32[5,5,16,128]{3,2,1,0:T(8,128)S(1)}, f32[5,16,128]{2,1,0:T(8,128)S(1)}, s32[]{:T(128)}) %tuple.323), condition=%wide.region_17.18_spmd, body=%wide.region_15.17_spmd.sunk | while | flops 102402 | bytes 573541 | solution.py:82
  78.6 8.2 %while.175 = (s32[]{:T(128)}, f32[5,16,128]{2,1,0:T(8,128)S(1)}, f32[5,8,16,128]{3,2,1,0:T(8,128)S(1)}, f32[5,8,16,128]{3,2,1,0:T(8,128)S(1)}, f32[5,5,8,16,128]...) while((s32[]{:T(128)}, f32[5,16,128]{2,1,0:T(8,128)S(1)}, ...), condition=%wide.region_20.21_spmd, body=%wide.region_18.20_spmd.sunk | while | flops 112646 | bytes 532631 | solution.py:66
  87.1 22.2 %while.182 = (s32[]{:T(128)}, f32[5,5,8,128]{3,2,1,0:T(8,128)S(1)}, f32[5,8,128]{2,1,0:T(8,128)S(1)}, f32[5,5,8,16,128]{4,3,2,1,0:T(8,128)}, f32[5,8,16,128]{3,2,1,0:T(8,128)S(1)}, /*index=5*/s32[]{:T(128)}, s32[]{:T(128)}) while((s32[]{:T(128)}, f32[5,5,8,128]{3,2,1,0:T(8,128)S(1)}, f32[5,8,128]{2,1,0:T(8,128)S(1)}, ...), condition=%wide.region_25.26_spmd.clone, body=%wide.region_22.25_spmd.clone.sunk | while | flops 312323 | bytes 1003615 | solution.py:51
  109.3 43.7 %while.176 = (s32[]{:T(128)}, f32[5,8,128]{2,1,0:T(8,128)S(1)}, f32[5,5,8,128]{3,2,1,0:T(8,128)S(1)}, f32[5,8,128]{2,1,0:T(8,128)S(1)}, s32[]{:T(128)}) while((s32[]{:T(128)}, f32[5,8,128]{2,1,0:T(8,128)S(1)}, f32[5,5,8,128]{3,2,1,0:T(8,128)S(1)}, f32[5,8,128]{2,1,0:T(8,128)S(1)}, s32[]{:T(128)}) %tuple.332), condition=%wide.region_28.29_spmd, body=%wide.region_26.28_spmd.sunk | while | flops 51202 | bytes 286821 | solution.py:90
  126.6 5.2 %collective-permute-start.2 = (f32[5,8,128]{2,1,0:T(8,128)S(1)}, f32[5,8,128]{2,1,0:T(8,128)S(1)}, u32[]{:S(2)}, u32[]{:S(2)}) collective-permute-start(f32[5,8,128]{2,1,0:T(8,128)S(1)} %add.327), channel_id=1, source_target_pairs={{0,1},{1,2},{2,3},{3,4},{4,5},{5,6},{6,7},{8,9},{9,10},{10,11},{11... | collective-permute-start | bytes 61448 | tf_op jit(solution)/shard_map/while/body/eval_jaxpr/ppermute | solution.py:12
  133.3 5.1 %collective-permute-start.2 = (f32[5,8,128]{2,1,0:T(8,128)S(1)}, f32[5,8,128]{2,1,0:T(8,128)S(1)}, u32[]{:S(2)}, u32[]{:S(2)}) collective-permute-start(f32[5,8,128]{2,1,0:T(8,128)S(1)} %add.327), channel_id=1, source_target_pairs={{0,1},{1,2},{2,3},{3,4},{4,5},{5,6},{6,7},{8,9},{9,10},{10,11},{11... | collective-permute-start | bytes 61448 | tf_op jit(solution)/shard_map/while/body/eval_jaxpr/ppermute | solution.py:12
  139.9 5.1 %collective-permute-start.2 = (f32[5,8,128]{2,1,0:T(8,128)S(1)}, f32[5,8,128]{2,1,0:T(8,128)S(1)}, u32[]{:S(2)}, u32[]{:S(2)}) collective-permute-start(f32[5,8,128]{2,1,0:T(8,128)S(1)} %add.327), channel_id=1, source_target_pairs={{0,1},{1,2},{2,3},{3,4},{4,5},{5,6},{6,7},{8,9},{9,10},{10,11},{11... | collective-permute-start | bytes 61448 | tf_op jit(solution)/shard_map/while/body/eval_jaxpr/ppermute | solution.py:12
  146.5 5.1 %collective-permute-start.2 = (f32[5,8,128]{2,1,0:T(8,128)S(1)}, f32[5,8,128]{2,1,0:T(8,128)S(1)}, u32[]{:S(2)}, u32[]{:S(2)}) collective-permute-start(f32[5,8,128]{2,1,0:T(8,128)S(1)} %add.327), channel_id=1, source_target_pairs={{0,1},{1,2},{2,3},{3,4},{4,5},{5,6},{6,7},{8,9},{9,10},{10,11},{11... | collective-permute-start | bytes 61448 | tf_op jit(solution)/shard_map/while/body/eval_jaxpr/ppermute | solution.py:12
  153.1 22.8 %while.177 = (s32[]{:T(128)}, f32[5,8,128]{2,1,0:T(8,128)S(1)}, f32[5,8,16,128]{3,2,1,0:T(8,128)S(1)}, f32[5,8,16,128]{3,2,1,0:T(8,128)S(1)}, f32[5,5,8,16,128]{4,3,2,1,0:T(8,128)}, /*index=5*/s32[]{:T(128)}, s32[]{:T(128)}) while((s32[]{:T(128)}, f32[5,8,128]{2,1,0:T(8,128)S(1)}, f32[5,8,16,128]{3,2,1,0:T(8,128)S(1)}, ...), condition=%wide.region_31.32_spmd, body=%wide.region_29.31_spmd.sunk | while | flops 56322 | bytes 532569 | solution.py:66
  176.0 22.3 %while.183 = (s32[]{:T(128)}, f32[5,5,8,128]{3,2,1,0:T(8,128)S(1)}, f32[5,8,128]{2,1,0:T(8,128)S(1)}, f32[5,5,8,16,128]{4,3,2,1,0:T(8,128)}, f32[5,8,16,128]{3,2...) while((s32[]{:T(128)}, f32[5,5,8,128]{3,2,1,0:T(8,128)S(1)}, ...), condition=%wide.region_35.36_spmd.clone, body=%wide.region_32.35_spmd.clone.sunk | while | flops 312327 | bytes 1003677 | solution.py:51
  198.3 46.5 %while.178 = (s32[]{:T(128)}, f32[5,8,128]{2,1,0:T(8,128)S(1)}, f32[5,5,8,128]{3,2,1,0:T(8,128)S(1)}, f32[5,8,128]{2,1,0:T(8,128)S(1)}, s32[]{:T(128)}) while((s32[]{:T(128)}, f32[5,8,128]{2,1,0:T(8,128)S(1)}, f32[5,5,8,128]{3,2,1,0:T(8,128)S(1)}, f32[5,8,128]{2,1,0:T(8,128)S(1)}, s32[]{:T(128)}) %tuple.341), condition=%wide.region_38.39_spmd, body=%wide.region_36.38_spmd.sunk | while | flops 51202 | bytes 286821 | solution.py:98
  200.3 4.9 %collective-permute-done.3 = f32[5,8,128]{2,1,0:T(8,128)S(1)} collective-permute-done((f32[5,8,128]{2,1,0:T(8,128)S(1)}, f32[5,8,128]{2,1,0:T(8,128)S(1)}, u32[]{:S(2)}, u32[]{:S(2)}) %collective-permute-start.3) | collective-permute-done | bytes 20512 | tf_op jit(solution)/shard_map/while/body/eval_jaxpr/ppermute | solution.py:12
  207.2 4.6 %collective-permute-done.3 = f32[5,8,128]{2,1,0:T(8,128)S(1)} collective-permute-done((f32[5,8,128]{2,1,0:T(8,128)S(1)}, f32[5,8,128]{2,1,0:T(8,128)S(1)}, u32[]{:S(2)}, u32[]{:S(2)}) %collective-permute-start.3) | collective-permute-done | bytes 20512 | tf_op jit(solution)/shard_map/while/body/eval_jaxpr/ppermute | solution.py:12
  213.8 4.6 %collective-permute-done.3 = f32[5,8,128]{2,1,0:T(8,128)S(1)} collective-permute-done((f32[5,8,128]{2,1,0:T(8,128)S(1)}, f32[5,8,128]{2,1,0:T(8,128)S(1)}, u32[]{:S(2)}, u32[]{:S(2)}) %collective-permute-start.3) | collective-permute-done | bytes 20512 | tf_op jit(solution)/shard_map/while/body/eval_jaxpr/ppermute | solution.py:12
  220.4 4.6 %collective-permute-done.3 = f32[5,8,128]{2,1,0:T(8,128)S(1)} collective-permute-done((f32[5,8,128]{2,1,0:T(8,128)S(1)}, f32[5,8,128]{2,1,0:T(8,128)S(1)}, u32[]{:S(2)}, u32[]{:S(2)}) %collective-permute-start.3) | collective-permute-done | bytes 20512 | tf_op jit(solution)/shard_map/while/body/eval_jaxpr/ppermute | solution.py:12
  227.0 4.6 %collective-permute-done.3 = f32[5,8,128]{2,1,0:T(8,128)S(1)} collective-permute-done((f32[5,8,128]{2,1,0:T(8,128)S(1)}, f32[5,8,128]{2,1,0:T(8,128)S(1)}, u32[]{:S(2)}, u32[]{:S(2)}) %collective-permute-start.3) | collective-permute-done | bytes 20512 | tf_op jit(solution)/shard_map/while/body/eval_jaxpr/ppermute | solution.py:12
  233.6 4.6 %collective-permute-done.3 = f32[5,8,128]{2,1,0:T(8,128)S(1)} collective-permute-done((f32[5,8,128]{2,1,0:T(8,128)S(1)}, f32[5,8,128]{2,1,0:T(8,128)S(1)}, u32[]{:S(2)}, u32[]{:S(2)}) %collective-permute-start.3) | collective-permute-done | bytes 20512 | tf_op jit(solution)/shard_map/while/body/eval_jaxpr/ppermute | solution.py:12
  240.2 4.6 %collective-permute-done.3 = f32[5,8,128]{2,1,0:T(8,128)S(1)} collective-permute-done((f32[5,8,128]{2,1,0:T(8,128)S(1)}, f32[5,8,128]{2,1,0:T(8,128)S(1)}, u32[]{:S(2)}, u32[]{:S(2)}) %collective-permute-start.3) | collective-permute-done | bytes 20512 | tf_op jit(solution)/shard_map/while/body/eval_jaxpr/ppermute | solution.py:12
  244.9 23.0 %while.179 = (s32[]{:T(128)}, f32[5,8,128]{2,1,0:T(8,128)S(1)}, f32[5,8,16,128]{3,2,1,0:T(8,128)S(1)}, f32[5,8,16,128]{3,2,1,0:T(8,128)S(1)}, f32[5,5,8,16,128]{...) while((s32[]{:T(128)}, f32[5,8,128]{2,1,0:T(8,128)S(1)}, ...), condition=%wide.region_41.42_spmd, body=%wide.region_39.41_spmd.sunk | while | flops 56326 | bytes 532631 | solution.py:66
  (621 shorter events, 205.0 us)
Async XLA Ops:
  1.0 5.8 %collective-permute-start.4 = (f32[5,2,16,128]{3,2,1,0:T(8,128)S(1)}, f32[5,2,16,128]{3,2,1,0:T(8,128)S(1)}, u32[]{:S(2)}, u32[]{:S(2)}) collective-permute-start(f32[5,2,16,128]{3,2,1,0:T(8,128)S(1)} %get-tuple-element.1235), channel_id=1, source_target_pairs={{0,8},{8,16},{16,24},{1,9},{9,17},{17,25},{2,10},{10,18},{18,26},{... | collective-permute-start | bytes 245768 | tf_op jit(solution)/shard_map/ppermute | solution.py:22
  2.9 5.7 %collective-permute-start.5 = (f32[5,2,16,128]{3,2,1,0:T(8,128)S(1)}, f32[5,2,16,128]{3,2,1,0:T(8,128)S(1)}, u32[]{:S(2)}, u32[]{:S(2)}) collective-permute-start(f32[5,2,16,128]{3,2,1,0:T(8,128)S(1)} %get-tuple-element.1234), channel_id=1, source_target_pairs={{8,0},{16,8},{24,16},{9,1},{17,9},{25,17},{10,2},{18,10},{26,18},{... | collective-permute-start | bytes 245768 | tf_op jit(solution)/shard_map/ppermute | solution.py:23
  9.3 6.3 %collective-permute-start.6 = (f32[5,12,2,128]{3,2,1,0:T(2,128)}, f32[5,12,2,128]{3,2,1,0:T(2,128)S(1)}, u32[]{:S(2)}, u32[]{:S(2)}) collective-permute-start(f32[5,12,2,128]{3,2,1,0:T(2,128)} %get-tuple-element.1229), channel_id=1, source_target_pairs={{0,1},{1,2},{2,3},{3,4},{4,5},{5,6},{6,7},{8,9},{9,10},{10,11},{11... | collective-permute-start | bytes 184328 | tf_op jit(solution)/shard_map/ppermute | solution.py:22
  12.7 7.2 %collective-permute-start.7 = (f32[5,12,2,128]{3,2,1,0:T(2,128)}, f32[5,12,2,128]{3,2,1,0:T(2,128)S(1)}, u32[]{:S(2)}, u32[]{:S(2)}) collective-permute-start(f32[5,12,2,128]{3,2,1,0:T(2,128)} %get-tuple-element.1230), channel_id=1, source_target_pairs={{1,0},{2,1},{3,2},{4,3},{5,4},{6,5},{7,6},{9,8},{10,9},{11,10},{12... | collective-permute-start | bytes 184328 | tf_op jit(solution)/shard_map/ppermute | solution.py:23
  30.7 5.3 %collective-permute-start = (f32[5,16,128]{2,1,0:T(8,128)S(1)}, f32[5,16,128]{2,1,0:T(8,128)S(1)}, u32[]{:S(2)}, u32[]{:S(2)}) collective-permute-start(f32[5,16,128]{2,1,0:T(8,128)S(1)} %add.320), channel_id=1, source_target_pairs={{0,8},{8,16},{16,24},{1,9},{9,17},{17,25},{2,10},{10,18},{18,26},{... | collective-permute-start | bytes 122888 | tf_op jit(solution)/shard_map/while/body/eval_jaxpr/ppermute | solution.py:12
  36.0 5.3 %collective-permute-start = (f32[5,16,128]{2,1,0:T(8,128)S(1)}, f32[5,16,128]{2,1,0:T(8,128)S(1)}, u32[]{:S(2)}, u32[]{:S(2)}) collective-permute-start(f32[5,16,128]{2,1,0:T(8,128)S(1)} %add.320), channel_id=1, source_target_pairs={{0,8},{8,16},{16,24},{1,9},{9,17},{17,25},{2,10},{10,18},{18,26},{... | collective-permute-start | bytes 122888 | tf_op jit(solution)/shard_map/while/body/eval_jaxpr/ppermute | solution.py:12
  41.4 5.3 %collective-permute-start = (f32[5,16,128]{2,1,0:T(8,128)S(1)}, f32[5,16,128]{2,1,0:T(8,128)S(1)}, u32[]{:S(2)}, u32[]{:S(2)}) collective-permute-start(f32[5,16,128]{2,1,0:T(8,128)S(1)} %add.320), channel_id=1, source_target_pairs={{0,8},{8,16},{16,24},{1,9},{9,17},{17,25},{2,10},{10,18},{18,26},{... | collective-permute-start | bytes 122888 | tf_op jit(solution)/shard_map/while/body/eval_jaxpr/ppermute | solution.py:12
  64.3 3.6 %collective-permute-start.1 = (f32[5,16,128]{2,1,0:T(8,128)S(1)}, f32[5,16,128]{2,1,0:T(8,128)S(1)}, u32[]{:S(2)}, u32[]{:S(2)}) collective-permute-start(f32[5,16,128]{2,1,0:T(8,128)S(1)} %add.323), channel_id=1, source_target_pairs={{8,0},{16,8},{24,16},{9,1},{17,9},{25,17},{10,2},{18,10},{26,18},{... | collective-permute-start | bytes 122888 | tf_op jit(solution)/shard_map/while/body/eval_jaxpr/ppermute | solution.py:12
  67.9 5.3 %collective-permute-start.1 = (f32[5,16,128]{2,1,0:T(8,128)S(1)}, f32[5,16,128]{2,1,0:T(8,128)S(1)}, u32[]{:S(2)}, u32[]{:S(2)}) collective-permute-start(f32[5,16,128]{2,1,0:T(8,128)S(1)} %add.323), channel_id=1, source_target_pairs={{8,0},{16,8},{24,16},{9,1},{17,9},{25,17},{10,2},{18,10},{26,18},{... | collective-permute-start | bytes 122888 | tf_op jit(solution)/shard_map/while/body/eval_jaxpr/ppermute | solution.py:12
  73.3 5.3 %collective-permute-start.1 = (f32[5,16,128]{2,1,0:T(8,128)S(1)}, f32[5,16,128]{2,1,0:T(8,128)S(1)}, u32[]{:S(2)}, u32[]{:S(2)}) collective-permute-start(f32[5,16,128]{2,1,0:T(8,128)S(1)} %add.323), channel_id=1, source_target_pairs={{8,0},{16,8},{24,16},{9,1},{17,9},{25,17},{10,2},{18,10},{26,18},{... | collective-permute-start | bytes 122888 | tf_op jit(solution)/shard_map/while/body/eval_jaxpr/ppermute | solution.py:12
  109.4 5.7 %collective-permute-start.2 = (f32[5,8,128]{2,1,0:T(8,128)S(1)}, f32[5,8,128]{2,1,0:T(8,128)S(1)}, u32[]{:S(2)}, u32[]{:S(2)}) collective-permute-start(f32[5,8,128]{2,1,0:T(8,128)S(1)} %add.327), channel_id=1, source_target_pairs={{0,1},{1,2},{2,3},{3,4},{4,5},{5,6},{6,7},{8,9},{9,10},{10,11},{11... | collective-permute-start | bytes 61448 | tf_op jit(solution)/shard_map/while/body/eval_jaxpr/ppermute | solution.py:12
  115.1 5.7 %collective-permute-start.2 = (f32[5,8,128]{2,1,0:T(8,128)S(1)}, f32[5,8,128]{2,1,0:T(8,128)S(1)}, u32[]{:S(2)}, u32[]{:S(2)}) collective-permute-start(f32[5,8,128]{2,1,0:T(8,128)S(1)} %add.327), channel_id=1, source_target_pairs={{0,1},{1,2},{2,3},{3,4},{4,5},{5,6},{6,7},{8,9},{9,10},{10,11},{11... | collective-permute-start | bytes 61448 | tf_op jit(solution)/shard_map/while/body/eval_jaxpr/ppermute | solution.py:12
  120.8 5.8 %collective-permute-start.2 = (f32[5,8,128]{2,1,0:T(8,128)S(1)}, f32[5,8,128]{2,1,0:T(8,128)S(1)}, u32[]{:S(2)}, u32[]{:S(2)}) collective-permute-start(f32[5,8,128]{2,1,0:T(8,128)S(1)} %add.327), channel_id=1, source_target_pairs={{0,1},{1,2},{2,3},{3,4},{4,5},{5,6},{6,7},{8,9},{9,10},{10,11},{11... | collective-permute-start | bytes 61448 | tf_op jit(solution)/shard_map/while/body/eval_jaxpr/ppermute | solution.py:12
  126.6 6.7 %collective-permute-start.2 = (f32[5,8,128]{2,1,0:T(8,128)S(1)}, f32[5,8,128]{2,1,0:T(8,128)S(1)}, u32[]{:S(2)}, u32[]{:S(2)}) collective-permute-start(f32[5,8,128]{2,1,0:T(8,128)S(1)} %add.327), channel_id=1, source_target_pairs={{0,1},{1,2},{2,3},{3,4},{4,5},{5,6},{6,7},{8,9},{9,10},{10,11},{11... | collective-permute-start | bytes 61448 | tf_op jit(solution)/shard_map/while/body/eval_jaxpr/ppermute | solution.py:12
  133.3 6.6 %collective-permute-start.2 = (f32[5,8,128]{2,1,0:T(8,128)S(1)}, f32[5,8,128]{2,1,0:T(8,128)S(1)}, u32[]{:S(2)}, u32[]{:S(2)}) collective-permute-start(f32[5,8,128]{2,1,0:T(8,128)S(1)} %add.327), channel_id=1, source_target_pairs={{0,1},{1,2},{2,3},{3,4},{4,5},{5,6},{6,7},{8,9},{9,10},{10,11},{11... | collective-permute-start | bytes 61448 | tf_op jit(solution)/shard_map/while/body/eval_jaxpr/ppermute | solution.py:12
  139.9 6.6 %collective-permute-start.2 = (f32[5,8,128]{2,1,0:T(8,128)S(1)}, f32[5,8,128]{2,1,0:T(8,128)S(1)}, u32[]{:S(2)}, u32[]{:S(2)}) collective-permute-start(f32[5,8,128]{2,1,0:T(8,128)S(1)} %add.327), channel_id=1, source_target_pairs={{0,1},{1,2},{2,3},{3,4},{4,5},{5,6},{6,7},{8,9},{9,10},{10,11},{11... | collective-permute-start | bytes 61448 | tf_op jit(solution)/shard_map/while/body/eval_jaxpr/ppermute | solution.py:12
  146.5 6.6 %collective-permute-start.2 = (f32[5,8,128]{2,1,0:T(8,128)S(1)}, f32[5,8,128]{2,1,0:T(8,128)S(1)}, u32[]{:S(2)}, u32[]{:S(2)}) collective-permute-start(f32[5,8,128]{2,1,0:T(8,128)S(1)} %add.327), channel_id=1, source_target_pairs={{0,1},{1,2},{2,3},{3,4},{4,5},{5,6},{6,7},{8,9},{9,10},{10,11},{11... | collective-permute-start | bytes 61448 | tf_op jit(solution)/shard_map/while/body/eval_jaxpr/ppermute | solution.py:12
  198.4 6.9 %collective-permute-start.3 = (f32[5,8,128]{2,1,0:T(8,128)S(1)}, f32[5,8,128]{2,1,0:T(8,128)S(1)}, u32[]{:S(2)}, u32[]{:S(2)}) collective-permute-start(f32[5,8,128]{2,1,0:T(8,128)S(1)} %add.330), channel_id=1, source_target_pairs={{1,0},{2,1},{3,2},{4,3},{5,4},{6,5},{7,6},{9,8},{10,9},{11,10},{12... | collective-permute-start | bytes 61448 | tf_op jit(solution)/shard_map/while/body/eval_jaxpr/ppermute | solution.py:12
  205.3 6.6 %collective-permute-start.3 = (f32[5,8,128]{2,1,0:T(8,128)S(1)}, f32[5,8,128]{2,1,0:T(8,128)S(1)}, u32[]{:S(2)}, u32[]{:S(2)}) collective-permute-start(f32[5,8,128]{2,1,0:T(8,128)S(1)} %add.330), channel_id=1, source_target_pairs={{1,0},{2,1},{3,2},{4,3},{5,4},{6,5},{7,6},{9,8},{10,9},{11,10},{12... | collective-permute-start | bytes 61448 | tf_op jit(solution)/shard_map/while/body/eval_jaxpr/ppermute | solution.py:12
  211.9 6.6 %collective-permute-start.3 = (f32[5,8,128]{2,1,0:T(8,128)S(1)}, f32[5,8,128]{2,1,0:T(8,128)S(1)}, u32[]{:S(2)}, u32[]{:S(2)}) collective-permute-start(f32[5,8,128]{2,1,0:T(8,128)S(1)} %add.330), channel_id=1, source_target_pairs={{1,0},{2,1},{3,2},{4,3},{5,4},{6,5},{7,6},{9,8},{10,9},{11,10},{12... | collective-permute-start | bytes 61448 | tf_op jit(solution)/shard_map/while/body/eval_jaxpr/ppermute | solution.py:12
  218.5 6.6 %collective-permute-start.3 = (f32[5,8,128]{2,1,0:T(8,128)S(1)}, f32[5,8,128]{2,1,0:T(8,128)S(1)}, u32[]{:S(2)}, u32[]{:S(2)}) collective-permute-start(f32[5,8,128]{2,1,0:T(8,128)S(1)} %add.330), channel_id=1, source_target_pairs={{1,0},{2,1},{3,2},{4,3},{5,4},{6,5},{7,6},{9,8},{10,9},{11,10},{12... | collective-permute-start | bytes 61448 | tf_op jit(solution)/shard_map/while/body/eval_jaxpr/ppermute | solution.py:12
  225.1 6.6 %collective-permute-start.3 = (f32[5,8,128]{2,1,0:T(8,128)S(1)}, f32[5,8,128]{2,1,0:T(8,128)S(1)}, u32[]{:S(2)}, u32[]{:S(2)}) collective-permute-start(f32[5,8,128]{2,1,0:T(8,128)S(1)} %add.330), channel_id=1, source_target_pairs={{1,0},{2,1},{3,2},{4,3},{5,4},{6,5},{7,6},{9,8},{10,9},{11,10},{12... | collective-permute-start | bytes 61448 | tf_op jit(solution)/shard_map/while/body/eval_jaxpr/ppermute | solution.py:12
  231.7 6.6 %collective-permute-start.3 = (f32[5,8,128]{2,1,0:T(8,128)S(1)}, f32[5,8,128]{2,1,0:T(8,128)S(1)}, u32[]{:S(2)}, u32[]{:S(2)}) collective-permute-start(f32[5,8,128]{2,1,0:T(8,128)S(1)} %add.330), channel_id=1, source_target_pairs={{1,0},{2,1},{3,2},{4,3},{5,4},{6,5},{7,6},{9,8},{10,9},{11,10},{12... | collective-permute-start | bytes 61448 | tf_op jit(solution)/shard_map/while/body/eval_jaxpr/ppermute | solution.py:12
  238.3 6.6 %collective-permute-start.3 = (f32[5,8,128]{2,1,0:T(8,128)S(1)}, f32[5,8,128]{2,1,0:T(8,128)S(1)}, u32[]{:S(2)}, u32[]{:S(2)}) collective-permute-start(f32[5,8,128]{2,1,0:T(8,128)S(1)} %add.330), channel_id=1, source_target_pairs={{1,0},{2,1},{3,2},{4,3},{5,4},{6,5},{7,6},{9,8},{10,9},{11,10},{12... | collective-permute-start | bytes 61448 | tf_op jit(solution)/shard_map/while/body/eval_jaxpr/ppermute | solution.py:12
  (4 other events, 65.2 us)
where the time goes:
time: 273 us; the launch traced here: 269 us
  local copies, waits for them, and re-layouts  86.3 us (32%)
  starting transfers between devices  70.6 us (26%)
  waiting for transfers between devices  66.3 us (24%)
  other arithmetic  39.4 us (14%)
  loops' own time  5.65 us (2%)
    ppermute x20, waiting for transfers between devices, from_behind(): lax.ppermute(value, axis, [(source, source + steps) for source in range(f...  60.6 us
    ppermute x20, starting transfers between devices, from_behind(): lax.ppermute(value, axis, [(source, source + steps) for source in range(f...  59.2 us
    dynamic_slice x32, local copies, waits for them, and re-layouts, run_advance(): here = lax.dynamic_index_in_dim(coupling, k, line_axis + 1, keepdims=False)  39.2 us
    dynamic_slice x32, local copies, waits for them, and re-layouts, compose_advance(): here = lax.dynamic_index_in_dim(coupling, k, line_axis + 1, keepdims=False)  39.2 us
    reduce_sum x118, other arithmetic, apply_block(): return jnp.sum(blocks * vector[None], axis=1)  32.4 us
    ppermute x2, starting transfers between devices, extended(): after = lax.ppermute(first, axis, down)  6.06 us
  transfers between devices with their start and end apart: 24, of which 24 were waited for; matrix products, arithmetic and copies ran while one was open for 0% of the time, Pallas kernels for 0%

commit v1 on v0

v1 whole, which is shorter than its diff:
```python
import functools

import jax
import jax.numpy as jnp
from jax import lax
from jax.experimental import pallas as pl
from jax.experimental.pallas import tpu as pltpu
from jax.sharding import PartitionSpec as P

DISSIPATION = 0.1
NVAR = 5
F32 = jnp.float32
ROWS = 8
VMEM_BYTES = 56 * 1024 * 1024


def call(kernel, name, out_shapes, scratch=()):
    shapes = [jax.ShapeDtypeStruct(s, F32) for s in out_shapes]
    single = len(shapes) == 1
    return pl.pallas_call(
        kernel,
        name=name,
        out_shape=shapes[0] if single else shapes,
        scratch_shapes=[pltpu.VMEM(s, F32) for s in scratch],
        compiler_params=pltpu.CompilerParams(vmem_limit_bytes=VMEM_BYTES),
    )


def tree(terms):
    while len(terms) > 1:
        pairs = [terms[k] + terms[k + 1] for k in range(0, len(terms) - 1, 2)]
        terms = pairs + (terms[-1:] if len(terms) % 2 else [])
    return terms[0]


def matvec(load, vector):
    return [tree([load(a, b) * vector[b] for b in range(NVAR)]) for a in range(NVAR)]


def matmat(load, matrix):
    out = []
    for a in range(NVAR):
        row = [load(a, b) for b in range(NVAR)]
        for c in range(NVAR):
            out.append(tree([row[b] * matrix[NVAR * b + c] for b in range(NVAR)]))
    return out


def plus(left, right):
    return [p + q for p, q in zip(left, right, strict=True)]


def minus(left, right):
    return [p - q for p, q in zip(left, right, strict=True)]


def compose_lines(length, lower_at, upper_at, store_p, load_p, emit):
    first = [-lower_at(0, a, b) for a in range(NVAR) for b in range(NVAR)]
    store_p(0, first)

    def forward(i, p):
        p = [-q for q in matmat(lambda a, b: lower_at(i, a, b), p)]
        store_p(i, p)
        return tuple(p)

    last = lax.fori_loop(1, length, forward, tuple(first))
    emit(0, last)

    def backward(k, carried):
        w, r = carried
        i = length - 1 - k
        at = lambda a, b: upper_at(i, a, b)
        w = minus(load_p(i), matmat(at, list(w)))
        r = [-q for q in matmat(at, list(r))]
        return tuple(w), tuple(r)

    r = tuple(-upper_at(length - 1, a, b) for a in range(NVAR) for b in range(NVAR))
    w, r = lax.fori_loop(1, length, backward, (last, r))
    emit(1, r)
    emit(2, w)


def compose_x_kernel(lower, upper, out, held):
    cells, rows = lower.shape[2], lower.shape[3]

    def group(g, _):
        here = pl.ds(pl.multiple_of(g * ROWS, ROWS), ROWS)

        def emit(which, matrix):
            for a in range(NVAR):
                for b in range(NVAR):
                    out[which, a, b, here] = matrix[NVAR * a + b]

        def store_p(i, p):
            for k in range(NVAR * NVAR):
                held[i, k] = p[k]

        compose_lines(
            cells,
            lambda i, a, b: lower[a, b, i, here],
            lambda i, a, b: upper[a, b, i, here],
            store_p,
            lambda i: [held[i, k] for k in range(NVAR * NVAR)],
            emit,
        )
        return 0

    lax.fori_loop(0, rows // ROWS, group, 0)


def compose_y_kernel(cells_x, cells_y, lower, upper, out, held):
    def emit(which, matrix):
        for a in range(NVAR):
            for b in range(NVAR):
                out[which, a, b] = matrix[NVAR * a + b]

    def store_p(i, p):
        for k in range(NVAR * NVAR):
            held[i, k] = p[k]

    compose_lines(
        cells_y,
        lambda j, a, b: lower[a, b, pl.ds(j, cells_x, stride=cells_y), :],
        lambda j, a, b: upper[a, b, pl.ds(j, cells_x, stride=cells_y), :],
        store_p,
        lambda i: [held[i, k] for k in range(NVAR * NVAR)],
        emit,
    )


def local_x_kernel(
    field, forcing, x_before, x_after, y_before, y_after, inverse, lower, upper,
    reduced, source_out, padded, held,
):
    cells, rows, lanes = field.shape[1:]
    zero = jnp.zeros((rows, lanes), F32)
    middle = pl.ds(ROWS, rows)
    for c in range(NVAR):
        for i in range(cells):
            padded[c, i + 2, middle] = field[c, i]
            padded[c, i + 2, ROWS - 2 : ROWS] = y_before[c, i]
            padded[c, i + 2, ROWS + rows : ROWS + rows + 2] = y_after[c, i]
        for k in range(2):
            padded[c, k, middle] = x_before[c, k]
            padded[c, cells + 2 + k, middle] = x_after[c, k]

    def right_side(i):
        out = []
        for c in range(NVAR):
            centre = padded[c, i + 2, middle]
            along_x = (
                padded[c, i, middle] - 4.0 * padded[c, i + 1, middle] + 6.0 * centre
                - 4.0 * padded[c, i + 3, middle] + padded[c, i + 4, middle]
            )
            along_y = (
                padded[c, i + 2, pl.ds(ROWS - 2, rows)]
                - 4.0 * padded[c, i + 2, pl.ds(ROWS - 1, rows)]
                + 6.0 * centre
                - 4.0 * padded[c, i + 2, pl.ds(ROWS + 1, rows)]
                + padded[c, i + 2, pl.ds(ROWS + 2, rows)]
            )
            out.append(forcing[c, i] - DISSIPATION * (along_x + along_y))
        return out

    def forward(i, v):
        s = matvec(lambda a, b: inverse[a, b, i], right_side(i))
        for c in range(NVAR):
            source_out[c, i] = s[c]
        v = minus(s, matvec(lambda a, b: lower[a, b, i], list(v)))
        for c in range(NVAR):
            held[c, i] = v[c]
        return tuple(v)

    v = lax.fori_loop(0, cells, forward, (zero,) * NVAR)
    for c in range(NVAR):
        reduced[0, c] = v[c]

    def backward(k, w):
        i = cells - 1 - k
        product = matvec(lambda a, b: upper[a, b, i], list(w))
        return tuple(held[c, i] - product[c] for c in range(NVAR))

    w = lax.fori_loop(0, cells, backward, (zero,) * NVAR)
    for c in range(NVAR):
        reduced[1, c] = w[c]


def vec(ref, which):
    return [ref[which, c] for c in range(NVAR)]


def block(ref, which):
    return lambda a, b: ref[which, a, b]


def combine_vectors_kernel(last, bits, own_m, got_m, own_v, got_v, out):
    def body(left_m, left_v, right_m, right_v):
        a_left, c_right = vec(left_v, 0), vec(right_v, 1)
        a = plus(matvec(block(right_m, 0), a_left), vec(right_v, 0))
        middle = plus(matvec(block(right_m, 2), a_left), c_right)
        c = plus(matvec(block(left_m, 1), middle), vec(left_v, 1))
        for k in range(NVAR):
            out[0, k] = a[k]
            out[1, k] = c[k]

    @pl.when(bits[0, 0] == 0)
    def _():
        body(own_m, own_v, got_m, got_v)

    @pl.when(bits[0, 0] == 1)
    def _():
        body(got_m, got_v, own_m, own_v)


def combine_matrices_kernel(bits, own, got, out):
    def body(left, right):
        lines = left.shape[3]

        def group(g, _):
            here = pl.ds(pl.multiple_of(g * ROWS, ROWS), ROWS)

            def block_of(ref, which):
                return lambda a, b: ref[which, a, b, here]

            def whole(ref, which):
                return [ref[which, a, b, here] for a in range(NVAR) for b in range(NVAR)]

            def emit(which, matrix):
                for a in range(NVAR):
                    for b in range(NVAR):
                        out[which, a, b, here] = matrix[NVAR * a + b]

            a_left = whole(left, 0)
            emit(0, matmat(block_of(right, 0), a_left))
            through = matmat(block_of(right, 2), a_left)
            emit(2, plus(matmat(block_of(left, 1), through), whole(left, 2)))
            emit(1, matmat(block_of(left, 1), whole(right, 1)))
            return 0

        lax.fori_loop(0, lines // ROWS, group, 0)

    @pl.when(bits[0, 0] == 0)
    def _():
        body(own, got)

    @pl.when(bits[0, 0] == 1)
    def _():
        body(got, own)


def descend(levels, bits, refs, f_ref, b_ref):
    top = levels - 1
    own_m, got_c, own_v, got = refs[top]
    shape = f_ref.shape[1:]

    @pl.when(bits[top, 0] == 0)
    def _():
        b = plus(
            matvec(lambda a, b: got_c[a, b], vec(own_v, 0)),
            [got[k] for k in range(NVAR)],
        )
        for k in range(NVAR):
            f_ref[k] = jnp.zeros(shape, F32)
            b_ref[k] = b[k]

    @pl.when(bits[top, 0] == 1)
    def _():
        for k in range(NVAR):
            f_ref[k] = got[k]
            b_ref[k] = jnp.zeros(shape, F32)

    for l in reversed(range(top)):
        own_m, got_m, own_v, got_v = refs[l]

        @pl.when(bits[l, 0] == 0)
        def _(own_m=own_m, got_m=got_m, own_v=own_v, got_v=got_v):
            f = [f_ref[k] for k in range(NVAR)]
            b = [b_ref[k] for k in range(NVAR)]
            mid = plus(matvec(block(own_m, 0), f), vec(own_v, 0))
            out = plus(
                plus(matvec(block(got_m, 1), b), matvec(block(got_m, 2), mid)),
                vec(got_v, 1),
            )
            for k in range(NVAR):
                b_ref[k] = out[k]

        @pl.when(bits[l, 0] == 1)
        def _(own_m=own_m, got_m=got_m, own_v=own_v, got_v=got_v):
            f = [f_ref[k] for k in range(NVAR)]
            out = plus(matvec(block(got_m, 0), f), vec(got_v, 0))
            for k in range(NVAR):
                f_ref[k] = out[k]


def middle_kernel(
    levels, bits, *rest
):
    refs = [rest[4 * l : 4 * l + 4] for l in range(levels)]
    (source, x_lower, x_upper, y_inverse, y_lower, y_upper,
     reduced, y_source, f_ref, b_ref, held) = rest[4 * levels :]
    cells, rows = source.shape[1:3]
    descend(levels, bits, refs, f_ref, b_ref)

    def forward(i, v):
        product = matvec(lambda a, b: x_lower[a, b, i], list(v))
        v = [source[c, i] - product[c] for c in range(NVAR)]
        for c in range(NVAR):
            held[c, pl.ds(pl.multiple_of(i * rows, rows), rows)] = v[c]
        return tuple(v)

    lax.fori_loop(0, cells, forward, tuple(f_ref[k] for k in range(NVAR)))

    def backward(k, w):
        i = cells - 1 - k
        here = pl.ds(pl.multiple_of(i * rows, rows), rows)
        product = matvec(lambda a, b: x_upper[a, b, i], list(w))
        w = [held[c, here] - product[c] for c in range(NVAR)]
        s = matvec(lambda a, b: y_inverse[a, b, here], w)
        for c in range(NVAR):
            y_source[c, here] = s[c]
        return tuple(w)

    lax.fori_loop(0, cells, backward, tuple(b_ref[k] for k in range(NVAR)))

    def line(j):
        return pl.ds(j, cells, stride=rows)

    zero = jnp.zeros((cells, source.shape[3]), F32)

    def y_forward(j, v):
        product = matvec(lambda a, b: y_lower[a, b, line(j), :], list(v))
        v = [y_source[c, line(j), :] - product[c] for c in range(NVAR)]
        for c in range(NVAR):
            held[c, pl.ds(pl.multiple_of(j * cells, cells), cells)] = v[c]
        return tuple(v)

    v = lax.fori_loop(0, rows, y_forward, (zero,) * NVAR)

    def y_backward(k, w):
        j = rows - 1 - k
        product = matvec(lambda a, b: y_upper[a, b, line(j), :], list(w))
        here = pl.ds(pl.multiple_of(j * cells, cells), cells)
        return tuple(held[c, here] - product[c] for c in range(NVAR))

    w = lax.fori_loop(0, rows, y_backward, (zero,) * NVAR)
    for c in range(NVAR):
        reduced[0, c] = v[c]
        reduced[1, c] = w[c]


def end_kernel(levels, cells, rows, bits, *rest):
    refs = [rest[4 * l : 4 * l + 4] for l in range(levels)]
    y_source, y_lower, y_upper, out, f_ref, b_ref, held = rest[4 * levels :]
    descend(levels, bits, refs, f_ref, b_ref)

    def line(j):
        return pl.ds(j, cells, stride=rows)

    def forward(j, v):
        product = matvec(lambda a, b: y_lower[a, b, line(j), :], list(v))
        v = [y_source[c, line(j), :] - product[c] for c in range(NVAR)]
        for c in range(NVAR):
            held[c, pl.ds(pl.multiple_of(j * cells, cells), cells)] = v[c]
        return tuple(v)

    lax.fori_loop(0, rows, forward, tuple(f_ref[k] for k in range(NVAR)))

    def backward(k, w):
        j = rows - 1 - k
        here = pl.ds(pl.multiple_of(j * cells, cells), cells)
        product = matvec(lambda a, b: y_upper[a, b, line(j), :], list(w))
        w = [held[c, here] - product[c] for c in range(NVAR)]
        for c in range(NVAR):
            out[c, line(j), :] = w[c]
        return tuple(w)

    lax.fori_loop(0, rows, backward, tuple(b_ref[k] for k in range(NVAR)))


def per_device(field, forcing, x_inverse, x_lower, x_upper, y_inverse, y_lower, y_upper):
    cells, rows, lanes = field.shape[1:]
    n_px, n_py = lax.axis_size("px"), lax.axis_size("py")
    x_levels, y_levels = n_px.bit_length() - 1, n_py.bit_length() - 1

    def swap(value, axis, level):
        n = lax.axis_size(axis)
        return lax.ppermute(value, axis, [(i, i ^ (1 << level)) for i in range(n)])

    def shift(value, axis, step):
        n = lax.axis_size(axis)
        return lax.ppermute(
            value, axis, [(i, i + step) for i in range(n) if 0 <= i + step < n]
        )

    def bits_of(axis, levels):
        return ((lax.axis_index(axis) >> jnp.arange(levels)) & 1).astype(jnp.int32)[:, None]

    smem = pl.BlockSpec(memory_space=pltpu.SMEM)
    vmem = pl.BlockSpec(memory_space=pltpu.VMEM)

    def with_bits(kernel, name, out_shapes, operands, bits, scratch=()):
        shapes = [jax.ShapeDtypeStruct(s, F32) for s in out_shapes]
        single = len(shapes) == 1
        return pl.pallas_call(
            kernel,
            name=name,
            out_shape=shapes[0] if single else shapes,
            in_specs=[smem] + [vmem] * len(operands),
            out_specs=vmem if single else [vmem] * len(shapes),
            scratch_shapes=[pltpu.VMEM(s, F32) for s in scratch],
            compiler_params=pltpu.CompilerParams(vmem_limit_bytes=VMEM_BYTES),
        )(bits, *operands)

    x_bits, y_bits = bits_of("px", x_levels), bits_of("py", y_levels)

    y_before = shift(field[:, :, rows - 2 :], "py", 1)
    y_after = shift(field[:, :, :2], "py", -1)
    x_before = shift(field[:, cells - 2 :], "px", 1)
    x_after = shift(field[:, :2], "px", -1)

    flat = lambda m: m.reshape(m.shape[:2] + (cells * rows, lanes))
    y_inverse, y_lower, y_upper = flat(y_inverse), flat(y_lower), flat(y_upper)

    x_m = [call(compose_x_kernel, "compose_x", [(3, NVAR, NVAR, rows, lanes)],
                [(cells, NVAR * NVAR, ROWS, lanes)])(x_lower, x_upper)]
    y_m = [call(functools.partial(compose_y_kernel, cells, rows), "compose_y",
                [(3, NVAR, NVAR, cells, lanes)],
                [(rows, NVAR * NVAR, cells, lanes)])(y_lower, y_upper)]

    def exchange_matrices(own, axis, levels, bits):
        got = []
        for l in range(levels):
            if l == levels - 1:
                got.append(swap(own[l][2], axis, l))
            else:
                got.append(swap(own[l], axis, l))
                own.append(with_bits(combine_matrices_kernel, "join_matrices",
                                     [own[l].shape], [own[l], got[l]], bits[l:l + 1]))
        return got

    x_got_m = exchange_matrices(x_m, "px", x_levels, x_bits)
    y_got_m = exchange_matrices(y_m, "py", y_levels, y_bits)

    reduced, source = call(
        local_x_kernel, "local_x",
        [(2, NVAR, rows, lanes), (NVAR, cells, rows, lanes)],
        [(NVAR, cells + 4, rows + 2 * ROWS, lanes), (NVAR, cells, rows, lanes)],
    )(field, forcing, x_before, x_after, y_before, y_after, x_inverse, x_lower, x_upper)

    def exchange_vectors(own, axis, levels, bits, own_m, got_m):
        operands = []
        for l in range(levels):
            if l == levels - 1:
                send = jnp.where(bits[l, 0] == 0, own[0], own[1])
                got = swap(send, axis, l)
            else:
                got = swap(own, axis, l)
            operands += [own_m[l], got_m[l], own, got]
            if l < levels - 1:
                own = with_bits(functools.partial(combine_vectors_kernel, False), "join_vectors",
                                [own.shape], [own_m[l], got_m[l], own, got], bits[l:l + 1])
        return operands

    operands = exchange_vectors(reduced, "px", x_levels, x_bits, x_m, x_got_m)
    reduced, y_source = with_bits(
        functools.partial(middle_kernel, x_levels), "middle",
        [(2, NVAR, cells, lanes), (NVAR, cells * rows, lanes)],
        operands + [source, x_lower, x_upper, y_inverse, y_lower, y_upper],
        x_bits,
        [(NVAR, rows, lanes), (NVAR, rows, lanes), (NVAR, cells * rows, lanes)],
    )
    operands = exchange_vectors(reduced, "py", y_levels, y_bits, y_m, y_got_m)
    out = with_bits(
        functools.partial(end_kernel, y_levels, cells, rows), "end",
        [(NVAR, cells * rows, lanes)],
        operands + [y_source, y_lower, y_upper],
        y_bits,
        [(NVAR, cells, lanes), (NVAR, cells, lanes), (NVAR, cells * rows, lanes)],
    )
    return out.reshape(NVAR, cells, rows, lanes)


def solution(mesh):
    cell = P(None, "px", "py", None)
    blocks = P(None, None, "px", "py", None)
    return jax.shard_map(
        per_device,
        mesh=mesh,
        in_specs=(cell, cell) + (blocks,) * 6,
        out_specs=cell,
        check_vma=False,
    )
```

time: 273 us -> 92.8 us (0.34)
  the two profiles are of different devices: /device:TPU:6 before, /device:TPU:0 now
where the time goes in v1:
time: 92.8 us; the launch traced here: 92.2 us
  Pallas kernels  42.7 us (46%)
  starting transfers between devices  22.3 us (24%)
  local copies, waits for them, and re-layouts  11.8 us (13%)
  waiting for transfers between devices  11.3 us (12%)
  other arithmetic  2.75 us (3%)
  between operations  1.38 us (1%)
    pallas_call x8, Pallas kernels, with_bits(): pl.pallas_call(kernel, name=name, out_shape=shapes[0] if single else shap...  28.5 us
    ppermute x10, starting transfers between devices, swap(): return lax.ppermute(value, axis, [(i, i ^ 1 << level) for i in range(n)])  14 us
    ppermute x4, starting transfers between devices, shift(): lax.ppermute(value, axis, [(i, i + step) for i in range(n) if 0 <= i + st...  8.37 us
    unnamed x28, local copies, waits for them, and re-layouts  6.72 us
    ppermute x10, waiting for transfers between devices, swap(): return lax.ppermute(value, axis, [(i, i ^ 1 << level) for i in range(n)])  6.03 us
    pallas_call x1, Pallas kernels, per_device(): call(functools.partial(compose_y_kernel, cells, rows), 'compose_y', [(3,...  5.41 us
    ppermute x4, waiting for transfers between devices, shift(): lax.ppermute(value, axis, [(i, i + step) for i in range(n) if 0 <= i + st...  5.26 us
    pallas_call x1, Pallas kernels, per_device(): call(compose_x_kernel, 'compose_x', [(3, NVAR, NVAR, rows, lanes)], [(cel...  4.46 us
  transfers between devices with their start and end apart: 14, of which 5 were waited for; matrix products, arithmetic and copies ran while one was open for 7% of the time, Pallas kernels for 38%

profile of v1, /device:TPU:0, one launch (start us, length us, event | category | flops | bytes accessed | tf_op | source)
XLA Modules:
  0.0 92.2 jit_solution(2881319991362357308)
XLA Ops:
  0.9 2.4 %collective-permute-start.2 = (f32[5,2,16,128]{3,2,1,0:T(8,128)S(1)}, f32[5,2,16,128]{3,2,1,0:T(8,128)S(1)}, u32[]{:S(2)}, u32[]{:S(2)}) collective-permute-start(f32[5,2,16,128]{3,2,1,0:T(8,128)S(1)} %get-tuple-element.16), channel_id=1, source_target_pairs={{0,8},{8,16},{16,24},{1,9},{9,17},{17,25},{2,10},{10,18},{18,26},{... | collective-permute-start | bytes 245768 | tf_op jit(solution)/shard_map/ppermute | solution.py:391
  3.3 1.3 %collective-permute-start.3 = (f32[5,2,16,128]{3,2,1,0:T(8,128)S(1)}, f32[5,2,16,128]{3,2,1,0:T(8,128)S(1)}, u32[]{:S(2)}, u32[]{:S(2)}) collective-permute-start(f32[5,2,16,128]{3,2,1,0:T(8,128)S(1)} %get-tuple-element.15), channel_id=1, source_target_pairs={{8,0},{16,8},{24,16},{9,1},{17,9},{25,17},{10,2},{18,10},{26,18},{... | collective-permute-start | bytes 245768 | tf_op jit(solution)/shard_map/ppermute | solution.py:391
  4.6 4.5 %compose_x.1.own.own_m.rest_0_ = f32[3,5,5,16,128]{4,3,2,1,0:T(8,128)} custom-call(f32[5,5,8,16,128]{4,3,2,1,0:T(8,128)} %rest_9_.1, f32[5,5,8,16,128]{4,3,2,1,0:T(8,128)} %rest_10_.1), custom_call_target="tpu_custom_call" | custom-call | tf_op jit(solution)/shard_map/compose_x/pallas_call | solution.py:424
  9.1 3.2 %collective-permute-start.1 = (f32[3,5,5,16,128]{4,3,2,1,0:T(8,128)}, f32[3,5,5,16,128]{4,3,2,1,0:T(8,128)S(1)}, u32[]{:S(2)}, u32[]{:S(2)}) collective-permute-start(f32[3,5,5,16,128]{4,3,2,1,0:T(8,128)} %compose_x.1.own.own_m.rest_0_), channel_id=1, source_target_pairs={{0,8},{8,0},{16,24},{24,16},{1,9},{9,1},{17,25},{25,17},{2,10},{10... | collective-permute-start | bytes 1843208 | tf_op jit(solution)/shard_map/ppermute | solution.py:387
  13.3 3.4 %collective-permute-start.4 = (f32[5,8,2,128]{3,2,1,0:T(2,128)S(1)}, f32[5,8,2,128]{3,2,1,0:T(2,128)S(1)}, u32[]{:S(2)}, u32[]{:S(2)}) collective-permute-start(f32[5,8,2,128]{3,2,1,0:T(2,128)S(1)} %get-tuple-element.14), channel_id=1, source_target_pairs={{0,1},{1,2},{2,3},{3,4},{4,5},{5,6},{6,7},{8,9},{9,10},{10,11},{11... | collective-permute-start | bytes 122888 | tf_op jit(solution)/shard_map/ppermute | solution.py:391
  16.8 5.4 %compose_y.1.own.own_m.rest_0_ = f32[3,5,5,8,128]{4,3,2,1,0:T(8,128)} custom-call(f32[5,5,128,128]{3,2,1,0:T(8,128)} %bitcast.17, f32[5,5,128,128]{3,2,1,0:T(8,128)} %bitcast.20), custom_call_target="tpu_custom_call" | custom-call | tf_op jit(solution)/shard_map/compose_y/pallas_call | solution.py:426
  22.2 1.5 %collective-permute-start = (f32[3,5,5,8,128]{4,3,2,1,0:T(8,128)}, f32[3,5,5,8,128]{4,3,2,1,0:T(8,128)S(1)}, u32[]{:S(2)}, u32[]{:S(2)}) collective-permute-start(f32[3,5,5,8,128]{4,3,2,1,0:T(8,128)} %compose_y.1.own.own_m.rest_0_), channel_id=1, source_target_pairs={{0,1},{1,0},{2,3},{3,2},{4,5},{5,4},{6,7},{7,6},{8,9},{9,8},{10,11... | collective-permute-start | bytes 921608 | tf_op jit(solution)/shard_map/ppermute | solution.py:387
  24.4 1.3 %collective-permute-start.5 = (f32[5,8,2,128]{3,2,1,0:T(2,128)S(1)}, f32[5,8,2,128]{3,2,1,0:T(2,128)S(1)}, u32[]{:S(2)}, u32[]{:S(2)}) collective-permute-start(f32[5,8,2,128]{3,2,1,0:T(2,128)S(1)} %get-tuple-element.13), channel_id=1, source_target_pairs={{1,0},{2,1},{3,2},{4,3},{5,4},{6,5},{7,6},{9,8},{10,9},{11,10},{12... | collective-permute-start | bytes 122888 | tf_op jit(solution)/shard_map/ppermute | solution.py:391
  26.9 5.2 %collective-permute-done.5.y_after = f32[5,8,2,128]{3,2,1,0:T(2,128)S(1)} collective-permute-done((f32[5,8,2,128]{3,2,1,0:T(2,128)S(1)}, f32[5,8,2,128]{3,2,1,0:T(2,128)S(1)}, u32[]{:S(2)}, u32[]{:S(2)}) %collective-permute-start.5) | collective-permute-done | bytes 40992 | tf_op jit(solution)/shard_map/ppermute | solution.py:391
  33.5 4.3 %local_x.1 = (f32[2,5,16,128]{3,2,1,0:T(8,128)}, f32[5,8,16,128]{3,2,1,0:T(8,128)}) custom-call(f32[5,8,16,128]{3,2,1,0:T(8,128)} %field.1, f32[5,8,16,128]{3,2,1,0:T(8,128)} %forcing.1, f32[5,2,16,128]{3,2,1,0:T(8,128)} %copy-done.8, f32[5,2,16,128]{3,2,1,0:T(8,128)} %copy-done.9, f32[5,8,2,128]{3,2,1,0:T(2,128)} %copy-done.10, ...), custom_call_target="tpu_custom_call" | custom-call | tf_op jit(solution)/shard_map/local_x/pallas_call | solution.py:444
  38.5 2.6 %join_matrices.4.own.own_m.rest_4_ = f32[3,5,5,8,128]{4,3,2,1,0:T(8,128)} custom-call(s32[1,1]{1,0:T(1,128)} %bitcast.7.bits, f32[3,5,5,8,128]{4,3,2,1,0:T(8,128)} %compose_y.1.own.own_m.rest_0_, f32[3,5,5,8,128]{4,3,2,1,0:T(8,128)} %copy-done.1), custom_call_target="tpu_custom_call" | custom-call | tf_op jit(solution)/shard_map/join_matrices/pallas_call | solution.py:404
  41.1 1.6 %collective-permute-start.10 = (f32[3,5,5,8,128]{4,3,2,1,0:T(8,128)}, f32[3,5,5,8,128]{4,3,2,1,0:T(8,128)S(1)}, u32[]{:S(2)}, u32[]{:S(2)}) collective-permute-start(f32[3,5,5,8,128]{4,3,2,1,0:T(8,128)} %join_matrices.4.own.own_m.rest_4_), channel_id=1, source_target_pairs={{0,2},{1,3},{2,0},{3,1},{4,6},{5,7},{6,4},{7,5},{8,10},{9,11},{10,... | collective-permute-start | bytes 921608 | tf_op jit(solution)/shard_map/ppermute | solution.py:387
  43.5 3.1 %join_matrices.3.rest_4_ = f32[3,5,5,16,128]{4,3,2,1,0:T(8,128)} custom-call(s32[1,1]{1,0:T(1,128)} %bitcast.2.bits, f32[3,5,5,16,128]{4,3,2,1,0:T(8,128)} %compose_x.1.own.own_m.rest_0_, f32[3,5,5,16,128]{4,3,2,1,0:T(8,128)} %copy-done), custom_call_target="tpu_custom_call" | custom-call | tf_op jit(solution)/shard_map/join_matrices/pallas_call | solution.py:404
  47.5 2.2 %collective-permute-start.7 = (f32[5,5,16,128]{3,2,1,0:T(8,128)S(1)}, f32[5,5,16,128]{3,2,1,0:T(8,128)S(1)}, u32[]{:S(2)}, u32[]{:S(2)}) collective-permute-start(f32[5,5,16,128]{3,2,1,0:T(8,128)S(1)} %slice_bitcast_fusion), channel_id=1, source_target_pairs={{0,16},{8,24},{16,0},{24,8},{1,17},{9,25},{17,1},{25,9},{2,18},{10... | collective-permute-start | bytes 614408 | tf_op jit(solution)/shard_map/ppermute | solution.py:387
  50.3 2.7 %join_vectors.3.rest_6_ = f32[2,5,16,128]{3,2,1,0:T(8,128)} custom-call(s32[1,1]{1,0:T(1,128)} %bitcast.2.bits, f32[3,5,5,16,128]{4,3,2,1,0:T(8,128)} %compose_x.1.own.own_m.rest_0_, f32[3,5,5,16,128]{4,3,2,1,0:T(8,128)} %copy-done, f32[2,5,16,128]{3,2,1,0:T(8,128)} %get-tuple-element.9.own_v.rest_2_, f32[2,5,16,128]{3,2,1,0:T(8,128)} %copy-done.3), custom_call_target="tpu_custom_call" | custom-call | tf_op jit(solution)/shard_map/join_vectors/pallas_call | solution.py:404
  54.4 3.4 %collective-permute-done.8.rest_7_ = f32[5,16,128]{2,1,0:T(8,128)S(1)} collective-permute-done((f32[5,16,128]{2,1,0:T(8,128)S(1)}, f32[5,16,128]{2,1,0:T(8,128)S(1)}, u32[]{:S(2)}, u32[]{:S(2)}) %collective-permute-start.8) | collective-permute-done | bytes 40992 | tf_op jit(solution)/shard_map/ppermute | solution.py:387
  58.5 7.6 %middle.1 = (f32[2,5,8,128]{3,2,1,0:T(8,128)}, f32[5,128,128]{2,1,0:T(8,128)}) custom-call(s32[2,1]{1,0:T(2,128)} %shift-right-arithmetic_and_fusion.1.bits, f32[3,5,5,16,128]{4,3,2,1,0:T(8,128)} %compose_x.1.own.own_m.rest_0_, f32[3,5,5,16,128]{4,3,2,1,0:T(8,128)} %copy-done, f32[2,5,16,128]{3,2,1,0:T(8,128)} %get-tuple-element.9.own_v.rest_2_, ...), custom_call_target="tpu_custom_call" | custom-call | tf_op jit(solution)/shard_map/middle/pallas_call | solution.py:404
  67.4 2.5 %join_matrices.5.rest_8_ = f32[3,5,5,8,128]{4,3,2,1,0:T(8,128)} custom-call(s32[1,1]{1,0:T(1,128)} %bitcast.8.bits, f32[3,5,5,8,128]{4,3,2,1,0:T(8,128)} %join_matrices.4.own.own_m.rest_4_, f32[3,5,5,8,128]{4,3,2,1,0:T(8,128)} %copy-done.2), custom_call_target="tpu_custom_call" | custom-call | tf_op jit(solution)/shard_map/join_matrices/pallas_call | solution.py:404
  70.9 2.4 %join_vectors.4.own_v.rest_6_ = f32[2,5,8,128]{3,2,1,0:T(8,128)} custom-call(s32[1,1]{1,0:T(1,128)} %bitcast.7.bits, f32[3,5,5,8,128]{4,3,2,1,0:T(8,128)} %compose_y.1.own.own_m.rest_0_, f32[3,5,5,8,128]{4,3,2,1,0:T(8,128)} %copy-done.1, f32[2,5,8,128]{3,2,1,0:T(8,128)} %get-tuple-element.11.own_v.rest_2_, f32[2,5,8,128]{3,2,1,0:T(8,128)} %copy-done.5), custom_call_target="tpu_custom_call" | custom-call | tf_op jit(solution)/shard_map/join_vectors/pallas_call | solution.py:404
  74.6 2.6 %collective-permute-start.12 = (f32[5,5,8,128]{3,2,1,0:T(8,128)S(1)}, f32[5,5,8,128]{3,2,1,0:T(8,128)S(1)}, u32[]{:S(2)}, u32[]{:S(2)}) collective-permute-start(f32[5,5,8,128]{3,2,1,0:T(8,128)S(1)} %slice_bitcast_fusion.1), channel_id=1, source_target_pairs={{0,4},{1,5},{2,6},{3,7},{4,0},{5,1},{6,2},{7,3},{8,12},{9,13},{10,... | collective-permute-start | bytes 307208 | tf_op jit(solution)/shard_map/ppermute | solution.py:387
  78.3 2.3 %join_vectors.5.rest_10_ = f32[2,5,8,128]{3,2,1,0:T(8,128)} custom-call(s32[1,1]{1,0:T(1,128)} %bitcast.8.bits, f32[3,5,5,8,128]{4,3,2,1,0:T(8,128)} %join_matrices.4.own.own_m.rest_4_, f32[3,5,5,8,128]{4,3,2,1,0:T(8,128)} %copy-done.2, f32[2,5,8,128]{3,2,1,0:T(8,128)} %join_vectors.4.own_v.rest_6_, f32[2,5,8,128]{3,2,1,0:T(8,128)} %copy-done.6), custom_call_target="tpu_custom_call" | custom-call | tf_op jit(solution)/shard_map/join_vectors/pallas_call | solution.py:404
  81.3 2.4 %collective-permute-start.13 = (f32[5,8,128]{2,1,0:T(8,128)S(1)}, f32[5,8,128]{2,1,0:T(8,128)S(1)}, u32[]{:S(2)}, u32[]{:S(2)}) collective-permute-start(f32[5,8,128]{2,1,0:T(8,128)S(1)} %fusion.1), channel_id=1, source_target_pairs={{0,4},{1,5},{2,6},{3,7},{4,0},{5,1},{6,2},{7,3},{8,12},{9,13},{10,... | collective-permute-start | bytes 61448 | tf_op jit(solution)/shard_map/ppermute | solution.py:387
  84.3 1.7 %collective-permute-done.13.rest_11_ = f32[5,8,128]{2,1,0:T(8,128)S(1)} collective-permute-done((f32[5,8,128]{2,1,0:T(8,128)S(1)}, f32[5,8,128]{2,1,0:T(8,128)S(1)}, u32[]{:S(2)}, u32[]{:S(2)}) %collective-permute-start.13) | collective-permute-done | bytes 20512 | tf_op jit(solution)/shard_map/ppermute | solution.py:387
  86.6 5.6 %end.1 = f32[5,128,128]{2,1,0:T(8,128)} custom-call(s32[3,1]{1,0:T(4,128)} %shift-right-arithmetic_and_fusion.bits, f32[3,5,5,8,128]{4,3,2,1,0:T(8,128)} %compose_y.1.own.own_m.rest_0_, f32[3,5,5,8,128]{4,3,2,1,0:T(8,128)} %copy-done.1, f32[2,5,8,128]{3,2,1,0:T(8,128)} %get-tuple-element.11.own_v.rest_2_, f32[2,5,8,128]{3,2,1,0:T(8,128)} %copy-done.5, ...), custom_call_target="tpu_custom_call" | custom-call | tf_op jit(solution)/shard_map/end/pallas_call | solution.py:404
  (55 shorter events, 15.9 us)
Async XLA Ops:
  0.9 31.2 %collective-permute-start.2 = (f32[5,2,16,128]{3,2,1,0:T(8,128)S(1)}, f32[5,2,16,128]{3,2,1,0:T(8,128)S(1)}, u32[]{:S(2)}, u32[]{:S(2)}) collective-permute-start(f32[5,2,16,128]{3,2,1,0:T(8,128)S(1)} %get-tuple-element.16), channel_id=1, source_target_pairs={{0,8},{8,16},{16,24},{1,9},{9,17},{17,25},{2,10},{10,18},{18,26},{... | collective-permute-start | bytes 245768 | tf_op jit(solution)/shard_map/ppermute | solution.py:391
  3.3 28.9 %collective-permute-start.3 = (f32[5,2,16,128]{3,2,1,0:T(8,128)S(1)}, f32[5,2,16,128]{3,2,1,0:T(8,128)S(1)}, u32[]{:S(2)}, u32[]{:S(2)}) collective-permute-start(f32[5,2,16,128]{3,2,1,0:T(8,128)S(1)} %get-tuple-element.15), channel_id=1, source_target_pairs={{8,0},{16,8},{24,16},{9,1},{17,9},{25,17},{10,2},{18,10},{26,18},{... | collective-permute-start | bytes 245768 | tf_op jit(solution)/shard_map/ppermute | solution.py:391
  9.1 33.6 %collective-permute-start.1 = (f32[3,5,5,16,128]{4,3,2,1,0:T(8,128)}, f32[3,5,5,16,128]{4,3,2,1,0:T(8,128)S(1)}, u32[]{:S(2)}, u32[]{:S(2)}) collective-permute-start(f32[3,5,5,16,128]{4,3,2,1,0:T(8,128)} %compose_x.1.own.own_m.rest_0_), channel_id=1, source_target_pairs={{0,8},{8,0},{16,24},{24,16},{1,9},{9,1},{17,25},{25,17},{2,10},{10... | collective-permute-start | bytes 1843208 | tf_op jit(solution)/shard_map/ppermute | solution.py:387
  13.3 11.0 %collective-permute-start.4 = (f32[5,8,2,128]{3,2,1,0:T(2,128)S(1)}, f32[5,8,2,128]{3,2,1,0:T(2,128)S(1)}, u32[]{:S(2)}, u32[]{:S(2)}) collective-permute-start(f32[5,8,2,128]{3,2,1,0:T(2,128)S(1)} %get-tuple-element.14), channel_id=1, source_target_pairs={{0,1},{1,2},{2,3},{3,4},{4,5},{5,6},{6,7},{8,9},{9,10},{10,11},{11... | collective-permute-start | bytes 122888 | tf_op jit(solution)/shard_map/ppermute | solution.py:391
  22.2 15.6 %collective-permute-start = (f32[3,5,5,8,128]{4,3,2,1,0:T(8,128)}, f32[3,5,5,8,128]{4,3,2,1,0:T(8,128)S(1)}, u32[]{:S(2)}, u32[]{:S(2)}) collective-permute-start(f32[3,5,5,8,128]{4,3,2,1,0:T(8,128)} %compose_y.1.own.own_m.rest_0_), channel_id=1, source_target_pairs={{0,1},{1,0},{2,3},{3,2},{4,5},{5,4},{6,7},{7,6},{8,9},{9,8},{10,11... | collective-permute-start | bytes 921608 | tf_op jit(solution)/shard_map/ppermute | solution.py:387
  24.4 7.8 %copy-start.10 = (f32[5,8,2,128]{3,2,1,0:T(2,128)}, f32[5,8,2,128]{3,2,1,0:T(2,128)S(1)}, u32[]{:S(2)}) copy-start(f32[5,8,2,128]{3,2,1,0:T(2,128)S(1)} %collective-permute-done.4.y_before) | copy-start | bytes 122884
  24.4 7.8 %collective-permute-start.5 = (f32[5,8,2,128]{3,2,1,0:T(2,128)S(1)}, f32[5,8,2,128]{3,2,1,0:T(2,128)S(1)}, u32[]{:S(2)}, u32[]{:S(2)}) collective-permute-start(f32[5,8,2,128]{3,2,1,0:T(2,128)S(1)} %get-tuple-element.13), channel_id=1, source_target_pairs={{1,0},{2,1},{3,2},{4,3},{5,4},{6,5},{7,6},{9,8},{10,9},{11,10},{12... | collective-permute-start | bytes 122888 | tf_op jit(solution)/shard_map/ppermute | solution.py:391
  32.2 0.6 copy-start.8
  32.8 0.6 copy-start.9
  37.7 12.0 %collective-permute-start.6 = (f32[2,5,16,128]{3,2,1,0:T(8,128)}, f32[2,5,16,128]{3,2,1,0:T(8,128)S(1)}, u32[]{:S(2)}, u32[]{:S(2)}) collective-permute-start(f32[2,5,16,128]{3,2,1,0:T(8,128)} %get-tuple-element.9.own_v.rest_2_), channel_id=1, source_target_pairs={{0,8},{8,0},{16,24},{24,16},{1,9},{9,1},{17,25},{25,17},{2,10},{10... | collective-permute-start | bytes 245768 | tf_op jit(solution)/shard_map/ppermute | solution.py:387
  37.7 0.7 copy-start.1
  41.1 25.6 %collective-permute-start.10 = (f32[3,5,5,8,128]{4,3,2,1,0:T(8,128)}, f32[3,5,5,8,128]{4,3,2,1,0:T(8,128)S(1)}, u32[]{:S(2)}, u32[]{:S(2)}) collective-permute-start(f32[3,5,5,8,128]{4,3,2,1,0:T(8,128)} %join_matrices.4.own.own_m.rest_4_), channel_id=1, source_target_pairs={{0,2},{1,3},{2,0},{3,1},{4,6},{5,7},{6,4},{7,5},{8,10},{9,11},{10,... | collective-permute-start | bytes 921608 | tf_op jit(solution)/shard_map/ppermute | solution.py:387
  42.7 0.8 copy-start
  47.5 10.3 %collective-permute-start.7 = (f32[5,5,16,128]{3,2,1,0:T(8,128)S(1)}, f32[5,5,16,128]{3,2,1,0:T(8,128)S(1)}, u32[]{:S(2)}, u32[]{:S(2)}) collective-permute-start(f32[5,5,16,128]{3,2,1,0:T(8,128)S(1)} %slice_bitcast_fusion), channel_id=1, source_target_pairs={{0,16},{8,24},{16,0},{24,8},{1,17},{9,25},{17,1},{25,9},{2,18},{10... | collective-permute-start | bytes 614408 | tf_op jit(solution)/shard_map/ppermute | solution.py:387
  49.7 0.6 copy-start.3
  53.8 4.0 %collective-permute-start.8 = (f32[5,16,128]{2,1,0:T(8,128)S(1)}, f32[5,16,128]{2,1,0:T(8,128)S(1)}, u32[]{:S(2)}, u32[]{:S(2)}) collective-permute-start(f32[5,16,128]{2,1,0:T(8,128)S(1)} %fusion), channel_id=1, source_target_pairs={{0,16},{8,24},{16,0},{24,8},{1,17},{9,25},{17,1},{25,9},{2,18},{10... | collective-permute-start | bytes 122888 | tf_op jit(solution)/shard_map/ppermute | solution.py:387
  57.8 0.7 copy-start.4
  66.1 4.2 %collective-permute-start.9 = (f32[2,5,8,128]{3,2,1,0:T(8,128)}, f32[2,5,8,128]{3,2,1,0:T(8,128)S(1)}, u32[]{:S(2)}, u32[]{:S(2)}) collective-permute-start(f32[2,5,8,128]{3,2,1,0:T(8,128)} %get-tuple-element.11.own_v.rest_2_), channel_id=1, source_target_pairs={{0,1},{1,0},{2,3},{3,2},{4,5},{5,4},{6,7},{7,6},{8,9},{9,8},{10,11... | collective-permute-start | bytes 122888 | tf_op jit(solution)/shard_map/ppermute | solution.py:387
  66.7 0.7 copy-start.2
  70.3 0.6 copy-start.5
  73.3 4.4 %collective-permute-start.11 = (f32[2,5,8,128]{3,2,1,0:T(8,128)}, f32[2,5,8,128]{3,2,1,0:T(8,128)S(1)}, u32[]{:S(2)}, u32[]{:S(2)}) collective-permute-start(f32[2,5,8,128]{3,2,1,0:T(8,128)} %join_vectors.4.own_v.rest_6_), channel_id=1, source_target_pairs={{0,2},{1,3},{2,0},{3,1},{4,6},{5,7},{6,4},{7,5},{8,10},{9,11},{10,... | collective-permute-start | bytes 122888 | tf_op jit(solution)/shard_map/ppermute | solution.py:387
  74.6 9.7 %collective-permute-start.12 = (f32[5,5,8,128]{3,2,1,0:T(8,128)S(1)}, f32[5,5,8,128]{3,2,1,0:T(8,128)S(1)}, u32[]{:S(2)}, u32[]{:S(2)}) collective-permute-start(f32[5,5,8,128]{3,2,1,0:T(8,128)S(1)} %slice_bitcast_fusion.1), channel_id=1, source_target_pairs={{0,4},{1,5},{2,6},{3,7},{4,0},{5,1},{6,2},{7,3},{8,12},{9,13},{10,... | collective-permute-start | bytes 307208 | tf_op jit(solution)/shard_map/ppermute | solution.py:387
  81.3 4.7 %collective-permute-start.13 = (f32[5,8,128]{2,1,0:T(8,128)S(1)}, f32[5,8,128]{2,1,0:T(8,128)S(1)}, u32[]{:S(2)}, u32[]{:S(2)}) collective-permute-start(f32[5,8,128]{2,1,0:T(8,128)S(1)} %fusion.1), channel_id=1, source_target_pairs={{0,4},{1,5},{2,6},{3,7},{4,0},{5,1},{6,2},{7,3},{8,12},{9,13},{10,... | collective-permute-start | bytes 61448 | tf_op jit(solution)/shard_map/ppermute | solution.py:387
  84.3 1.7 %copy-start.7 = (f32[5,5,8,128]{3,2,1,0:T(8,128)}, f32[5,5,8,128]{3,2,1,0:T(8,128)S(1)}, u32[]{:S(2)}) copy-start(f32[5,5,8,128]{3,2,1,0:T(8,128)S(1)} %collective-permute-done.12.rest_9_) | copy-start | bytes 307204
  (4 other events, 2.5 us)

commit v2 on v1

v2 whole, which is shorter than its diff:
```python
import functools

import jax
import jax.numpy as jnp
from jax import lax
from jax.experimental import pallas as pl
from jax.experimental.pallas import tpu as pltpu
from jax.sharding import PartitionSpec as P

DISSIPATION = 0.1
NVAR = 5
F32 = jnp.float32
ROWS = 8
VMEM_BYTES = 12 * 1024 * 1024


def call(kernel, name, out_shapes, operands, scratch=(), result_in_hbm=False, from_hbm=(),
         copies=0):
    vmem = pl.BlockSpec(memory_space=pltpu.VMEM)
    make = jax.ShapeDtypeStruct if result_in_hbm else pltpu.VMEM
    shapes = [make(s, F32) for s in out_shapes]
    single = len(shapes) == 1
    operands = [pltpu.with_memory_space_constraint(x, pltpu.VMEM) for x in operands]
    outer = [pltpu.with_memory_space_constraint(x, pltpu.HBM) for x in from_hbm]
    semaphores = [pltpu.SemaphoreType.DMA((copies,))] if copies else []
    return pl.pallas_call(
        kernel,
        name=name,
        out_shape=shapes[0] if single else shapes,
        in_specs=[vmem] * len(operands) + [pl.BlockSpec(memory_space=pltpu.HBM)] * len(outer),
        out_specs=vmem if single else [vmem] * len(shapes),
        scratch_shapes=[pltpu.VMEM(s, F32) for s in scratch] + semaphores,
        compiler_params=pltpu.CompilerParams(vmem_limit_bytes=VMEM_BYTES),
    )(*operands, *outer)


class Loads:
    def __init__(self, semaphores):
        self.semaphores, self.used = semaphores, 0

    def start(self, source, target):
        copies = []
        for k in range(source.shape[0]):
            copy = pltpu.make_async_copy(source.at[k], target.at[k], self.semaphores.at[self.used])
            copy.start()
            copies.append(copy)
            self.used += 1
        return copies


def wait(copies):
    for copy in copies:
        copy.wait()


def hold(arrays, *others):
    def nothing(*refs):
        pass

    operands = [pltpu.with_memory_space_constraint(x, pltpu.VMEM) for x in (*arrays, *others)]
    anywhere = pl.BlockSpec(memory_space=pl.ANY)
    held = pl.pallas_call(
        nothing,
        name="hold",
        out_shape=[pltpu.VMEM(x.shape, F32) for x in arrays],
        in_specs=[anywhere] * len(operands),
        out_specs=[anywhere] * len(arrays),
        input_output_aliases={k: k for k in range(len(arrays))},
        compiler_params=pltpu.CompilerParams(vmem_limit_bytes=1024 * 1024),
    )(*operands)
    return list(held)


def bit(axis, level):
    return (lax.axis_index(axis) >> level) & 1


def tree(terms):
    while len(terms) > 1:
        pairs = [terms[k] + terms[k + 1] for k in range(0, len(terms) - 1, 2)]
        terms = pairs + (terms[-1:] if len(terms) % 2 else [])
    return terms[0]


def matvec(load, vector):
    return [tree([load(a, b) * vector[b] for b in range(NVAR)]) for a in range(NVAR)]


def matmat(load, matrix):
    out = []
    for a in range(NVAR):
        row = [load(a, b) for b in range(NVAR)]
        for c in range(NVAR):
            out.append(tree([row[b] * matrix[NVAR * b + c] for b in range(NVAR)]))
    return out


def plus(left, right):
    return [p + q for p, q in zip(left, right, strict=True)]


def minus(left, right):
    return [p - q for p, q in zip(left, right, strict=True)]


def compose_lines(length, lower_at, upper_at, store_p, load_p, emit, turn=lambda: None):
    first = [-lower_at(0, a, b) for a in range(NVAR) for b in range(NVAR)]
    store_p(0, first)

    def forward(i, p):
        p = [-q for q in matmat(lambda a, b: lower_at(i, a, b), p)]
        store_p(i, p)
        return tuple(p)

    last = lax.fori_loop(1, length, forward, tuple(first))
    emit(0, last)
    turn()

    def backward(k, carried):
        w, r = carried
        i = length - 1 - k
        here = [upper_at(i, a, b) for a in range(NVAR) for b in range(NVAR)]
        at = lambda a, b: here[NVAR * a + b]
        w = minus(load_p(i), matmat(at, list(w)))
        r = [-q for q in matmat(at, list(r))]
        return tuple(w), tuple(r)

    r = tuple(-upper_at(length - 1, a, b) for a in range(NVAR) for b in range(NVAR))
    w, r = lax.fori_loop(1, length, backward, (last, r))
    emit(1, r)
    emit(2, w)


def compose_x_kernel(lower, upper, forcing_hbm, x_inverse_hbm, y_inverse_hbm,
                     out, forcing, x_inverse, y_inverse, held, semaphores):
    loads = Loads(semaphores)
    copies = loads.start(forcing_hbm, forcing) + loads.start(x_inverse_hbm, x_inverse)
    copies += loads.start(y_inverse_hbm, y_inverse)
    cells, rows = lower.shape[2], lower.shape[3]

    def group(g, _):
        here = pl.ds(pl.multiple_of(g * ROWS, ROWS), ROWS)

        def emit(which, matrix):
            for a in range(NVAR):
                for b in range(NVAR):
                    out[which, a, b, here] = matrix[NVAR * a + b]

        def store_p(i, p):
            for k in range(NVAR * NVAR):
                held[i, k] = p[k]

        compose_lines(
            cells,
            lambda i, a, b: lower[a, b, i, here],
            lambda i, a, b: upper[a, b, i, here],
            store_p,
            lambda i: [held[i, k] for k in range(NVAR * NVAR)],
            emit,
        )
        return 0

    lax.fori_loop(0, rows // ROWS, group, 0)
    wait(copies)


def compose_y_kernel(cells_x, cells_y, lower_hbm, upper_hbm, x_lower_hbm, x_upper_hbm,
                     out, lower_t, upper_t, x_lower, x_upper, held, lower, upper, semaphores):
    loads = Loads(semaphores)
    first, second = loads.start(lower_hbm, lower), loads.start(upper_hbm, upper)
    others = loads.start(x_lower_hbm, x_lower) + loads.start(x_upper_hbm, x_upper)
    wait(first)

    def emit(which, matrix):
        for a in range(NVAR):
            for b in range(NVAR):
                out[which, a, b] = matrix[NVAR * a + b]

    def store_p(i, p):
        for k in range(NVAR * NVAR):
            held[i, k] = p[k]

    def at(ref, kept):
        def load(j, a, b):
            value = ref[a, b, pl.ds(j, cells_x, stride=cells_y), :]
            kept[j, NVAR * a + b] = value
            return value

        return load

    compose_lines(
        cells_y,
        at(lower, lower_t),
        at(upper, upper_t),
        store_p,
        lambda i: [held[i, k] for k in range(NVAR * NVAR)],
        emit,
        lambda: wait(second),
    )
    wait(others)


def local_x_kernel(
    field, forcing, x_pair, x_cross, y_pair, y_cross, inverse, lower, upper,
    reduced, source_out, padded, held,
):
    cells, rows, lanes = field.shape[1:]
    zero = jnp.zeros((rows, lanes), F32)
    middle = pl.ds(ROWS, rows)
    for c in range(NVAR):
        for i in range(cells):
            padded[c, i + 2, middle] = field[c, i]

    def y_before(value):
        for c in range(NVAR):
            for k in range(2):
                for i in range(cells):
                    padded[c, i + 2, ROWS - 2 + k] = value(c, k, i)

    def y_after(value):
        for c in range(NVAR):
            for k in range(2):
                for i in range(cells):
                    padded[c, i + 2, ROWS + rows + k] = value(c, k, i)

    def x_before(value):
        for c in range(NVAR):
            for k in range(2):
                padded[c, k, middle] = value(c, k)

    def x_after(value):
        for c in range(NVAR):
            for k in range(2):
                padded[c, cells + 2 + k, middle] = value(c, k)

    for axis, before, behind, pair, cross, empty in (
        ("px", x_before, x_after, x_pair, x_cross, jnp.zeros((rows, lanes), F32)),
        ("py", y_before, y_after, y_pair, y_cross, jnp.zeros((lanes,), F32)),
    ):
        at, count = lax.axis_index(axis), lax.axis_size(axis)

        @pl.when(bit(axis, 0) == 0)
        def _(before=before, behind=behind, pair=pair, cross=cross):
            before(lambda *k: cross[k])
            behind(lambda *k: pair[k])

        @pl.when(bit(axis, 0) == 1)
        def _(before=before, behind=behind, pair=pair, cross=cross):
            before(lambda *k: pair[k])
            behind(lambda *k: cross[k])

        @pl.when(at == 0)
        def _(before=before, empty=empty):
            before(lambda *k: empty)

        @pl.when(at == count - 1)
        def _(behind=behind, empty=empty):
            behind(lambda *k: empty)

    def right_side(i):
        out = []
        for c in range(NVAR):
            centre = padded[c, i + 2, middle]
            along_x = (
                padded[c, i, middle] - 4.0 * padded[c, i + 1, middle] + 6.0 * centre
                - 4.0 * padded[c, i + 3, middle] + padded[c, i + 4, middle]
            )
            along_y = (
                padded[c, i + 2, pl.ds(ROWS - 2, rows)]
                - 4.0 * padded[c, i + 2, pl.ds(ROWS - 1, rows)]
                + 6.0 * centre
                - 4.0 * padded[c, i + 2, pl.ds(ROWS + 1, rows)]
                + padded[c, i + 2, pl.ds(ROWS + 2, rows)]
            )
            out.append(forcing[c, i] - DISSIPATION * (along_x + along_y))
        return out

    def forward(i, v):
        s = matvec(lambda a, b: inverse[a, b, i], right_side(i))
        for c in range(NVAR):
            source_out[c, i] = s[c]
        v = minus(s, matvec(lambda a, b: lower[a, b, i], list(v)))
        for c in range(NVAR):
            held[c, i] = v[c]
        return tuple(v)

    v = lax.fori_loop(0, cells, forward, (zero,) * NVAR, unroll=True)
    for c in range(NVAR):
        reduced[0, c] = v[c]

    def backward(k, w):
        i = cells - 1 - k
        product = matvec(lambda a, b: upper[a, b, i], list(w))
        return tuple(held[c, i] - product[c] for c in range(NVAR))

    w = lax.fori_loop(0, cells, backward, (zero,) * NVAR, unroll=True)
    for c in range(NVAR):
        reduced[1, c] = w[c]


def vec(ref, which):
    return [ref[which, c] for c in range(NVAR)]


def block(ref, which):
    return lambda a, b: ref[which, a, b]


def pack_kernel(cells, rows, field, y_pair, y_cross, x_pair, x_cross):
    def y_layers(out, j):
        for c in range(NVAR):
            for k in range(2):
                out[c, k] = field[c, pl.ds(j + k, cells, stride=rows), :]

    def x_layers(out, i):
        for c in range(NVAR):
            for k in range(2):
                out[c, k] = field[c, pl.ds((i + k) * rows, rows), :]

    for axis, put, pair, cross, length in (
        ("py", y_layers, y_pair, y_cross, rows),
        ("px", x_layers, x_pair, x_cross, cells),
    ):

        @pl.when(bit(axis, 0) == 0)
        def _(put=put, pair=pair, cross=cross, length=length):
            put(pair, length - 2)
            put(cross, 0)

        @pl.when(bit(axis, 0) == 1)
        def _(put=put, pair=pair, cross=cross, length=length):
            put(pair, 0)
            put(cross, length - 2)


def join_vectors_kernel(axis, level, last, own_m, got_m, own_v, got_v, out):
    def union_a(left_v, right_m, right_v):
        return plus(matvec(block(right_m, 0), vec(left_v, 0)), vec(right_v, 0))

    def union_c(left_m, left_v, right_m, right_v):
        middle = plus(matvec(block(right_m, 2), vec(left_v, 0)), vec(right_v, 1))
        return plus(matvec(block(left_m, 1), middle), vec(left_v, 1))

    def body(left_m, left_v, right_m, right_v):
        if not last:
            a = union_a(left_v, right_m, right_v)
            c = union_c(left_m, left_v, right_m, right_v)
            for k in range(NVAR):
                out[0, k] = a[k]
                out[1, k] = c[k]
            return

        @pl.when(bit(axis, level + 1) == 0)
        def _():
            for k, value in enumerate(union_a(left_v, right_m, right_v)):
                out[k] = value

        @pl.when(bit(axis, level + 1) == 1)
        def _():
            for k, value in enumerate(union_c(left_m, left_v, right_m, right_v)):
                out[k] = value

    @pl.when(bit(axis, level) == 0)
    def _():
        body(own_m, own_v, got_m, got_v)

    @pl.when(bit(axis, level) == 1)
    def _():
        body(got_m, got_v, own_m, own_v)


def join_matrices_kernel(axis, level, last, own, got, out):
    def body(left, right):
        lines = left.shape[3]

        def group(g, _):
            here = pl.ds(pl.multiple_of(g * ROWS, ROWS), ROWS)

            def block_of(ref, which):
                return lambda a, b: ref[which, a, b, here]

            def whole(ref, which):
                return [ref[which, a, b, here] for a in range(NVAR) for b in range(NVAR)]

            def emit(which, matrix):
                for a in range(NVAR):
                    for b in range(NVAR):
                        if last:
                            out[a, b, here] = matrix[NVAR * a + b]
                        else:
                            out[which, a, b, here] = matrix[NVAR * a + b]

            a_left = whole(left, 0)
            through = matmat(block_of(right, 2), a_left)
            emit(2, plus(matmat(block_of(left, 1), through), whole(left, 2)))
            if not last:
                emit(0, matmat(block_of(right, 0), a_left))
                emit(1, matmat(block_of(left, 1), whole(right, 1)))
            return 0

        lax.fori_loop(0, lines // ROWS, group, 0)

    wanted = bit(axis, level + 1) == 1 if last else True

    @pl.when((bit(axis, level) == 0) & wanted)
    def _():
        body(own, got)

    @pl.when((bit(axis, level) == 1) & wanted)
    def _():
        body(got, own)


def descend(axis, levels, refs, f_ref, b_ref):
    top = levels - 1
    got_c, own, got = refs[4 * top : 4 * top + 3]
    shape = f_ref.shape[1:]

    @pl.when(bit(axis, top) == 0)
    def _():
        through = matvec(lambda a, b: got_c[a, b], [own[k] for k in range(NVAR)])
        for k in range(NVAR):
            f_ref[k] = jnp.zeros(shape, F32)
            b_ref[k] = through[k] + got[k]

    @pl.when(bit(axis, top) == 1)
    def _():
        for k in range(NVAR):
            f_ref[k] = got[k]
            b_ref[k] = jnp.zeros(shape, F32)

    for l in reversed(range(top)):
        own_m, got_m, own_v, got_v = refs[4 * l : 4 * l + 4]

        @pl.when(bit(axis, l) == 0)
        def _(own_m=own_m, got_m=got_m, own_v=own_v, got_v=got_v):
            f = [f_ref[k] for k in range(NVAR)]
            b = [b_ref[k] for k in range(NVAR)]
            mid = plus(matvec(block(own_m, 0), f), vec(own_v, 0))
            out = plus(
                plus(matvec(block(got_m, 1), b), matvec(block(got_m, 2), mid)),
                vec(got_v, 1),
            )
            for k in range(NVAR):
                b_ref[k] = out[k]

        @pl.when(bit(axis, l) == 1)
        def _(own_m=own_m, got_m=got_m, own_v=own_v, got_v=got_v):
            f = [f_ref[k] for k in range(NVAR)]
            out = plus(matvec(block(got_m, 0), f), vec(got_v, 0))
            for k in range(NVAR):
                f_ref[k] = out[k]


def middle_kernel(levels, *rest):
    (source, x_lower, x_upper, y_inverse, y_lower, y_upper,
     reduced, y_source, f_ref, b_ref, held) = rest[4 * levels - 1 :]
    cells, rows = source.shape[1:3]
    descend("px", levels, rest, f_ref, b_ref)

    def forward(i, v):
        product = matvec(lambda a, b: x_lower[a, b, i], list(v))
        v = [source[c, i] - product[c] for c in range(NVAR)]
        for c in range(NVAR):
            held[c, pl.ds(pl.multiple_of(i * rows, rows), rows)] = v[c]
        return tuple(v)

    lax.fori_loop(0, cells, forward, tuple(f_ref[k] for k in range(NVAR)), unroll=True)

    def backward(k, w):
        i = cells - 1 - k
        here = pl.ds(pl.multiple_of(i * rows, rows), rows)
        product = matvec(lambda a, b: x_upper[a, b, i], list(w))
        w = [held[c, here] - product[c] for c in range(NVAR)]
        s = matvec(lambda a, b: y_inverse[a, b, here], w)
        for c in range(NVAR):
            y_source[c, here] = s[c]
        return tuple(w)

    lax.fori_loop(0, cells, backward, tuple(b_ref[k] for k in range(NVAR)), unroll=True)

    def line(j):
        return pl.ds(j, cells, stride=rows)

    zero = jnp.zeros((cells, source.shape[3]), F32)

    def y_forward(j, v):
        product = matvec(lambda a, b: y_lower[j, NVAR * a + b], list(v))
        v = [y_source[c, line(j), :] - product[c] for c in range(NVAR)]
        for c in range(NVAR):
            held[c, pl.ds(pl.multiple_of(j * cells, cells), cells)] = v[c]
        return tuple(v)

    v = lax.fori_loop(0, rows, y_forward, (zero,) * NVAR, unroll=True)

    def y_backward(k, w):
        j = rows - 1 - k
        product = matvec(lambda a, b: y_upper[j, NVAR * a + b], list(w))
        here = pl.ds(pl.multiple_of(j * cells, cells), cells)
        return tuple(held[c, here] - product[c] for c in range(NVAR))

    w = lax.fori_loop(0, rows, y_backward, (zero,) * NVAR, unroll=True)
    for c in range(NVAR):
        reduced[0, c] = v[c]
        reduced[1, c] = w[c]


def end_kernel(levels, cells, rows, *rest):
    y_source, y_lower, y_upper, out, f_ref, b_ref, held = rest[4 * levels - 1 :]
    descend("py", levels, rest, f_ref, b_ref)

    def line(j):
        return pl.ds(j, cells, stride=rows)

    def forward(j, v):
        product = matvec(lambda a, b: y_lower[j, NVAR * a + b], list(v))
        v = [y_source[c, line(j), :] - product[c] for c in range(NVAR)]
        for c in range(NVAR):
            held[c, pl.ds(pl.multiple_of(j * cells, cells), cells)] = v[c]
        return tuple(v)

    lax.fori_loop(0, rows, forward, tuple(f_ref[k] for k in range(NVAR)), unroll=True)

    def backward(k, w):
        j = rows - 1 - k
        here = pl.ds(pl.multiple_of(j * cells, cells), cells)
        product = matvec(lambda a, b: y_upper[j, NVAR * a + b], list(w))
        w = [held[c, here] - product[c] for c in range(NVAR)]
        for c in range(NVAR):
            out[c, line(j), :] = w[c]
        return tuple(w)

    lax.fori_loop(0, rows, backward, tuple(b_ref[k] for k in range(NVAR)), unroll=True)


def per_device(field, forcing, x_inverse, x_lower, x_upper, y_inverse, y_lower, y_upper):
    cells, rows, lanes = field.shape[1:]
    x_levels = lax.axis_size("px").bit_length() - 1
    y_levels = lax.axis_size("py").bit_length() - 1

    def swap(value, axis, level):
        pairs = [(i, i ^ (1 << level)) for i in range(lax.axis_size(axis))]
        return lax.ppermute(value, axis, pairs)

    def across(value, axis):
        n = lax.axis_size(axis)
        pairs = [(i, (i + 1) % n) for i in range(1, n, 2)]
        return lax.ppermute(value, axis, pairs + [(j, i) for i, j in pairs])

    flat = lambda m: m.reshape(m.shape[:-3] + (cells * rows, lanes))
    y_inverse, y_lower, y_upper = flat(y_inverse), flat(y_lower), flat(y_upper)

    y_pair, y_cross, x_pair, x_cross = call(
        functools.partial(pack_kernel, cells, rows), "pack",
        [(NVAR, 2, cells, lanes)] * 2 + [(NVAR, 2, rows, lanes)] * 2,
        [flat(field)],
    )
    y_cross, x_cross = across(y_cross, "py"), across(x_cross, "px")
    y_pair, x_pair = swap(y_pair, "py", 0), swap(x_pair, "px", 0)
    halos = (x_pair, x_cross, y_pair, y_cross)

    def exchange(axis, levels, own_m, got_m, own_v, rest):
        operands = []
        for l in range(levels - 1):
            last = l == levels - 2
            next_m = call(functools.partial(join_matrices_kernel, axis, l, last),
                          "join_matrices", [own_m.shape[last:]], [own_m, got_m])
            next_got = swap(next_m, axis, l + 1)
            got_v = swap(own_v, axis, l)
            operands += [own_m, got_m, own_v, got_v]
            held = hold(operands + rest)
            operands, rest = held[: len(operands)], held[len(operands) :]
            own_v = call(functools.partial(join_vectors_kernel, axis, l, last),
                         "join_vectors", [own_v.shape[last:]], operands[-4:])
            own_m, got_m = next_m, next_got
            if not last:
                (got_m,) = hold([got_m], own_v)
        operands += [got_m, own_v, swap(own_v, axis, levels - 1)]
        held = hold(operands + rest)
        return held[: len(operands)], held[len(operands) :]

    y_m, y_lower, y_upper, x_lower, x_upper = call(
        functools.partial(compose_y_kernel, cells, rows), "compose_y",
        [(3, NVAR, NVAR, cells, lanes)] + [(rows, NVAR * NVAR, cells, lanes)] * 2
        + [x_lower.shape] * 2,
        [],
        [(rows, NVAR * NVAR, cells, lanes)] + [y_lower.shape] * 2,
        from_hbm=[y_lower, y_upper, x_lower, x_upper],
        copies=4 * NVAR,
    )
    x_m, forcing, x_inverse, y_inverse = call(
        compose_x_kernel, "compose_x",
        [(3, NVAR, NVAR, rows, lanes), forcing.shape, x_inverse.shape, y_inverse.shape],
        [x_lower, x_upper], [(cells, NVAR * NVAR, ROWS, lanes)],
        from_hbm=[forcing, x_inverse, y_inverse], copies=3 * NVAR,
    )
    kept = [y_m, x_m, forcing, x_inverse, y_inverse, x_lower, x_upper, y_lower, y_upper]
    kept = hold(kept, *halos)
    y_m, x_m, forcing, x_inverse, y_inverse, x_lower, x_upper, y_lower, y_upper = kept
    y_got, x_got = swap(y_m, "py", 0), swap(x_m, "px", 0)
    reduced, source = call(
        local_x_kernel, "local_x",
        [(2, NVAR, rows, lanes), (NVAR, cells, rows, lanes)],
        [field, forcing, *halos, x_inverse, x_lower, x_upper],
        [(NVAR, cells + 4, rows + 2 * ROWS, lanes), (NVAR, cells, rows, lanes)],
    )
    operands, rest = exchange(
        "px", x_levels, x_m, x_got, reduced,
        [source, x_lower, x_upper, y_inverse, y_lower, y_upper],
    )
    y_m, y_got = hold([y_m, y_got], operands[-1])
    reduced, source = call(
        functools.partial(middle_kernel, x_levels), "middle",
        [(2, NVAR, cells, lanes), (NVAR, cells * rows, lanes)],
        operands + rest,
        [(NVAR, rows, lanes), (NVAR, rows, lanes), (NVAR, cells * rows, lanes)],
    )
    operands, rest = exchange("py", y_levels, y_m, y_got, reduced, [source, *rest[-2:]])
    out = call(
        functools.partial(end_kernel, y_levels, cells, rows), "end",
        [(NVAR, cells * rows, lanes)],
        operands + rest,
        [(NVAR, cells, lanes), (NVAR, cells, lanes), (NVAR, cells * rows, lanes)],
        result_in_hbm=True,
    )
    return out.reshape(NVAR, cells, rows, lanes)


def solution(mesh):
    cell = P(None, "px", "py", None)
    blocks = P(None, None, "px", "py", None)
    return jax.shard_map(
        per_device,
        mesh=mesh,
        in_specs=(cell, cell) + (blocks,) * 6,
        out_specs=cell,
        check_vma=False,
    )
```

time: 92.8 us -> 45.7 us (0.49)
  Pallas kernels: 42.7 us -> 9.8 us
  local copies, waits for them, and re-layouts: 11.8 us -> 0.98 us
  waiting for transfers between devices: 11.3 us -> 19.5 us
  starting transfers between devices: 22.3 us -> 15.2 us
  other arithmetic: 2.75 us -> 0 us
  between operations: 1.38 us -> 0.17 us
    pallas_call x11 -> x20, Pallas kernels: 42.7 us -> 9.8 us  [the longest x12 9.79 us: call(): pl.pallas_call(kernel, name=name, out_shape=shapes[0] if single else shap...]
    ppermute x14, waiting for transfers between devices: 11.3 us -> 19.5 us  [the longest x12 19.5 us: swap(): return lax.ppermute(value, axis, pairs)]
    ppermute x14, starting transfers between devices: 22.3 us -> 15.2 us  [the longest x12 9 us: swap(): return lax.ppermute(value, axis, pairs)]
    unnamed x28 -> x4, local copies, waits for them, and re-layouts: 6.72 us -> 0.98 us
    slice x4 -> x0, local copies, waits for them, and re-layouts: 3.21 us -> none  [the longest x2 1.25 us: exchange_vectors(): send = jnp.where(bits[l, 0] == 0, own[0], own[1])]
    squeeze x2 -> x0, local copies, waits for them, and re-layouts: 1.84 us -> none  [exchange_matrices(): got.append(swap(own[l][2], axis, l))]
    select_n x2 -> x0, other arithmetic: 1.55 us -> none  [exchange_vectors(): send = jnp.where(bits[l, 0] == 0, own[0], own[1])]
    and x4 -> x0, other arithmetic: 1.2 us -> none  [bits_of(): lax.axis_index(axis) >> jnp.arange(levels) & 1]
  transfers between devices with their start and end apart: 14 -> 14, of which waited for: 5 -> 7; matrix products, arithmetic and copies ran while one was open for 7% -> 0% of each run, Pallas kernels for 38% -> 18%
where the time goes in v2:
time: 45.7 us; the launch traced here: 45.6 us
  waiting for transfers between devices  19.5 us (43%)
  starting transfers between devices  15.2 us (33%)
  Pallas kernels  9.8 us (21%)
  local copies, waits for them, and re-layouts  0.98 us (2%)
    ppermute x12, waiting for transfers between devices, swap(): return lax.ppermute(value, axis, pairs)  19.5 us
    pallas_call x12, Pallas kernels, call(): pl.pallas_call(kernel, name=name, out_shape=shapes[0] if single else shap...  9.79 us
    ppermute x12, starting transfers between devices, swap(): return lax.ppermute(value, axis, pairs)  9 us
    ppermute x2, starting transfers between devices, across(): return lax.ppermute(value, axis, pairs + [(j, i) for i, j in pairs])  6.16 us
    unnamed x4, local copies, waits for them, and re-layouts  0.98 us
  transfers between devices with their start and end apart: 14, of which 7 were waited for; matrix products, arithmetic and copies ran while one was open for 0% of the time, Pallas kernels for 18%

profile of v2, /device:TPU:0, one launch (start us, length us, event | category | flops | bytes accessed | tf_op | source)
XLA Modules:
  0.0 45.6 jit_solution(10104124977039449437)
XLA Ops:
  0.0 1.0 %copy-done = f32[5,8,16,128]{3,2,1,0:T(8,128)S(1)} copy-done((f32[5,8,16,128]{3,2,1,0:T(8,128)S(1)}, f32[5,8,16,128]{3,2,1,0:T(8,128)}, u32[]{:S(2)}) %copy-start) | copy-done | bytes 327704
  1.0 0.5 %collective-permute-start = (f32[5,2,16,128]{3,2,1,0:T(8,128)S(1)}, f32[5,2,16,128]{3,2,1,0:T(8,128)S(1)}, u32[]{:S(2)}, u32[]{:S(2)}) collective-permute-start(f32[5,2,16,128]{3,2,1,0:T(8,128)S(1)} %get-tuple-element.97), channel_id=1, source_target_pairs={{0,8},{8,0},{16,24},{24,16},{1,9},{9,1},{17,25},{25,17},{2,10},{10... | collective-permute-start | bytes 245768 | tf_op jit(solution)/shard_map/ppermute | solution.py:543
  1.6 2.6 %collective-permute-start.1 = (f32[5,2,16,128]{3,2,1,0:T(8,128)S(1)}, f32[5,2,16,128]{3,2,1,0:T(8,128)S(1)}, u32[]{:S(2)}, u32[]{:S(2)}) collective-permute-start(f32[5,2,16,128]{3,2,1,0:T(8,128)S(1)} %get-tuple-element.98), channel_id=1, source_target_pairs={{8,16},{24,0},{16,8},{0,24},{9,17},{25,1},{17,9},{1,25},{10,18},{2... | collective-permute-start | bytes 245768 | tf_op jit(solution)/shard_map/ppermute | solution.py:548
  4.2 1.5 %collective-permute-start.2 = (f32[5,2,8,128]{3,2,1,0:T(8,128)S(1)}, f32[5,2,8,128]{3,2,1,0:T(8,128)S(1)}, u32[]{:S(2)}, u32[]{:S(2)}) collective-permute-start(f32[5,2,8,128]{3,2,1,0:T(8,128)S(1)} %get-tuple-element.99), channel_id=1, source_target_pairs={{0,1},{1,0},{2,3},{3,2},{4,5},{5,4},{6,7},{7,6},{8,9},{9,8},{10,11... | collective-permute-start | bytes 122888 | tf_op jit(solution)/shard_map/ppermute | solution.py:543
  5.7 3.5 %collective-permute-start.3 = (f32[5,2,8,128]{3,2,1,0:T(8,128)S(1)}, f32[5,2,8,128]{3,2,1,0:T(8,128)S(1)}, u32[]{:S(2)}, u32[]{:S(2)}) collective-permute-start(f32[5,2,8,128]{3,2,1,0:T(8,128)S(1)} %get-tuple-element.100), channel_id=1, source_target_pairs={{1,2},{3,4},{5,6},{7,0},{2,1},{4,3},{6,5},{0,7},{9,10},{11,12},{13... | collective-permute-start | bytes 122888 | tf_op jit(solution)/shard_map/ppermute | solution.py:548
  9.2 4.6 %compose_y.1 = (f32[3,5,5,8,128]{4,3,2,1,0:T(8,128)S(1)}, f32[16,25,8,128]{3,2,1,0:T(8,128)S(1)}, f32[16,25,8,128]{3,2,1,0:T(8,128)S(1)}, f32[5,5,8,16,128]{4,3,2,1,0:T(8,128)S(1)}, f32[5,5,8,16,128]{4,3,2,1,0:T(8,128)S(1)}) custom-call(f32[5,5,128,128]{3,2,1,0:T(8,128)} %bitcast.6, f32[5,5,128,128]{3,2,1,0:T(8,128)} %bitcast.7, ...), custom_call_target="tpu_custom_call" | custom-call | tf_op jit(solution)/shard_map/compose_y/pallas_call | solution.py:26
  13.8 2.2 %compose_x.1 = (f32[3,5,5,16,128]{4,3,2,1,0:T(8,128)S(1)}, f32[5,8,16,128]{3,2,1,0:T(8,128)S(1)}, f32[5,5,8,16,128]{4,3,2,1,0:T(8,128)S(1)}, f32[5,5,128,128]{3,2,1,0:T(8,128)S(1)}) custom-call(f32[5,5,8,16,128]{4,3,2,1,0:T(8,128)S(1)} %get-tuple-element.89.lower.refs_5_, f32[5,5,8,16,128]{4,3,2,1,0:T(8,128)S(1)} %get-tuple-element.90.upper.refs_6_, ...), custom_call_target="tpu_custom_call" | custom-call | tf_op jit(solution)/shard_map/compose_x/pallas_call | solution.py:26
  16.2 1.9 %collective-permute-done.5.refs_1_.got = f32[3,5,5,16,128]{4,3,2,1,0:T(8,128)S(1)} collective-permute-done((f32[3,5,5,16,128]{4,3,2,1,0:T(8,128)S(1)}, f32[3,5,5,16,128]{4,3,2,1,0:T(8,128)S(1)}, u32[]{:S(2)}, u32[]{:S(2)}) %collective-permute-start.5) | collective-permute-done | bytes 614432 | tf_op jit(solution)/shard_map/ppermute | solution.py:543
  18.2 0.8 %collective-permute-start.7 = (f32[5,5,16,128]{3,2,1,0:T(8,128)S(1)}, f32[5,5,16,128]{3,2,1,0:T(8,128)S(1)}, u32[]{:S(2)}, u32[]{:S(2)}) collective-permute-start(f32[5,5,16,128]{3,2,1,0:T(8,128)S(1)} %join_matrices.3), channel_id=1, source_target_pairs={{0,16},{8,24},{16,0},{24,8},{1,17},{9,25},{17,1},{25,9},{2,18},{10... | collective-permute-start | bytes 614408 | tf_op jit(solution)/shard_map/ppermute | solution.py:543
  19.0 0.8 %local_x.1 = (f32[2,5,16,128]{3,2,1,0:T(8,128)S(1)}, f32[5,8,16,128]{3,2,1,0:T(8,128)S(1)}) custom-call(f32[5,8,16,128]{3,2,1,0:T(8,128)S(1)} %copy-done.1, f32[5,8,16,128]{3,2,1,0:T(8,128)S(1)} %get-tuple-element.103.forcing, f32[5,2,16,128]{3,2,1,0:T(8,128)S(1)} %collective-permute-done.refs_9_.x_pair, ...), custom_call_target="tpu_custom_call" | custom-call | tf_op jit(solution)/shard_map/local_x/pallas_call | solution.py:26
  19.8 1.3 %collective-permute-done.6.refs_3_ = f32[2,5,16,128]{3,2,1,0:T(8,128)S(1)} collective-permute-done((f32[2,5,16,128]{3,2,1,0:T(8,128)S(1)}, f32[2,5,16,128]{3,2,1,0:T(8,128)S(1)}, u32[]{:S(2)}, u32[]{:S(2)}) %collective-permute-start.6) | collective-permute-done | bytes 81952 | tf_op jit(solution)/shard_map/ppermute | solution.py:543
  21.1 1.4 %collective-permute-start.8 = (f32[5,16,128]{2,1,0:T(8,128)S(1)}, f32[5,16,128]{2,1,0:T(8,128)S(1)}, u32[]{:S(2)}, u32[]{:S(2)}) collective-permute-start(f32[5,16,128]{2,1,0:T(8,128)S(1)} %join_vectors.3.refs_5_), channel_id=1, source_target_pairs={{0,16},{8,24},{16,0},{24,8},{1,17},{9,25},{17,1},{25,9},{2,18},{10... | collective-permute-start | bytes 122888 | tf_op jit(solution)/shard_map/ppermute | solution.py:543
  22.5 3.7 %collective-permute-done.8.refs_6_ = f32[5,16,128]{2,1,0:T(8,128)S(1)} collective-permute-done((f32[5,16,128]{2,1,0:T(8,128)S(1)}, f32[5,16,128]{2,1,0:T(8,128)S(1)}, u32[]{:S(2)}, u32[]{:S(2)}) %collective-permute-start.8) | collective-permute-done | bytes 40992 | tf_op jit(solution)/shard_map/ppermute | solution.py:543
  26.2 0.1 join_matrices.4.refs_4_.own
  26.4 0.8 %middle.1 = (f32[2,5,8,128]{3,2,1,0:T(8,128)S(1)}, f32[5,128,128]{2,1,0:T(8,128)S(1)}) custom-call(f32[3,5,5,16,128]{4,3,2,1,0:T(8,128)S(1)} %get-tuple-element.125.rest_0_, f32[3,5,5,16,128]{4,3,2,1,0:T(8,128)S(1)} %get-tuple-element.126.rest_1_, f32[2,5,16,128]{3,2,1,0:T(8,128)S(1)} %get-tuple-element.127.rest_2_, ...), custom_call_target="tpu_custom_call" | custom-call | tf_op jit(solution)/shard_map/middle/pallas_call | solution.py:26
  27.2 1.1 %collective-permute-start.9 = (f32[2,5,8,128]{3,2,1,0:T(8,128)S(1)}, f32[2,5,8,128]{3,2,1,0:T(8,128)S(1)}, u32[]{:S(2)}, u32[]{:S(2)}) collective-permute-start(f32[2,5,8,128]{3,2,1,0:T(8,128)S(1)} %get-tuple-element.137.refs_2_), channel_id=1, source_target_pairs={{0,1},{1,0},{2,3},{3,2},{4,5},{5,4},{6,7},{7,6},{8,9},{9,8},{10,11... | collective-permute-start | bytes 122888 | tf_op jit(solution)/shard_map/ppermute | solution.py:543
  28.3 3.0 %collective-permute-done.9.refs_3_ = f32[2,5,8,128]{3,2,1,0:T(8,128)S(1)} collective-permute-done((f32[2,5,8,128]{3,2,1,0:T(8,128)S(1)}, f32[2,5,8,128]{3,2,1,0:T(8,128)S(1)}, u32[]{:S(2)}, u32[]{:S(2)}) %collective-permute-start.9) | collective-permute-done | bytes 40992 | tf_op jit(solution)/shard_map/ppermute | solution.py:543
  31.3 3.6 %collective-permute-done.10.refs_0_ = f32[3,5,5,8,128]{4,3,2,1,0:T(8,128)S(1)} collective-permute-done((f32[3,5,5,8,128]{4,3,2,1,0:T(8,128)S(1)}, f32[3,5,5,8,128]{4,3,2,1,0:T(8,128)S(1)}, u32[]{:S(2)}, u32[]{:S(2)}) %collective-permute-start.10) | collective-permute-done | bytes 307232 | tf_op jit(solution)/shard_map/ppermute | solution.py:543
  34.9 0.6 %collective-permute-start.12 = (f32[5,5,8,128]{3,2,1,0:T(8,128)S(1)}, f32[5,5,8,128]{3,2,1,0:T(8,128)S(1)}, u32[]{:S(2)}, u32[]{:S(2)}) collective-permute-start(f32[5,5,8,128]{3,2,1,0:T(8,128)S(1)} %join_matrices.5), channel_id=1, source_target_pairs={{0,4},{1,5},{2,6},{3,7},{4,0},{5,1},{6,2},{7,3},{8,12},{9,13},{10,... | collective-permute-start | bytes 307208 | tf_op jit(solution)/shard_map/ppermute | solution.py:543
  35.6 0.5 %collective-permute-start.11 = (f32[2,5,8,128]{3,2,1,0:T(8,128)S(1)}, f32[2,5,8,128]{3,2,1,0:T(8,128)S(1)}, u32[]{:S(2)}, u32[]{:S(2)}) collective-permute-start(f32[2,5,8,128]{3,2,1,0:T(8,128)S(1)} %join_vectors.4.refs_1_.refs_6_), channel_id=1, source_target_pairs={{0,2},{1,3},{2,0},{3,1},{4,6},{5,7},{6,4},{7,5},{8,10},{9,11},{10,... | collective-permute-start | bytes 122888 | tf_op jit(solution)/shard_map/ppermute | solution.py:543
  36.1 3.5 %collective-permute-done.11.refs_7_ = f32[2,5,8,128]{3,2,1,0:T(8,128)S(1)} collective-permute-done((f32[2,5,8,128]{3,2,1,0:T(8,128)S(1)}, f32[2,5,8,128]{3,2,1,0:T(8,128)S(1)}, u32[]{:S(2)}, u32[]{:S(2)}) %collective-permute-start.11) | collective-permute-done | bytes 40992 | tf_op jit(solution)/shard_map/ppermute | solution.py:543
  39.6 2.3 %collective-permute-start.13 = (f32[5,8,128]{2,1,0:T(8,128)S(1)}, f32[5,8,128]{2,1,0:T(8,128)S(1)}, u32[]{:S(2)}, u32[]{:S(2)}) collective-permute-start(f32[5,8,128]{2,1,0:T(8,128)S(1)} %join_vectors.5.refs_9_), channel_id=1, source_target_pairs={{0,4},{1,5},{2,6},{3,7},{4,0},{5,1},{6,2},{7,3},{8,12},{9,13},{10,... | collective-permute-start | bytes 61448 | tf_op jit(solution)/shard_map/ppermute | solution.py:543
  41.9 2.4 %collective-permute-done.13.refs_10_ = f32[5,8,128]{2,1,0:T(8,128)S(1)} collective-permute-done((f32[5,8,128]{2,1,0:T(8,128)S(1)}, f32[5,8,128]{2,1,0:T(8,128)S(1)}, u32[]{:S(2)}, u32[]{:S(2)}) %collective-permute-start.13) | collective-permute-done | bytes 20512 | tf_op jit(solution)/shard_map/ppermute | solution.py:543
  44.4 1.2 %end.1 = f32[5,128,128]{2,1,0:T(8,128)} custom-call(f32[3,5,5,8,128]{4,3,2,1,0:T(8,128)S(1)} %get-tuple-element.157.rest_0_, f32[3,5,5,8,128]{4,3,2,1,0:T(8,128)S(1)} %get-tuple-element.158.rest_1_, f32[2,5,8,128]{3,2,1,0:T(8,128)S(1)} %get-tuple-element.159.rest_2_, f32[2,5,8,128]{3,2,1,0:T(8,128)S(1)} %get-tuple-element.160.rest_3_, ...), custom_call_target="tpu_custom_call" | custom-call | tf_op jit(solution)/shard_map/end/pallas_call | solution.py:26
  (28 shorter events, 0.5 us)
Async XLA Ops:
  0.0 1.0 %copy-start = (f32[5,8,16,128]{3,2,1,0:T(8,128)S(1)}, f32[5,8,16,128]{3,2,1,0:T(8,128)}, u32[]{:S(2)}) copy-start(f32[5,8,16,128]{3,2,1,0:T(8,128)} %field.1) | copy-start | bytes 983044
  1.0 15.0 %collective-permute-start = (f32[5,2,16,128]{3,2,1,0:T(8,128)S(1)}, f32[5,2,16,128]{3,2,1,0:T(8,128)S(1)}, u32[]{:S(2)}, u32[]{:S(2)}) collective-permute-start(f32[5,2,16,128]{3,2,1,0:T(8,128)S(1)} %get-tuple-element.97), channel_id=1, source_target_pairs={{0,8},{8,0},{16,24},{24,16},{1,9},{9,1},{17,25},{25,17},{2,10},{10... | collective-permute-start | bytes 245768 | tf_op jit(solution)/shard_map/ppermute | solution.py:543
  1.6 14.5 %collective-permute-start.1 = (f32[5,2,16,128]{3,2,1,0:T(8,128)S(1)}, f32[5,2,16,128]{3,2,1,0:T(8,128)S(1)}, u32[]{:S(2)}, u32[]{:S(2)}) collective-permute-start(f32[5,2,16,128]{3,2,1,0:T(8,128)S(1)} %get-tuple-element.98), channel_id=1, source_target_pairs={{8,16},{24,0},{16,8},{0,24},{9,17},{25,1},{17,9},{1,25},{10,18},{2... | collective-permute-start | bytes 245768 | tf_op jit(solution)/shard_map/ppermute | solution.py:548
  4.2 11.9 %collective-permute-start.2 = (f32[5,2,8,128]{3,2,1,0:T(8,128)S(1)}, f32[5,2,8,128]{3,2,1,0:T(8,128)S(1)}, u32[]{:S(2)}, u32[]{:S(2)}) collective-permute-start(f32[5,2,8,128]{3,2,1,0:T(8,128)S(1)} %get-tuple-element.99), channel_id=1, source_target_pairs={{0,1},{1,0},{2,3},{3,2},{4,5},{5,4},{6,7},{7,6},{8,9},{9,8},{10,11... | collective-permute-start | bytes 122888 | tf_op jit(solution)/shard_map/ppermute | solution.py:543
  5.7 10.4 %collective-permute-start.3 = (f32[5,2,8,128]{3,2,1,0:T(8,128)S(1)}, f32[5,2,8,128]{3,2,1,0:T(8,128)S(1)}, u32[]{:S(2)}, u32[]{:S(2)}) collective-permute-start(f32[5,2,8,128]{3,2,1,0:T(8,128)S(1)} %get-tuple-element.100), channel_id=1, source_target_pairs={{1,2},{3,4},{5,6},{7,0},{2,1},{4,3},{6,5},{0,7},{9,10},{11,12},{13... | collective-permute-start | bytes 122888 | tf_op jit(solution)/shard_map/ppermute | solution.py:548
  16.1 2.9 %copy-start.1 = (f32[5,8,16,128]{3,2,1,0:T(8,128)S(1)}, f32[5,8,16,128]{3,2,1,0:T(8,128)}, u32[]{:S(2)}) copy-start(f32[5,8,16,128]{3,2,1,0:T(8,128)} %field.1) | copy-start | bytes 983044
  16.1 2.1 %collective-permute-start.5 = (f32[3,5,5,16,128]{4,3,2,1,0:T(8,128)S(1)}, f32[3,5,5,16,128]{4,3,2,1,0:T(8,128)S(1)}, u32[]{:S(2)}, u32[]{:S(2)}) collective-permute-start(f32[3,5,5,16,128]{4,3,2,1,0:T(8,128)S(1)} %get-tuple-element.102.refs_0_.own), channel_id=1, source_target_pairs={{0,8},{8,0},{16,24},{24,16},{1,9},{9,1},{17,25},{25,17},{2,10},{10... | collective-permute-start | bytes 1843208 | tf_op jit(solution)/shard_map/ppermute | solution.py:543
  16.2 10.0 %collective-permute-start.4 = (f32[3,5,5,8,128]{4,3,2,1,0:T(8,128)S(1)}, f32[3,5,5,8,128]{4,3,2,1,0:T(8,128)S(1)}, u32[]{:S(2)}, u32[]{:S(2)}) collective-permute-start(f32[3,5,5,8,128]{4,3,2,1,0:T(8,128)S(1)} %get-tuple-element.101.refs_0_), channel_id=1, source_target_pairs={{0,1},{1,0},{2,3},{3,2},{4,5},{5,4},{6,7},{7,6},{8,9},{9,8},{10,11... | collective-permute-start | bytes 921608 | tf_op jit(solution)/shard_map/ppermute | solution.py:543
  18.2 8.0 %collective-permute-start.7 = (f32[5,5,16,128]{3,2,1,0:T(8,128)S(1)}, f32[5,5,16,128]{3,2,1,0:T(8,128)S(1)}, u32[]{:S(2)}, u32[]{:S(2)}) collective-permute-start(f32[5,5,16,128]{3,2,1,0:T(8,128)S(1)} %join_matrices.3), channel_id=1, source_target_pairs={{0,16},{8,24},{16,0},{24,8},{1,17},{9,25},{17,1},{25,9},{2,18},{10... | collective-permute-start | bytes 614408 | tf_op jit(solution)/shard_map/ppermute | solution.py:543
  19.7 1.3 %collective-permute-start.6 = (f32[2,5,16,128]{3,2,1,0:T(8,128)S(1)}, f32[2,5,16,128]{3,2,1,0:T(8,128)S(1)}, u32[]{:S(2)}, u32[]{:S(2)}) collective-permute-start(f32[2,5,16,128]{3,2,1,0:T(8,128)S(1)} %get-tuple-element.107.refs_2_), channel_id=1, source_target_pairs={{0,8},{8,0},{16,24},{24,16},{1,9},{9,1},{17,25},{25,17},{2,10},{10... | collective-permute-start | bytes 245768 | tf_op jit(solution)/shard_map/ppermute | solution.py:543
  21.1 5.1 %collective-permute-start.8 = (f32[5,16,128]{2,1,0:T(8,128)S(1)}, f32[5,16,128]{2,1,0:T(8,128)S(1)}, u32[]{:S(2)}, u32[]{:S(2)}) collective-permute-start(f32[5,16,128]{2,1,0:T(8,128)S(1)} %join_vectors.3.refs_5_), channel_id=1, source_target_pairs={{0,16},{8,24},{16,0},{24,8},{1,17},{9,25},{17,1},{25,9},{2,18},{10... | collective-permute-start | bytes 122888 | tf_op jit(solution)/shard_map/ppermute | solution.py:543
  26.4 8.6 %collective-permute-start.10 = (f32[3,5,5,8,128]{4,3,2,1,0:T(8,128)S(1)}, f32[3,5,5,8,128]{4,3,2,1,0:T(8,128)S(1)}, u32[]{:S(2)}, u32[]{:S(2)}) collective-permute-start(f32[3,5,5,8,128]{4,3,2,1,0:T(8,128)S(1)} %join_matrices.4.refs_4_.own), channel_id=1, source_target_pairs={{0,2},{1,3},{2,0},{3,1},{4,6},{5,7},{6,4},{7,5},{8,10},{9,11},{10,... | collective-permute-start | bytes 921608 | tf_op jit(solution)/shard_map/ppermute | solution.py:543
  27.2 4.1 %collective-permute-start.9 = (f32[2,5,8,128]{3,2,1,0:T(8,128)S(1)}, f32[2,5,8,128]{3,2,1,0:T(8,128)S(1)}, u32[]{:S(2)}, u32[]{:S(2)}) collective-permute-start(f32[2,5,8,128]{3,2,1,0:T(8,128)S(1)} %get-tuple-element.137.refs_2_), channel_id=1, source_target_pairs={{0,1},{1,0},{2,3},{3,2},{4,5},{5,4},{6,7},{7,6},{8,9},{9,8},{10,11... | collective-permute-start | bytes 122888 | tf_op jit(solution)/shard_map/ppermute | solution.py:543
  34.9 9.4 %collective-permute-start.12 = (f32[5,5,8,128]{3,2,1,0:T(8,128)S(1)}, f32[5,5,8,128]{3,2,1,0:T(8,128)S(1)}, u32[]{:S(2)}, u32[]{:S(2)}) collective-permute-start(f32[5,5,8,128]{3,2,1,0:T(8,128)S(1)} %join_matrices.5), channel_id=1, source_target_pairs={{0,4},{1,5},{2,6},{3,7},{4,0},{5,1},{6,2},{7,3},{8,12},{9,13},{10,... | collective-permute-start | bytes 307208 | tf_op jit(solution)/shard_map/ppermute | solution.py:543
  35.6 4.0 %collective-permute-start.11 = (f32[2,5,8,128]{3,2,1,0:T(8,128)S(1)}, f32[2,5,8,128]{3,2,1,0:T(8,128)S(1)}, u32[]{:S(2)}, u32[]{:S(2)}) collective-permute-start(f32[2,5,8,128]{3,2,1,0:T(8,128)S(1)} %join_vectors.4.refs_1_.refs_6_), channel_id=1, source_target_pairs={{0,2},{1,3},{2,0},{3,1},{4,6},{5,7},{6,4},{7,5},{8,10},{9,11},{10,... | collective-permute-start | bytes 122888 | tf_op jit(solution)/shard_map/ppermute | solution.py:543
  39.6 4.7 %collective-permute-start.13 = (f32[5,8,128]{2,1,0:T(8,128)S(1)}, f32[5,8,128]{2,1,0:T(8,128)S(1)}, u32[]{:S(2)}, u32[]{:S(2)}) collective-permute-start(f32[5,8,128]{2,1,0:T(8,128)S(1)} %join_vectors.5.refs_9_), channel_id=1, source_target_pairs={{0,4},{1,5},{2,6},{3,7},{4,0},{5,1},{6,2},{7,3},{8,12},{9,13},{10,... | collective-permute-start | bytes 61448 | tf_op jit(solution)/shard_map/ppermute | solution.py:543

commit v3 on v2

v3 whole, which is shorter than its diff:
```python
import functools

import jax
import jax.numpy as jnp
from jax import lax
from jax.experimental import pallas as pl
from jax.experimental.pallas import tpu as pltpu
from jax.sharding import PartitionSpec as P

DISSIPATION = 0.1
NVAR = 5
F32 = jnp.float32
ROWS = 8
UNROLL = 3
MATRICES = 3 * NVAR * NVAR
VX = 5
PIECES = {"px": (25,), "py": (13, 12)}
VMEM_BYTES = 12 * 1024 * 1024


def call(kernel, name, out_shapes, operands, scratch=(), result_in_hbm=False, from_hbm=(),
         copies=0):
    vmem = pl.BlockSpec(memory_space=pltpu.VMEM)
    make = jax.ShapeDtypeStruct if result_in_hbm else pltpu.VMEM
    shapes = [make(s, F32) for s in out_shapes]
    single = len(shapes) == 1
    operands = [pltpu.with_memory_space_constraint(x, pltpu.VMEM) for x in operands]
    outer = [pltpu.with_memory_space_constraint(x, pltpu.HBM) for x in from_hbm]
    semaphores = [pltpu.SemaphoreType.DMA((copies,))] if copies else []
    return pl.pallas_call(
        kernel,
        name=name,
        out_shape=shapes[0] if single else shapes,
        in_specs=[vmem] * len(operands) + [pl.BlockSpec(memory_space=pltpu.HBM)] * len(outer),
        out_specs=vmem if single else [vmem] * len(shapes),
        scratch_shapes=[pltpu.VMEM(s, F32) for s in scratch] + semaphores,
        compiler_params=pltpu.CompilerParams(vmem_limit_bytes=VMEM_BYTES),
    )(*operands, *outer)


def hold(arrays, *others):
    def nothing(*refs):
        pass

    operands = [pltpu.with_memory_space_constraint(x, pltpu.VMEM) for x in (*arrays, *others)]
    anywhere = pl.BlockSpec(memory_space=pl.ANY)
    held = pl.pallas_call(
        nothing,
        name="hold",
        out_shape=[pltpu.VMEM(x.shape, F32) for x in arrays],
        in_specs=[anywhere] * len(operands),
        out_specs=[anywhere] * len(arrays),
        input_output_aliases={k: k for k in range(len(arrays))},
        compiler_params=pltpu.CompilerParams(vmem_limit_bytes=1024 * 1024),
    )(*operands)
    return list(held)


def bit(axis, level):
    return (lax.axis_index(axis) >> level) & 1


def tree(terms):
    while len(terms) > 1:
        pairs = [terms[k] + terms[k + 1] for k in range(0, len(terms) - 1, 2)]
        terms = pairs + (terms[-1:] if len(terms) % 2 else [])
    return terms[0]


def matvec(load, vector):
    return [tree([load(a, b) * vector[b] for b in range(NVAR)]) for a in range(NVAR)]


def matmat(load, matrix):
    out = []
    for a in range(NVAR):
        row = [load(a, b) for b in range(NVAR)]
        for c in range(NVAR):
            out.append(tree([row[b] * matrix[NVAR * b + c] for b in range(NVAR)]))
    return out


def plus(left, right):
    return [p + q for p, q in zip(left, right, strict=True)]


def minus(left, right):
    return [p - q for p, q in zip(left, right, strict=True)]


def compose_lines(length, lower_at, upper_at, store_p, load_p, emit):
    entries = [(a, b) for a in range(NVAR) for b in range(NVAR)]
    signed = lambda m: [-q for q in m] if length % 2 else list(m)
    first = [lower_at(0, a, b) for a, b in entries]
    store_p(0, first)

    def forward(i, p):
        p = matmat(lambda a, b: lower_at(i, a, b), p)
        store_p(i, p)
        return tuple(p)

    last = lax.fori_loop(1, length, forward, tuple(first), unroll=UNROLL)
    emit(0, signed(last))

    def backward(k, carried):
        w, r = carried
        i = length - 1 - k
        here = [upper_at(i, a, b) for a, b in entries]
        at = lambda a, b: here[NVAR * a + b]
        return tuple(plus(load_p(i), matmat(at, w))), tuple(matmat(at, r))

    r = tuple(upper_at(length - 1, a, b) for a, b in entries)
    w, r = lax.fori_loop(1, length, backward, (last, r), unroll=UNROLL)
    emit(1, signed(r))
    emit(2, [-q for q in w])


def compose_x_kernel(cells, lower, upper, _, field, y_inverse_hbm, out, y_inverse, held, semaphores):
    load = pltpu.make_async_copy(y_inverse_hbm, y_inverse, semaphores.at[0])
    load.start()
    rows = lower.shape[3]

    for side, first in enumerate((cells - 2, 0)):

        @pl.when(bit("px", 0) == side)
        def _(first=first):
            for c in range(NVAR):
                for k in range(2):
                    out[MATRICES + 2 * c + k] = field[c, pl.ds((first + k) * rows, rows), :]

    def group(g, _):
        here = pl.ds(pl.multiple_of(g * ROWS, ROWS), ROWS)

        def emit(which, matrix):
            for a in range(NVAR):
                for b in range(NVAR):
                    out[entry(which, a, b), here] = matrix[NVAR * a + b]

        def store_p(i, p):
            for k in range(NVAR * NVAR):
                held[i, k] = p[k]

        compose_lines(
            cells,
            lambda i, a, b: lower[a, b, i, here],
            lambda i, a, b: upper[a, b, i, here],
            store_p,
            lambda i: [held[i, k] for k in range(NVAR * NVAR)],
            emit,
        )
        return 0

    lax.fori_loop(0, rows // ROWS, group, 0)
    load.wait()


def compose_y_kernel(lower, upper, out, held):
    cells_y = lower.shape[1]

    def emit(which, matrix):
        for a in range(NVAR):
            for b in range(NVAR):
                out[entry(which, a, b)] = matrix[NVAR * a + b]

    def store_p(i, p):
        for k in range(NVAR * NVAR):
            held[i, k] = p[k]

    compose_lines(
        cells_y,
        lambda j, a, b: lower[NVAR * a + b, j],
        lambda j, a, b: upper[NVAR * a + b, j],
        store_p,
        lambda i: [held[i, k] for k in range(NVAR * NVAR)],
        emit,
    )


def local_x_kernel(
    field, forcing, x_got, x_cross, y_pair, y_cross, inverse, lower, upper,
    reduced, source_out, padded, held,
):
    cells, rows, lanes = field.shape[1:]
    zero = jnp.zeros((rows, lanes), F32)
    middle = pl.ds(ROWS, rows)
    for c in range(NVAR):
        for i in range(cells):
            padded[c, i + 2, middle] = field[c, i]

    def x_pair(c, k):
        return x_got[MATRICES + 2 * c + k]

    def y_before(value):
        for c in range(NVAR):
            for k in range(2):
                for i in range(cells):
                    padded[c, i + 2, ROWS - 2 + k] = value(c, k, i)

    def y_after(value):
        for c in range(NVAR):
            for k in range(2):
                for i in range(cells):
                    padded[c, i + 2, ROWS + rows + k] = value(c, k, i)

    def x_before(value):
        for c in range(NVAR):
            for k in range(2):
                padded[c, k, middle] = value(c, k)

    def x_after(value):
        for c in range(NVAR):
            for k in range(2):
                padded[c, cells + 2 + k, middle] = value(c, k)

    for axis, before, behind, pair, cross, empty in (
        ("px", x_before, x_after, x_pair, x_cross, jnp.zeros((rows, lanes), F32)),
        ("py", y_before, y_after, lambda *k: y_pair[k], y_cross, jnp.zeros((lanes,), F32)),
    ):
        at, count = lax.axis_index(axis), lax.axis_size(axis)

        @pl.when(bit(axis, 0) == 0)
        def _(before=before, behind=behind, pair=pair, cross=cross):
            before(lambda *k: cross[k])
            behind(pair)

        @pl.when(bit(axis, 0) == 1)
        def _(before=before, behind=behind, pair=pair, cross=cross):
            before(pair)
            behind(lambda *k: cross[k])

        @pl.when(at == 0)
        def _(before=before, empty=empty):
            before(lambda *k: empty)

        @pl.when(at == count - 1)
        def _(behind=behind, empty=empty):
            behind(lambda *k: empty)

    def right_side(i):
        out = []
        for c in range(NVAR):
            centre = padded[c, i + 2, middle]
            along_x = (
                padded[c, i, middle] - 4.0 * padded[c, i + 1, middle] + 6.0 * centre
                - 4.0 * padded[c, i + 3, middle] + padded[c, i + 4, middle]
            )
            along_y = (
                padded[c, i + 2, pl.ds(ROWS - 2, rows)]
                - 4.0 * padded[c, i + 2, pl.ds(ROWS - 1, rows)]
                + 6.0 * centre
                - 4.0 * padded[c, i + 2, pl.ds(ROWS + 1, rows)]
                + padded[c, i + 2, pl.ds(ROWS + 2, rows)]
            )
            out.append(forcing[c, i] - DISSIPATION * (along_x + along_y))
        return out

    def forward(i, v):
        s = matvec(lambda a, b: inverse[a, b, i], right_side(i))
        for c in range(NVAR):
            source_out[c, i] = s[c]
        v = minus(s, matvec(lambda a, b: lower[a, b, i], list(v)))
        for c in range(NVAR):
            held[c, i] = v[c]
        return tuple(v)

    v = lax.fori_loop(0, cells, forward, (zero,) * NVAR, unroll=True)
    for c in range(NVAR):
        reduced[0, c] = v[c]

    def backward(k, w):
        i = cells - 1 - k
        product = matvec(lambda a, b: upper[a, b, i], list(w))
        return tuple(held[c, i] - product[c] for c in range(NVAR))

    w = lax.fori_loop(0, cells, backward, (zero,) * NVAR, unroll=True)
    for c in range(NVAR):
        reduced[1, c] = w[c]


def vec(ref, which):
    return [ref[which, c] for c in range(NVAR)]


def entry(which, a, b):
    return (which * NVAR + a) * NVAR + b


def block(matrices, which, rows=slice(None)):
    return lambda a, b: matrices[entry(which, a, b), rows]


def whole(load):
    return [load(a, b) for a in range(NVAR) for b in range(NVAR)]


def in_order(axis, level, radix, bundles, then):
    place = (lax.axis_index(axis) >> level) & (radix - 1)
    for q in range(radix):

        @pl.when(place == q)
        def _(q=q):
            then(q, [bundles[m ^ q] for m in range(radix)])


def pack_kernel(cells, rows, field_hbm, lower_hbm, upper_hbm,
                y_pair, y_cross, x_cross, field, lower, upper, semaphores):
    first = pltpu.make_async_copy(field_hbm, field, semaphores.at[0])
    first.start()
    copies = []
    for source, target in ((lower_hbm, lower), (upper_hbm, upper)):
        for x in range(cells):
            copy = pltpu.make_async_copy(
                source.at[:, pl.ds(x * rows, rows), :],
                target.at[:, :, x, :],
                semaphores.at[1 + len(copies)],
            )
            copy.start()
            copies.append(copy)
    first.wait()

    def y_layers(out, j):
        for c in range(NVAR):
            for k in range(2):
                out[c, k] = field[c, pl.ds(j + k, cells, stride=rows), :]

    def x_layers(out, i):
        for c in range(NVAR):
            for k in range(2):
                out[c, k] = field[c, pl.ds((i + k) * rows, rows), :]

    @pl.when(bit("py", 0) == 0)
    def _():
        y_layers(y_pair, rows - 2)
        y_layers(y_cross, 0)

    @pl.when(bit("py", 0) == 1)
    def _():
        y_layers(y_pair, 0)
        y_layers(y_cross, rows - 2)

    for side, first_layer in enumerate((0, cells - 2)):

        @pl.when(bit("px", 0) == side)
        def _(first_layer=first_layer):
            x_layers(x_cross, first_layer)

    for copy in copies:
        copy.wait()


def grouped(refs, radix):
    return list(zip(refs[:radix], refs[radix : 2 * radix], strict=True))


def inflows(group, f):
    out = [f]
    for matrices, vectors in group:
        a = vec(vectors, 0)
        f = a if f is None else plus(matvec(block(matrices, 0), f), a)
        out.append(f)
    return out


def outflow(stretch, f, b):
    matrices, vectors = stretch
    out = vec(vectors, 1)
    if f is not None:
        out = plus(out, matvec(block(matrices, 2), f))
    if b is not None:
        out = plus(out, matvec(block(matrices, 1), b))
    return out


def join_vectors_kernel(axis, level, radix, last, *refs):
    out = refs[-1]

    def union_a(group):
        return inflows(group, None)[-1]

    def union_c(group):
        f, b = inflows(group[:-1], None), None
        for k in reversed(range(radix)):
            b = outflow(group[k], f[k], b)
        return b

    def then(q, group):
        if not last:
            for which, values in enumerate((union_a(group), union_c(group))):
                for k in range(NVAR):
                    out[which, k] = values[k]
            return

        for side, union in enumerate((union_a, union_c)):

            @pl.when(bit(axis, level + radix.bit_length() - 1) == side)
            def _(union=union):
                for k, value in enumerate(union(group)):
                    out[k] = value

    in_order(axis, level, radix, grouped(refs, radix), then)


def piece_of(axis, k):
    for piece, size in enumerate(PIECES[axis]):
        if k < size:
            return piece, k
        k -= size


def join_matrices_kernel(axis, level, radix, last, *refs):
    bundles, outs = refs[:radix], refs[radix:]
    lines = outs[0].shape[-2]

    def then(q, group):
        def register(g, _):
            here = pl.ds(pl.multiple_of(g * ROWS, ROWS), ROWS)
            at = lambda m, which: block(m, which, here)

            def emit(which, matrix):
                for k, value in enumerate(matrix):
                    if last:
                        piece, at_k = piece_of(axis, k)
                        outs[piece][at_k, here] = value
                    else:
                        outs[0][which * NVAR * NVAR + k, here] = value

            f = [None, whole(at(group[0], 0))]
            for m in group[1:-1]:
                f.append(matmat(at(m, 0), f[-1]))
            if not last:
                emit(0, matmat(at(group[-1], 0), f[-1]))
                r = whole(at(group[-1], 1))
                for m in reversed(group[:-1]):
                    r = matmat(at(m, 1), r)
                emit(1, r)
            c = matmat(at(group[-1], 2), f[-1])
            for k in reversed(range(1, radix - 1)):
                c = plus(matmat(at(group[k], 1), c), matmat(at(group[k], 2), f[k]))
            emit(2, plus(matmat(at(group[0], 1), c), whole(at(group[0], 2))))
            return 0

        lax.fori_loop(0, lines // ROWS, register, 0)

    wanted = bit(axis, level + radix.bit_length() - 1) == 1 if last else True

    @pl.when(wanted)
    def _():
        in_order(axis, level, radix, bundles, then)


def descend(axis, radices, refs, f_ref, b_ref):
    sizes = [2 * r for r in radices[:-1]]
    levels = [sum(r.bit_length() - 1 for r in radices[:t]) for t in range(len(radices))]
    *c_pieces, own, got = refs[sum(sizes) : descend_count(axis, radices)]
    shape = f_ref.shape[1:]

    def got_c(a, b):
        piece, at_k = piece_of(axis, NVAR * a + b)
        return c_pieces[piece][at_k]

    @pl.when(bit(axis, levels[-1]) == 0)
    def _():
        through = matvec(got_c, [own[k] for k in range(NVAR)])
        for k in range(NVAR):
            f_ref[k] = jnp.zeros(shape, F32)
            b_ref[k] = through[k] + got[k]

    @pl.when(bit(axis, levels[-1]) == 1)
    def _():
        for k in range(NVAR):
            f_ref[k] = got[k]
            b_ref[k] = jnp.zeros(shape, F32)

    for t in reversed(range(len(radices) - 1)):
        radix, first = radices[t], sum(sizes[:t])

        def then(q, group, radix=radix):
            f = inflows(group[:-1], [f_ref[k] for k in range(NVAR)])
            b = [b_ref[k] for k in range(NVAR)]
            for k in reversed(range(q + 1, radix)):
                b = outflow(group[k], f[k], b)
            for k in range(NVAR):
                f_ref[k] = f[q][k]
                b_ref[k] = b[k]

        here = grouped(refs[first : first + sizes[t]], radix)
        in_order(axis, levels[t], radix, here, then)


def descend_count(axis, radices):
    return sum(2 * r for r in radices[:-1]) + len(PIECES[axis]) + 2


def middle_kernel(radices, *rest):
    (source, x_lower, x_upper, y_inverse, y_lower, y_upper,
     reduced, y_source, f_ref, b_ref, held) = rest[descend_count("px", radices) :]
    cells, rows = source.shape[1:3]
    descend("px", radices, rest, f_ref, b_ref)

    def forward(i, v):
        product = matvec(lambda a, b: x_lower[a, b, i], list(v))
        v = [source[c, i] - product[c] for c in range(NVAR)]
        for c in range(NVAR):
            held[c, pl.ds(pl.multiple_of(i * rows, rows), rows)] = v[c]
        return tuple(v)

    lax.fori_loop(0, cells, forward, tuple(f_ref[k] for k in range(NVAR)), unroll=True)

    def backward(k, w):
        i = cells - 1 - k
        here = pl.ds(pl.multiple_of(i * rows, rows), rows)
        product = matvec(lambda a, b: x_upper[a, b, i], list(w))
        w = [held[c, here] - product[c] for c in range(NVAR)]
        s = matvec(lambda a, b: y_inverse[a, b, here], w)
        for c in range(NVAR):
            y_source[c, here] = s[c]
        return tuple(w)

    lax.fori_loop(0, cells, backward, tuple(b_ref[k] for k in range(NVAR)), unroll=True)

    def line(j):
        return pl.ds(j, cells, stride=rows)

    zero = jnp.zeros((cells, source.shape[3]), F32)

    def y_forward(j, v):
        product = matvec(lambda a, b: y_lower[NVAR * a + b, j], list(v))
        v = [y_source[c, line(j), :] - product[c] for c in range(NVAR)]
        for c in range(NVAR):
            held[c, pl.ds(pl.multiple_of(j * cells, cells), cells)] = v[c]
        return tuple(v)

    v = lax.fori_loop(0, rows, y_forward, (zero,) * NVAR, unroll=True)

    def y_backward(k, w):
        j = rows - 1 - k
        product = matvec(lambda a, b: y_upper[NVAR * a + b, j], list(w))
        here = pl.ds(pl.multiple_of(j * cells, cells), cells)
        return tuple(held[c, here] - product[c] for c in range(NVAR))

    w = lax.fori_loop(0, rows, y_backward, (zero,) * NVAR, unroll=True)
    for c in range(NVAR):
        reduced[0, c] = v[c]
        reduced[1, c] = w[c]


def end_kernel(radices, cells, rows, *rest):
    first = descend_count("py", radices)
    y_source, y_lower, y_upper, out, f_ref, b_ref, held = rest[first:]
    descend("py", radices, rest, f_ref, b_ref)

    def line(j):
        return pl.ds(j, cells, stride=rows)

    def forward(j, v):
        product = matvec(lambda a, b: y_lower[NVAR * a + b, j], list(v))
        v = [y_source[c, line(j), :] - product[c] for c in range(NVAR)]
        for c in range(NVAR):
            held[c, pl.ds(pl.multiple_of(j * cells, cells), cells)] = v[c]
        return tuple(v)

    lax.fori_loop(0, rows, forward, tuple(f_ref[k] for k in range(NVAR)), unroll=True)

    def backward(k, w):
        j = rows - 1 - k
        here = pl.ds(pl.multiple_of(j * cells, cells), cells)
        product = matvec(lambda a, b: y_upper[NVAR * a + b, j], list(w))
        w = [held[c, here] - product[c] for c in range(NVAR)]
        for c in range(NVAR):
            out[c, line(j), :] = w[c]
        return tuple(w)

    lax.fori_loop(0, rows, backward, tuple(b_ref[k] for k in range(NVAR)), unroll=True)


def radices_of(count):
    out, rest = [], count // 2
    while rest > 1:
        out.append(4 if rest % 4 == 0 else 2)
        rest //= out[-1]
    return out + [2]


def per_device(field, forcing, x_inverse, x_lower, x_upper, y_inverse, y_lower, y_upper):
    cells, rows, lanes = field.shape[1:]
    x_radices, y_radices = radices_of(lax.axis_size("px")), radices_of(lax.axis_size("py"))

    def swap(value, axis, step):
        pairs = [(i, i ^ step) for i in range(lax.axis_size(axis))]
        return lax.ppermute(value, axis, pairs)

    def across(value, axis):
        n = lax.axis_size(axis)
        pairs = [(i, (i + 1) % n) for i in range(1, n, 2)]
        return lax.ppermute(value, axis, pairs + [(j, i) for i, j in pairs])

    flat = lambda m: m.reshape(m.shape[:-3] + (cells * rows, lanes))
    y_inverse = flat(y_inverse)

    every = NVAR * NVAR
    y_pair, y_cross, x_cross, field, y_lower, y_upper = call(
        functools.partial(pack_kernel, cells, rows), "pack",
        [(NVAR, 2, cells, lanes)] * 2 + [(NVAR, 2, rows, lanes)]
        + [(NVAR, cells * rows, lanes)] + [(every, rows, cells, lanes)] * 2,
        [],
        from_hbm=[flat(field)] + [m.reshape(every, cells * rows, lanes) for m in (y_lower, y_upper)],
        copies=1 + 2 * cells,
    )
    field = field.reshape(NVAR, cells, rows, lanes)
    y_cross, x_cross = across(y_cross, "py"), across(x_cross, "px")
    y_pair = swap(y_pair, "py", 1)
    halos = (x_cross, y_pair, y_cross)

    def exchange(axis, radices, own_m, got_m, own_v, rest):
        operands, level = [], 0
        for t, radix in enumerate(radices[:-1]):
            last = t == len(radices) - 2
            settings = (axis, level, radix, last)
            got_v = [swap(own_v, axis, k << level) for k in range(1, radix)]
            lines = own_m.shape[1:]
            sizes = PIECES[axis] if last else (MATRICES,)
            next_m = call(functools.partial(join_matrices_kernel, *settings), "join_matrices",
                          [(size, *lines) for size in sizes], [own_m, *got_m])
            next_m = list(next_m) if len(sizes) > 1 else [next_m]
            next_level = level + radix.bit_length() - 1
            next_got = [swap(m, axis, k << next_level)
                        for k in range(1, radices[t + 1]) for m in next_m]
            count = len(operands)
            operands += [own_m, *got_m, own_v, *got_v]
            held = hold(operands + rest)
            operands, rest = held[: len(operands)], held[len(operands) :]
            own_v = call(functools.partial(join_vectors_kernel, *settings), "join_vectors",
                         [own_v.shape[last:]], operands[count:])
            if not last:
                next_got = hold(next_got, own_v)
            own_m, got_m, level = next_m[0], next_got, next_level
        operands += [*got_m, own_v, swap(own_v, axis, 1 << level)]
        held = hold(operands + rest)
        return held[: len(operands)], held[len(operands) :]

    y_m = call(compose_y_kernel, "compose_y", [(MATRICES, cells, lanes)],
               [y_lower, y_upper], [(rows, every, cells, lanes)])
    x_m, y_inverse = call(
        functools.partial(compose_x_kernel, cells), "compose_x",
        [(MATRICES + 2 * NVAR, rows, lanes), y_inverse.shape],
        [x_lower, x_upper, y_m, flat(field)], [(cells, every, ROWS, lanes)],
        from_hbm=[y_inverse], copies=1,
    )
    y_m, y_lower, y_upper, y_inverse, x_m = hold([y_m, y_lower, y_upper, y_inverse, x_m], *halos)
    y_got = [swap(y_m, "py", k) for k in range(1, y_radices[0])]
    x_got = [swap(x_m, "px", k) for k in range(1, x_radices[0])]
    reduced, source = call(
        local_x_kernel, "local_x",
        [(VX, NVAR, rows, lanes), (NVAR, cells, rows, lanes)],
        [field, forcing, x_got[0], *halos, x_inverse, x_lower, x_upper],
        [(NVAR, cells + 4, rows + 2 * ROWS, lanes), (NVAR, cells, rows, lanes)],
    )
    operands, (source, y_inverse, y_lower, y_upper) = exchange(
        "px", x_radices, x_m, x_got, reduced, [source, y_inverse, y_lower, y_upper]
    )
    reduced, source = call(
        functools.partial(middle_kernel, x_radices), "middle",
        [(2, NVAR, cells, lanes), (NVAR, cells * rows, lanes)],
        [*operands, source, x_lower, x_upper, y_inverse, y_lower, y_upper],
        [(NVAR, rows, lanes), (NVAR, rows, lanes), (NVAR, cells * rows, lanes)],
    )
    y_m, *y_got = hold([y_m, *y_got], reduced)
    operands, rest = exchange(
        "py", y_radices, y_m, y_got, reduced, [source, y_lower, y_upper]
    )
    out = call(
        functools.partial(end_kernel, y_radices, cells, rows), "end",
        [(NVAR, cells * rows, lanes)],
        operands + rest,
        [(NVAR, cells, lanes), (NVAR, cells, lanes), (NVAR, cells * rows, lanes)],
        result_in_hbm=True,
    )
    return out.reshape(NVAR, cells, rows, lanes)


def solution(mesh):
    cell = P(None, "px", "py", None)
    blocks = P(None, None, "px", "py", None)
    return jax.shard_map(
        per_device,
        mesh=mesh,
        in_specs=(cell, cell) + (blocks,) * 6,
        out_specs=cell,
        check_vma=False,
    )
```

time: 45.7 us -> 40.5 us (0.89)
  waiting for transfers between devices: 19.5 us -> 9.68 us
  starting transfers between devices: 15.2 us -> 21.9 us
  Pallas kernels: 9.8 us -> 8.28 us
  local copies, waits for them, and re-layouts: 0.98 us -> 0.39 us
    ppermute x12 -> x14, waiting for transfers between devices: 19.5 us -> 9.68 us  [swap(): return lax.ppermute(value, axis, pairs)]
    ppermute x12 -> x14, starting transfers between devices: 9 us -> 15.9 us  [swap(): return lax.ppermute(value, axis, pairs)]
    pallas_call x12 -> x10, Pallas kernels: 9.79 us -> 8.26 us  [call(): pl.pallas_call(kernel, name=name, out_shape=shapes[0] if single else shap...]
    unnamed x4 -> x8, local copies, waits for them, and re-layouts: 0.98 us -> 0.39 us
  transfers between devices with their start and end apart: 14 -> 16, of which waited for: 7 -> 6; matrix products, arithmetic and copies ran while one was open for 0% -> 0% of each run, Pallas kernels for 18% -> 12%
where the time goes in v3:
time: 40.5 us; the launch traced here: 40.4 us
  starting transfers between devices  21.9 us (54%)
  waiting for transfers between devices  9.68 us (24%)
  Pallas kernels  8.28 us (20%)
    ppermute x14, starting transfers between devices, swap(): return lax.ppermute(value, axis, pairs)  15.9 us
    ppermute x14, waiting for transfers between devices, swap(): return lax.ppermute(value, axis, pairs)  9.68 us
    pallas_call x10, Pallas kernels, call(): pl.pallas_call(kernel, name=name, out_shape=shapes[0] if single else shap...  8.26 us
    ppermute x2, starting transfers between devices, across(): return lax.ppermute(value, axis, pairs + [(j, i) for i, j in pairs])  5.99 us
  transfers between devices with their start and end apart: 16, of which 6 were waited for; matrix products, arithmetic and copies ran while one was open for 0% of the time, Pallas kernels for 12%

profile of v3, /device:TPU:0, one launch (start us, length us, event | category | flops | bytes accessed | tf_op | source)
XLA Modules:
  0.0 40.4 jit_solution(4220529565329172443)
XLA Ops:
  0.0 2.2 %pack.1 = (f32[5,2,8,128]{3,2,1,0:T(8,128)S(1)}, f32[5,2,8,128]{3,2,1,0:T(8,128)S(1)}, f32[5,2,16,128]{3,2,1,0:T(8,128)S(1)}, f32[5,128,128]{2,1,0:T(8,128)S(1)}...) custom-call(f32[5,128,128]{2,1,0:T(8,128)} %bitcast.10, f32[25,128,128]{2,1,0:T(8,128)} %bitcast.7, ...), custom_call_target="tpu_custom_call" | custom-call | tf_op jit(solution)/shard_map/pack/pallas_call | solution.py:30
  2.2 2.4 %collective-permute-start = (f32[5,2,16,128]{3,2,1,0:T(8,128)S(1)}, f32[5,2,16,128]{3,2,1,0:T(8,128)S(1)}, u32[]{:S(2)}, u32[]{:S(2)}) collective-permute-start(f32[5,2,16,128]{3,2,1,0:T(8,128)S(1)} %get-tuple-element.78), channel_id=1, source_target_pairs={{8,16},{24,0},{16,8},{0,24},{9,17},{25,1},{17,9},{1,25},{10,18},{2... | collective-permute-start | bytes 245768 | tf_op jit(solution)/shard_map/ppermute | solution.py:595
  4.6 1.5 %collective-permute-start.1 = (f32[5,2,8,128]{3,2,1,0:T(8,128)S(1)}, f32[5,2,8,128]{3,2,1,0:T(8,128)S(1)}, u32[]{:S(2)}, u32[]{:S(2)}) collective-permute-start(f32[5,2,8,128]{3,2,1,0:T(8,128)S(1)} %get-tuple-element.79), channel_id=1, source_target_pairs={{0,1},{1,0},{2,3},{3,2},{4,5},{5,4},{6,7},{7,6},{8,9},{9,8},{10,11... | collective-permute-start | bytes 122888 | tf_op jit(solution)/shard_map/ppermute | solution.py:590
  6.1 3.5 %collective-permute-start.2 = (f32[5,2,8,128]{3,2,1,0:T(8,128)S(1)}, f32[5,2,8,128]{3,2,1,0:T(8,128)S(1)}, u32[]{:S(2)}, u32[]{:S(2)}) collective-permute-start(f32[5,2,8,128]{3,2,1,0:T(8,128)S(1)} %get-tuple-element.80), channel_id=1, source_target_pairs={{1,2},{3,4},{5,6},{7,0},{2,1},{4,3},{6,5},{0,7},{9,10},{11,12},{13... | collective-permute-start | bytes 122888 | tf_op jit(solution)/shard_map/ppermute | solution.py:595
  9.7 1.5 %compose_y.1._.refs_0_ = f32[75,8,128]{2,1,0:T(8,128)S(1)} custom-call(f32[25,16,8,128]{3,2,1,0:T(8,128)S(1)} %get-tuple-element.73.lower.refs_1_, f32[25,16,8,128]{3,2,1,0:T(8,128)S(1)} %get-tuple-element.74.upper.refs_2_), custom_call_target="tpu_custom_call" | custom-call | tf_op jit(solution)/shard_map/compose_y/pallas_call | solution.py:30
  11.2 0.4 copy-done.1
  11.6 1.5 %compose_x.1 = (f32[85,16,128]{2,1,0:T(8,128)S(1)}, f32[5,5,128,128]{3,2,1,0:T(8,128)S(1)}) custom-call(f32[5,5,8,16,128]{4,3,2,1,0:T(8,128)S(1)} %copy-done, f32[5,5,8,16,128]{4,3,2,1,0:T(8,128)S(1)} %copy-done.1, f32[75,8,128]{2,1,0:T(8,128)S(1)} %compose_y.1._.refs_0_, f32[5,128,128]{2,1,0:T(8,128)S(1)} %get-tuple-element.75.field, f32[5,5,128,128]{3,2,1,0:T(8,128)} %bitcast.9), custom_call_target="tpu_custom_call" | custom-call | tf_op jit(solution)/shard_map/compose_x/pallas_call | solution.py:30
  13.4 1.1 %collective-permute-start.4 = (f32[75,8,128]{2,1,0:T(8,128)S(1)}, f32[75,8,128]{2,1,0:T(8,128)S(1)}, u32[]{:S(2)}, u32[]{:S(2)}) collective-permute-start(f32[75,8,128]{2,1,0:T(8,128)S(1)} %get-tuple-element.81.refs_0_), channel_id=1, source_target_pairs={{0,2},{1,3},{2,0},{3,1},{4,6},{5,7},{6,4},{7,5},{8,10},{9,11},{10,... | collective-permute-start | bytes 921608 | tf_op jit(solution)/shard_map/ppermute | solution.py:590
  14.5 2.4 %collective-permute-start.5 = (f32[75,8,128]{2,1,0:T(8,128)S(1)}, f32[75,8,128]{2,1,0:T(8,128)S(1)}, u32[]{:S(2)}, u32[]{:S(2)}) collective-permute-start(f32[75,8,128]{2,1,0:T(8,128)S(1)} %get-tuple-element.81.refs_0_), channel_id=1, source_target_pairs={{0,3},{1,2},{2,1},{3,0},{4,7},{5,6},{6,5},{7,4},{8,11},{9,10},{10,... | collective-permute-start | bytes 921608 | tf_op jit(solution)/shard_map/ppermute | solution.py:590
  16.9 0.8 %local_x.1 = (f32[5,5,16,128]{3,2,1,0:T(8,128)S(1)}, f32[5,8,16,128]{3,2,1,0:T(8,128)S(1)}) custom-call(f32[5,8,16,128]{3,2,1,0:T(8,128)S(1)} %bitcast.6, f32[5,8,16,128]{3,2,1,0:T(8,128)S(1)} %copy-done.3, f32[85,16,128]{2,1,0:T(8,128)S(1)} %collective-permute-done.6.x_got.refs_1_, f32[5,2,16,128]{3,2,1,0:T(8,128)S(1)} %collective-permute-done.refs_5_.x_cross, ...), custom_call_target="tpu_custom_call" | custom-call | tf_op jit(solution)/shard_map/local_x/pallas_call | solution.py:30
  17.8 0.8 %collective-permute-start.8 = (f32[25,16,128]{2,1,0:T(8,128)S(1)}, f32[25,16,128]{2,1,0:T(8,128)S(1)}, u32[]{:S(2)}, u32[]{:S(2)}) collective-permute-start(f32[25,16,128]{2,1,0:T(8,128)S(1)} %join_matrices.2), channel_id=1, source_target_pairs={{0,16},{8,24},{16,0},{24,8},{1,17},{9,25},{17,1},{25,9},{2,18},{10... | collective-permute-start | bytes 614408 | tf_op jit(solution)/shard_map/ppermute | solution.py:590
  18.6 0.7 %collective-permute-done.7.refs_3_ = f32[5,5,16,128]{3,2,1,0:T(8,128)S(1)} collective-permute-done((f32[5,5,16,128]{3,2,1,0:T(8,128)S(1)}, f32[5,5,16,128]{3,2,1,0:T(8,128)S(1)}, u32[]{:S(2)}, u32[]{:S(2)}) %collective-permute-start.7) | collective-permute-done | bytes 204832 | tf_op jit(solution)/shard_map/ppermute | solution.py:590
  19.3 0.8 %collective-permute-start.9 = (f32[5,16,128]{2,1,0:T(8,128)S(1)}, f32[5,16,128]{2,1,0:T(8,128)S(1)}, u32[]{:S(2)}, u32[]{:S(2)}) collective-permute-start(f32[5,16,128]{2,1,0:T(8,128)S(1)} %join_vectors.2.refs_5_), channel_id=1, source_target_pairs={{0,16},{8,24},{16,0},{24,8},{1,17},{9,25},{17,1},{25,9},{2,18},{10... | collective-permute-start | bytes 122888 | tf_op jit(solution)/shard_map/ppermute | solution.py:590
  20.1 5.7 %collective-permute-done.8.refs_4_ = f32[25,16,128]{2,1,0:T(8,128)S(1)} collective-permute-done((f32[25,16,128]{2,1,0:T(8,128)S(1)}, f32[25,16,128]{2,1,0:T(8,128)S(1)}, u32[]{:S(2)}, u32[]{:S(2)}) %collective-permute-start.8) | collective-permute-done | bytes 204832 | tf_op jit(solution)/shard_map/ppermute | solution.py:590
  25.8 0.4 %collective-permute-done.9.refs_6_ = f32[5,16,128]{2,1,0:T(8,128)S(1)} collective-permute-done((f32[5,16,128]{2,1,0:T(8,128)S(1)}, f32[5,16,128]{2,1,0:T(8,128)S(1)}, u32[]{:S(2)}, u32[]{:S(2)}) %collective-permute-start.9) | collective-permute-done | bytes 40992 | tf_op jit(solution)/shard_map/ppermute | solution.py:590
  26.2 0.8 %middle.1 = (f32[2,5,8,128]{3,2,1,0:T(8,128)S(1)}, f32[5,128,128]{2,1,0:T(8,128)S(1)}) custom-call(f32[85,16,128]{2,1,0:T(8,128)S(1)} %get-tuple-element.96.rest_0_, f32[85,16,128]{2,1,0:T(8,128)S(1)} %get-tuple-element.97.rest_1_, f32[5,5,16,128]{3,2,1,0:T(8,128)S(1)} %get-tuple-element.98.rest_2_, f32[5,5,16,128]{3,2,1,0:T(8,128)S(1)} %get-tuple-element.99.rest_3_, ...), custom_call_target="tpu_custom_call" | custom-call | tf_op jit(solution)/shard_map/middle/pallas_call | solution.py:30
  27.1 1.0 %collective-permute-start.11 = (f32[2,5,8,128]{3,2,1,0:T(8,128)S(1)}, f32[2,5,8,128]{3,2,1,0:T(8,128)S(1)}, u32[]{:S(2)}, u32[]{:S(2)}) collective-permute-start(f32[2,5,8,128]{3,2,1,0:T(8,128)S(1)} %get-tuple-element.107.refs_4_), channel_id=1, source_target_pairs={{0,2},{1,3},{2,0},{3,1},{4,6},{5,7},{6,4},{7,5},{8,10},{9,11},{10,... | collective-permute-start | bytes 122888 | tf_op jit(solution)/shard_map/ppermute | solution.py:590
  28.1 2.4 %collective-permute-start.12 = (f32[2,5,8,128]{3,2,1,0:T(8,128)S(1)}, f32[2,5,8,128]{3,2,1,0:T(8,128)S(1)}, u32[]{:S(2)}, u32[]{:S(2)}) collective-permute-start(f32[2,5,8,128]{3,2,1,0:T(8,128)S(1)} %get-tuple-element.107.refs_4_), channel_id=1, source_target_pairs={{0,3},{1,2},{2,1},{3,0},{4,7},{5,6},{6,5},{7,4},{8,11},{9,10},{10,... | collective-permute-start | bytes 122888 | tf_op jit(solution)/shard_map/ppermute | solution.py:590
  30.6 0.3 collective-permute-done.5.refs_3_
  30.8 1.2 %collective-permute-start.13 = (f32[13,8,128]{2,1,0:T(8,128)S(1)}, f32[13,8,128]{2,1,0:T(8,128)S(1)}, u32[]{:S(2)}, u32[]{:S(2)}) collective-permute-start(f32[13,8,128]{2,1,0:T(8,128)S(1)} %get-tuple-element.121), channel_id=1, source_target_pairs={{0,4},{1,5},{2,6},{3,7},{4,0},{5,1},{6,2},{7,3},{8,12},{9,13},{10,... | collective-permute-start | bytes 159752 | tf_op jit(solution)/shard_map/ppermute | solution.py:590
  32.1 1.7 %collective-permute-start.14 = (f32[12,8,128]{2,1,0:T(8,128)S(1)}, f32[12,8,128]{2,1,0:T(8,128)S(1)}, u32[]{:S(2)}, u32[]{:S(2)}) collective-permute-start(f32[12,8,128]{2,1,0:T(8,128)S(1)} %get-tuple-element.122), channel_id=1, source_target_pairs={{0,4},{1,5},{2,6},{3,7},{4,0},{5,1},{6,2},{7,3},{8,12},{9,13},{10,... | collective-permute-start | bytes 147464 | tf_op jit(solution)/shard_map/ppermute | solution.py:590
  33.8 2.6 %collective-permute-start.15 = (f32[5,8,128]{2,1,0:T(8,128)S(1)}, f32[5,8,128]{2,1,0:T(8,128)S(1)}, u32[]{:S(2)}, u32[]{:S(2)}) collective-permute-start(f32[5,8,128]{2,1,0:T(8,128)S(1)} %join_vectors.3.refs_10_), channel_id=1, source_target_pairs={{0,4},{1,5},{2,6},{3,7},{4,0},{5,1},{6,2},{7,3},{8,12},{9,13},{10,... | collective-permute-start | bytes 61448 | tf_op jit(solution)/shard_map/ppermute | solution.py:590
  36.4 2.4 %collective-permute-done.14.refs_9_ = f32[12,8,128]{2,1,0:T(8,128)S(1)} collective-permute-done((f32[12,8,128]{2,1,0:T(8,128)S(1)}, f32[12,8,128]{2,1,0:T(8,128)S(1)}, u32[]{:S(2)}, u32[]{:S(2)}) %collective-permute-start.14) | collective-permute-done | bytes 49184 | tf_op jit(solution)/shard_map/ppermute | solution.py:590
  39.0 1.3 %end.1 = f32[5,128,128]{2,1,0:T(8,128)} custom-call(f32[75,8,128]{2,1,0:T(8,128)S(1)} %get-tuple-element.126.rest_0_, f32[75,8,128]{2,1,0:T(8,128)S(1)} %get-tuple-element.127.rest_1_, f32[75,8,128]{2,1,0:T(8,128)S(1)} %get-tuple-element.128.rest_2_, f32[75,8,128]{2,1,0:T(8,128)S(1)} %get-tuple-element.129.rest_3_, ...), custom_call_target="tpu_custom_call" | custom-call | tf_op jit(solution)/shard_map/end/pallas_call | solution.py:30
  (32 shorter events, 0.7 us)
Async XLA Ops:
  2.2 10.9 %collective-permute-start = (f32[5,2,16,128]{3,2,1,0:T(8,128)S(1)}, f32[5,2,16,128]{3,2,1,0:T(8,128)S(1)}, u32[]{:S(2)}, u32[]{:S(2)}) collective-permute-start(f32[5,2,16,128]{3,2,1,0:T(8,128)S(1)} %get-tuple-element.78), channel_id=1, source_target_pairs={{8,16},{24,0},{16,8},{0,24},{9,17},{25,1},{17,9},{1,25},{10,18},{2... | collective-permute-start | bytes 245768 | tf_op jit(solution)/shard_map/ppermute | solution.py:595
  4.6 8.5 %collective-permute-start.1 = (f32[5,2,8,128]{3,2,1,0:T(8,128)S(1)}, f32[5,2,8,128]{3,2,1,0:T(8,128)S(1)}, u32[]{:S(2)}, u32[]{:S(2)}) collective-permute-start(f32[5,2,8,128]{3,2,1,0:T(8,128)S(1)} %get-tuple-element.79), channel_id=1, source_target_pairs={{0,1},{1,0},{2,3},{3,2},{4,5},{5,4},{6,7},{7,6},{8,9},{9,8},{10,11... | collective-permute-start | bytes 122888 | tf_op jit(solution)/shard_map/ppermute | solution.py:590
  6.1 7.0 %collective-permute-start.2 = (f32[5,2,8,128]{3,2,1,0:T(8,128)S(1)}, f32[5,2,8,128]{3,2,1,0:T(8,128)S(1)}, u32[]{:S(2)}, u32[]{:S(2)}) collective-permute-start(f32[5,2,8,128]{3,2,1,0:T(8,128)S(1)} %get-tuple-element.80), channel_id=1, source_target_pairs={{1,2},{3,4},{5,6},{7,0},{2,1},{4,3},{6,5},{0,7},{9,10},{11,12},{13... | collective-permute-start | bytes 122888 | tf_op jit(solution)/shard_map/ppermute | solution.py:595
  9.7 1.5 %copy-start = (f32[5,5,8,16,128]{4,3,2,1,0:T(8,128)S(1)}, f32[5,5,8,16,128]{4,3,2,1,0:T(8,128)}, u32[]{:S(2)}) copy-start(f32[5,5,8,16,128]{4,3,2,1,0:T(8,128)} %rest_8_.1) | copy-start | bytes 4915204
  9.7 1.9 %copy-start.1 = (f32[5,5,8,16,128]{4,3,2,1,0:T(8,128)S(1)}, f32[5,5,8,16,128]{4,3,2,1,0:T(8,128)}, u32[]{:S(2)}) copy-start(f32[5,5,8,16,128]{4,3,2,1,0:T(8,128)} %rest_9_.1) | copy-start | bytes 4915204
  13.1 3.8 %copy-start.2 = (f32[5,5,8,16,128]{4,3,2,1,0:T(8,128)S(1)}, f32[5,5,8,16,128]{4,3,2,1,0:T(8,128)}, u32[]{:S(2)}) copy-start(f32[5,5,8,16,128]{4,3,2,1,0:T(8,128)} %inverse.1) | copy-start | bytes 4915204
  13.1 3.8 %copy-start.3 = (f32[5,8,16,128]{3,2,1,0:T(8,128)S(1)}, f32[5,8,16,128]{3,2,1,0:T(8,128)}, u32[]{:S(2)}) copy-start(f32[5,8,16,128]{3,2,1,0:T(8,128)} %forcing.1) | copy-start | bytes 983044
  13.2 3.7 %collective-permute-start.6 = (f32[85,16,128]{2,1,0:T(8,128)S(1)}, f32[85,16,128]{2,1,0:T(8,128)S(1)}, u32[]{:S(2)}, u32[]{:S(2)}) collective-permute-start(f32[85,16,128]{2,1,0:T(8,128)S(1)} %get-tuple-element.82.refs_0_), channel_id=1, source_target_pairs={{0,8},{8,0},{16,24},{24,16},{1,9},{9,1},{17,25},{25,17},{2,10},{10... | collective-permute-start | bytes 2088968 | tf_op jit(solution)/shard_map/ppermute | solution.py:590
  13.4 14.8 %collective-permute-start.3 = (f32[75,8,128]{2,1,0:T(8,128)S(1)}, f32[75,8,128]{2,1,0:T(8,128)S(1)}, u32[]{:S(2)}, u32[]{:S(2)}) collective-permute-start(f32[75,8,128]{2,1,0:T(8,128)S(1)} %get-tuple-element.81.refs_0_), channel_id=1, source_target_pairs={{0,1},{1,0},{2,3},{3,2},{4,5},{5,4},{6,7},{7,6},{8,9},{9,8},{10,11... | collective-permute-start | bytes 921608 | tf_op jit(solution)/shard_map/ppermute | solution.py:590
  13.4 17.2 %collective-permute-start.4 = (f32[75,8,128]{2,1,0:T(8,128)S(1)}, f32[75,8,128]{2,1,0:T(8,128)S(1)}, u32[]{:S(2)}, u32[]{:S(2)}) collective-permute-start(f32[75,8,128]{2,1,0:T(8,128)S(1)} %get-tuple-element.81.refs_0_), channel_id=1, source_target_pairs={{0,2},{1,3},{2,0},{3,1},{4,6},{5,7},{6,4},{7,5},{8,10},{9,11},{10,... | collective-permute-start | bytes 921608 | tf_op jit(solution)/shard_map/ppermute | solution.py:590
  14.5 16.4 %collective-permute-start.5 = (f32[75,8,128]{2,1,0:T(8,128)S(1)}, f32[75,8,128]{2,1,0:T(8,128)S(1)}, u32[]{:S(2)}, u32[]{:S(2)}) collective-permute-start(f32[75,8,128]{2,1,0:T(8,128)S(1)} %get-tuple-element.81.refs_0_), channel_id=1, source_target_pairs={{0,3},{1,2},{2,1},{3,0},{4,7},{5,6},{6,5},{7,4},{8,11},{9,10},{10,... | collective-permute-start | bytes 921608 | tf_op jit(solution)/shard_map/ppermute | solution.py:590
  17.7 1.5 %collective-permute-start.7 = (f32[5,5,16,128]{3,2,1,0:T(8,128)S(1)}, f32[5,5,16,128]{3,2,1,0:T(8,128)S(1)}, u32[]{:S(2)}, u32[]{:S(2)}) collective-permute-start(f32[5,5,16,128]{3,2,1,0:T(8,128)S(1)} %get-tuple-element.83.refs_2_), channel_id=1, source_target_pairs={{0,8},{8,0},{16,24},{24,16},{1,9},{9,1},{17,25},{25,17},{2,10},{10... | collective-permute-start | bytes 614408 | tf_op jit(solution)/shard_map/ppermute | solution.py:590
  17.8 7.9 %collective-permute-start.8 = (f32[25,16,128]{2,1,0:T(8,128)S(1)}, f32[25,16,128]{2,1,0:T(8,128)S(1)}, u32[]{:S(2)}, u32[]{:S(2)}) collective-permute-start(f32[25,16,128]{2,1,0:T(8,128)S(1)} %join_matrices.2), channel_id=1, source_target_pairs={{0,16},{8,24},{16,0},{24,8},{1,17},{9,25},{17,1},{25,9},{2,18},{10... | collective-permute-start | bytes 614408 | tf_op jit(solution)/shard_map/ppermute | solution.py:590
  19.3 6.9 %collective-permute-start.9 = (f32[5,16,128]{2,1,0:T(8,128)S(1)}, f32[5,16,128]{2,1,0:T(8,128)S(1)}, u32[]{:S(2)}, u32[]{:S(2)}) collective-permute-start(f32[5,16,128]{2,1,0:T(8,128)S(1)} %join_vectors.2.refs_5_), channel_id=1, source_target_pairs={{0,16},{8,24},{16,0},{24,8},{1,17},{9,25},{17,1},{25,9},{2,18},{10... | collective-permute-start | bytes 122888 | tf_op jit(solution)/shard_map/ppermute | solution.py:590
  27.0 6.7 %collective-permute-start.10 = (f32[2,5,8,128]{3,2,1,0:T(8,128)S(1)}, f32[2,5,8,128]{3,2,1,0:T(8,128)S(1)}, u32[]{:S(2)}, u32[]{:S(2)}) collective-permute-start(f32[2,5,8,128]{3,2,1,0:T(8,128)S(1)} %get-tuple-element.107.refs_4_), channel_id=1, source_target_pairs={{0,1},{1,0},{2,3},{3,2},{4,5},{5,4},{6,7},{7,6},{8,9},{9,8},{10,11... | collective-permute-start | bytes 122888 | tf_op jit(solution)/shard_map/ppermute | solution.py:590
  27.1 6.7 %collective-permute-start.11 = (f32[2,5,8,128]{3,2,1,0:T(8,128)S(1)}, f32[2,5,8,128]{3,2,1,0:T(8,128)S(1)}, u32[]{:S(2)}, u32[]{:S(2)}) collective-permute-start(f32[2,5,8,128]{3,2,1,0:T(8,128)S(1)} %get-tuple-element.107.refs_4_), channel_id=1, source_target_pairs={{0,2},{1,3},{2,0},{3,1},{4,6},{5,7},{6,4},{7,5},{8,10},{9,11},{10,... | collective-permute-start | bytes 122888 | tf_op jit(solution)/shard_map/ppermute | solution.py:590
  28.1 5.6 %collective-permute-start.12 = (f32[2,5,8,128]{3,2,1,0:T(8,128)S(1)}, f32[2,5,8,128]{3,2,1,0:T(8,128)S(1)}, u32[]{:S(2)}, u32[]{:S(2)}) collective-permute-start(f32[2,5,8,128]{3,2,1,0:T(8,128)S(1)} %get-tuple-element.107.refs_4_), channel_id=1, source_target_pairs={{0,3},{1,2},{2,1},{3,0},{4,7},{5,6},{6,5},{7,4},{8,11},{9,10},{10,... | collective-permute-start | bytes 122888 | tf_op jit(solution)/shard_map/ppermute | solution.py:590
  30.8 8.0 %collective-permute-start.13 = (f32[13,8,128]{2,1,0:T(8,128)S(1)}, f32[13,8,128]{2,1,0:T(8,128)S(1)}, u32[]{:S(2)}, u32[]{:S(2)}) collective-permute-start(f32[13,8,128]{2,1,0:T(8,128)S(1)} %get-tuple-element.121), channel_id=1, source_target_pairs={{0,4},{1,5},{2,6},{3,7},{4,0},{5,1},{6,2},{7,3},{8,12},{9,13},{10,... | collective-permute-start | bytes 159752 | tf_op jit(solution)/shard_map/ppermute | solution.py:590
  32.1 6.7 %collective-permute-start.14 = (f32[12,8,128]{2,1,0:T(8,128)S(1)}, f32[12,8,128]{2,1,0:T(8,128)S(1)}, u32[]{:S(2)}, u32[]{:S(2)}) collective-permute-start(f32[12,8,128]{2,1,0:T(8,128)S(1)} %get-tuple-element.122), channel_id=1, source_target_pairs={{0,4},{1,5},{2,6},{3,7},{4,0},{5,1},{6,2},{7,3},{8,12},{9,13},{10,... | collective-permute-start | bytes 147464 | tf_op jit(solution)/shard_map/ppermute | solution.py:590
  33.8 5.2 %collective-permute-start.15 = (f32[5,8,128]{2,1,0:T(8,128)S(1)}, f32[5,8,128]{2,1,0:T(8,128)S(1)}, u32[]{:S(2)}, u32[]{:S(2)}) collective-permute-start(f32[5,8,128]{2,1,0:T(8,128)S(1)} %join_vectors.3.refs_10_), channel_id=1, source_target_pairs={{0,4},{1,5},{2,6},{3,7},{4,0},{5,1},{6,2},{7,3},{8,12},{9,13},{10,... | collective-permute-start | bytes 61448 | tf_op jit(solution)/shard_map/ppermute | solution.py:590

commit v4 on v3

--- a/solution.py
+++ b/solution.py
@@ -13,7 +13,7 @@
 ROWS = 8
 UNROLL = 3
 MATRICES = 3 * NVAR * NVAR
-VX = 5
+VX = 2
 PIECES = {"px": (25,), "py": (13, 12)}
 VMEM_BYTES = 12 * 1024 * 1024
 
@@ -115,18 +115,8 @@
     emit(2, [-q for q in w])
 
 
-def compose_x_kernel(cells, lower, upper, _, field, y_inverse_hbm, out, y_inverse, held, semaphores):
-    load = pltpu.make_async_copy(y_inverse_hbm, y_inverse, semaphores.at[0])
-    load.start()
-    rows = lower.shape[3]
-
-    for side, first in enumerate((cells - 2, 0)):
-
-        @pl.when(bit("px", 0) == side)
-        def _(first=first):
-            for c in range(NVAR):
-                for k in range(2):
-                    out[MATRICES + 2 * c + k] = field[c, pl.ds((first + k) * rows, rows), :]
+def compose_x(lower, upper, out, held):
+    cells, rows = lower.shape[2:4]
 
     def group(g, _):
         here = pl.ds(pl.multiple_of(g * ROWS, ROWS), ROWS)
@@ -151,10 +141,11 @@
         return 0
 
     lax.fori_loop(0, rows // ROWS, group, 0)
-    load.wait()
-
-
-def compose_y_kernel(lower, upper, out, held):
+
+
+def compose_y_kernel(lower, upper, y_inverse_hbm, out, y_inverse, held, semaphores):
+    load = pltpu.make_async_copy(y_inverse_hbm, y_inverse, semaphores.at[0])
+    load.start()
     cells_y = lower.shape[1]
 
     def emit(which, matrix):
@@ -174,10 +165,11 @@
         lambda i: [held[i, k] for k in range(NVAR * NVAR)],
         emit,
     )
+    load.wait()
 
 
 def local_x_kernel(
-    field, forcing, x_got, x_cross, y_pair, y_cross, inverse, lower, upper,
+    field, forcing, x_pair, x_cross, y_pair, y_cross, inverse, lower, upper, _,
     reduced, source_out, padded, held,
 ):
     cells, rows, lanes = field.shape[1:]
@@ -187,9 +179,6 @@
         for i in range(cells):
             padded[c, i + 2, middle] = field[c, i]
 
-    def x_pair(c, k):
-        return x_got[MATRICES + 2 * c + k]
-
     def y_before(value):
         for c in range(NVAR):
             for k in range(2):
@@ -213,7 +202,7 @@
                 padded[c, cells + 2 + k, middle] = value(c, k)
 
     for axis, before, behind, pair, cross, empty in (
-        ("px", x_before, x_after, x_pair, x_cross, jnp.zeros((rows, lanes), F32)),
+        ("px", x_before, x_after, lambda *k: x_pair[k], x_cross, jnp.zeros((rows, lanes), F32)),
         ("py", y_before, y_after, lambda *k: y_pair[k], y_cross, jnp.zeros((lanes,), F32)),
     ):
         at, count = lax.axis_index(axis), lax.axis_size(axis)
@@ -302,21 +291,20 @@
             then(q, [bundles[m ^ q] for m in range(radix)])
 
 
-def pack_kernel(cells, rows, field_hbm, lower_hbm, upper_hbm,
-                y_pair, y_cross, x_cross, field, lower, upper, semaphores):
-    first = pltpu.make_async_copy(field_hbm, field, semaphores.at[0])
-    first.start()
-    copies = []
-    for source, target in ((lower_hbm, lower), (upper_hbm, upper)):
+def begin_kernel(cells, rows, field_hbm, x_lower_hbm, x_upper_hbm, y_lower_hbm, y_upper_hbm,
+                 y_pair, y_cross, x_pair, x_cross, x_out, field, x_lower, x_upper, y_lower, y_upper,
+                 held, semaphores):
+    loads = [(field_hbm, field), (x_lower_hbm, x_lower), (x_upper_hbm, x_upper)]
+    for source, target in ((y_lower_hbm, y_lower), (y_upper_hbm, y_upper)):
         for x in range(cells):
-            copy = pltpu.make_async_copy(
-                source.at[:, pl.ds(x * rows, rows), :],
-                target.at[:, :, x, :],
-                semaphores.at[1 + len(copies)],
-            )
-            copy.start()
-            copies.append(copy)
-    first.wait()
+            loads.append((source.at[:, pl.ds(x * rows, rows), :], target.at[:, :, x, :]))
+    copies = [
+        pltpu.make_async_copy(source, target, semaphores.at[k])
+        for k, (source, target) in enumerate(loads)
+    ]
+    for copy in copies:
+        copy.start()
+    copies[0].wait()
 
     def y_layers(out, j):
         for c in range(NVAR):
@@ -338,13 +326,20 @@
         y_layers(y_pair, 0)
         y_layers(y_cross, rows - 2)
 
-    for side, first_layer in enumerate((0, cells - 2)):
-
-        @pl.when(bit("px", 0) == side)
-        def _(first_layer=first_layer):
-            x_layers(x_cross, first_layer)
-
-    for copy in copies:
+    @pl.when(bit("px", 0) == 0)
+    def _():
+        x_layers(x_pair, cells - 2)
+        x_layers(x_cross, 0)
+
+    @pl.when(bit("px", 0) == 1)
+    def _():
+        x_layers(x_pair, 0)
+        x_layers(x_cross, cells - 2)
+
+    copies[1].wait()
+    copies[2].wait()
+    compose_x(x_lower, x_upper, x_out, held)
+    for copy in copies[3:]:
         copy.wait()
 
 
@@ -592,24 +587,33 @@
     def across(value, axis):
         n = lax.axis_size(axis)
         pairs = [(i, (i + 1) % n) for i in range(1, n, 2)]
-        return lax.ppermute(value, axis, pairs + [(j, i) for i, j in pairs])
+        if axis == "px":
+            return lax.ppermute(value, axis, pairs + [(j, i) for i, j in pairs])
+        swaps = []
+        for x in range(lax.axis_size("px")):
+            inner = [(x * n + i, x * n + j) for i, j in pairs[:-1]]
+            swaps += inner + [(j, i) for i, j in inner]
+            swaps += [(x * n + i, (x ^ 1) * n + i) for i in (0, n - 1)]
+        return lax.ppermute(value, ("px", "py"), swaps)
 
     flat = lambda m: m.reshape(m.shape[:-3] + (cells * rows, lanes))
     y_inverse = flat(y_inverse)
 
     every = NVAR * NVAR
-    y_pair, y_cross, x_cross, field, y_lower, y_upper = call(
-        functools.partial(pack_kernel, cells, rows), "pack",
-        [(NVAR, 2, cells, lanes)] * 2 + [(NVAR, 2, rows, lanes)]
-        + [(NVAR, cells * rows, lanes)] + [(every, rows, cells, lanes)] * 2,
-        [],
-        from_hbm=[flat(field)] + [m.reshape(every, cells * rows, lanes) for m in (y_lower, y_upper)],
-        copies=1 + 2 * cells,
+    y_pair, y_cross, x_pair, x_cross, x_m, field, x_lower, x_upper, y_lower, y_upper = call(
+        functools.partial(begin_kernel, cells, rows), "begin",
+        [(NVAR, 2, cells, lanes)] * 2 + [(NVAR, 2, rows, lanes)] * 2
+        + [(MATRICES, rows, lanes), (NVAR, cells * rows, lanes)] + [x_lower.shape] * 2
+        + [(every, rows, cells, lanes)] * 2,
+        [], [(cells, every, ROWS, lanes)],
+        from_hbm=[flat(field), x_lower, x_upper]
+        + [m.reshape(every, cells * rows, lanes) for m in (y_lower, y_upper)],
+        copies=3 + 2 * cells,
     )
     field = field.reshape(NVAR, cells, rows, lanes)
     y_cross, x_cross = across(y_cross, "py"), across(x_cross, "px")
-    y_pair = swap(y_pair, "py", 1)
-    halos = (x_cross, y_pair, y_cross)
+    y_pair, x_pair = swap(y_pair, "py", 1), swap(x_pair, "px", 1)
+    halos = (x_pair, x_cross, y_pair, y_cross)
 
     def exchange(axis, radices, own_m, got_m, own_v, rest):
         operands, level = [], 0
@@ -638,35 +642,29 @@
         held = hold(operands + rest)
         return held[: len(operands)], held[len(operands) :]
 
-    y_m = call(compose_y_kernel, "compose_y", [(MATRICES, cells, lanes)],
-               [y_lower, y_upper], [(rows, every, cells, lanes)])
-    x_m, y_inverse = call(
-        functools.partial(compose_x_kernel, cells), "compose_x",
-        [(MATRICES + 2 * NVAR, rows, lanes), y_inverse.shape],
-        [x_lower, x_upper, y_m, flat(field)], [(cells, every, ROWS, lanes)],
-        from_hbm=[y_inverse], copies=1,
-    )
-    y_m, y_lower, y_upper, y_inverse, x_m = hold([y_m, y_lower, y_upper, y_inverse, x_m], *halos)
+    y_m, y_inverse = call(
+        compose_y_kernel, "compose_y", [(MATRICES, cells, lanes), y_inverse.shape],
+        [y_lower, y_upper], [(rows, every, cells, lanes)], from_hbm=[y_inverse], copies=1,
+    )
     y_got = [swap(y_m, "py", k) for k in range(1, y_radices[0])]
-    x_got = [swap(x_m, "px", k) for k in range(1, x_radices[0])]
     reduced, source = call(
         local_x_kernel, "local_x",
         [(VX, NVAR, rows, lanes), (NVAR, cells, rows, lanes)],
-        [field, forcing, x_got[0], *halos, x_inverse, x_lower, x_upper],
+        [field, forcing, *halos, x_inverse, x_lower, x_upper, y_m],
         [(NVAR, cells + 4, rows + 2 * ROWS, lanes), (NVAR, cells, rows, lanes)],
     )
-    operands, (source, y_inverse, y_lower, y_upper) = exchange(
-        "px", x_radices, x_m, x_got, reduced, [source, y_inverse, y_lower, y_upper]
-    )
+    x_got = [swap(x_m, "px", k) for k in range(1, x_radices[0])]
+    rest = [source, x_lower, x_upper, y_inverse, y_lower, y_upper]
+    operands, rest = exchange("px", x_radices, x_m, x_got, reduced, rest)
     reduced, source = call(
         functools.partial(middle_kernel, x_radices), "middle",
         [(2, NVAR, cells, lanes), (NVAR, cells * rows, lanes)],
-        [*operands, source, x_lower, x_upper, y_inverse, y_lower, y_upper],
+        operands + rest,
         [(NVAR, rows, lanes), (NVAR, rows, lanes), (NVAR, cells * rows, lanes)],
     )
     y_m, *y_got = hold([y_m, *y_got], reduced)
     operands, rest = exchange(
-        "py", y_radices, y_m, y_got, reduced, [source, y_lower, y_upper]
+        "py", y_radices, y_m, y_got, reduced, [source, *rest[-2:]]
     )
     out = call(
         functools.partial(end_kernel, y_radices, cells, rows), "end",

time: 40.5 us -> 39 us (0.963)
  waiting for transfers between devices: 9.68 us -> 7.88 us
  starting transfers between devices: 21.9 us -> 22.6 us
    ppermute x14 -> x15, starting transfers between devices: 15.9 us -> 20.8 us  [swap(): return lax.ppermute(value, axis, pairs)]
    ppermute x2 -> x1, starting transfers between devices: 5.99 us -> 1.6 us  [across(): return lax.ppermute(value, axis, pairs + [(j, i) for i, j in pairs])]
    ppermute x14 -> x15, waiting for transfers between devices: 9.68 us -> 6.26 us  [swap(): return lax.ppermute(value, axis, pairs)]
    ppermute x2 -> x1, waiting for transfers between devices: 0.01 us -> 1.62 us  [across(): return lax.ppermute(value, axis, pairs + [(j, i) for i, j in pairs])]
    pallas_call x10 -> x9, Pallas kernels: 8.26 us -> 8.25 us  [call(): pl.pallas_call(kernel, name=name, out_shape=shapes[0] if single else shap...]
  transfers between devices with their start and end apart: 16 -> 17, of which waited for: 6 -> 7; matrix products, arithmetic and copies ran while one was open for 0% -> 0% of each run, Pallas kernels for 12% -> 8%
where the time goes in v4:
time: 39 us; the launch traced here: 38.8 us
  starting transfers between devices  22.6 us (58%)
  Pallas kernels  8.25 us (21%)
  waiting for transfers between devices  7.88 us (20%)
    ppermute x15, starting transfers between devices, swap(): return lax.ppermute(value, axis, pairs)  20.8 us
    pallas_call x9, Pallas kernels, call(): pl.pallas_call(kernel, name=name, out_shape=shapes[0] if single else shap...  8.25 us
    ppermute x15, waiting for transfers between devices, swap(): return lax.ppermute(value, axis, pairs)  6.26 us
    ppermute x1, waiting for transfers between devices, across(): return lax.ppermute(value, axis, pairs + [(j, i) for i, j in pairs])  1.62 us
    ppermute x1, starting transfers between devices, across(): return lax.ppermute(value, axis, pairs + [(j, i) for i, j in pairs])  1.6 us
  transfers between devices with their start and end apart: 17, of which 7 were waited for; matrix products, arithmetic and copies ran while one was open for 0% of the time, Pallas kernels for 8%

profile of v4, /device:TPU:0, one launch (start us, length us, event | category | flops | bytes accessed | tf_op | source)
XLA Modules:
  0.0 38.8 jit_solution(7192956784618080057)
XLA Ops:
  0.0 3.7 %begin.1 = (f32[5,2,8,128]{3,2,1,0:T(8,128)S(1)}, f32[5,2,8,128]{3,2,1,0:T(8,128)S(1)}, f32[5,2,16,128]{3,2,1,0:T(8,128)S(1)}, f32[5,2,16,128]{3,2,1,0:T(8,128)S...) custom-call(f32[5,128,128]{2,1,0:T(8,128)} %bitcast.10, ...), custom_call_target="tpu_custom_call" | custom-call | tf_op jit(solution)/shard_map/begin/pallas_call | solution.py:30
  3.7 0.5 %collective-permute-start.3 = (f32[75,16,128]{2,1,0:T(8,128)S(1)}, f32[75,16,128]{2,1,0:T(8,128)S(1)}, u32[]{:S(2)}, u32[]{:S(2)}) collective-permute-start(f32[75,16,128]{2,1,0:T(8,128)S(1)} %get-tuple-element.79.refs_0_), channel_id=1, source_target_pairs={{0,8},{8,0},{16,24},{24,16},{1,9},{9,1},{17,25},{25,17},{2,10},{10... | collective-permute-start | bytes 1843208 | tf_op jit(solution)/shard_map/ppermute | solution.py:585
  4.2 2.6 %collective-permute-start.6 = (f32[5,2,8,128]{3,2,1,0:T(8,128)S(1)}, f32[5,2,8,128]{3,2,1,0:T(8,128)S(1)}, u32[]{:S(2)}, u32[]{:S(2)}) collective-permute-start(f32[5,2,8,128]{3,2,1,0:T(8,128)S(1)} %get-tuple-element.83), channel_id=1, source_target_pairs={{0,1},{1,0},{2,3},{3,2},{4,5},{5,4},{6,7},{7,6},{8,9},{9,8},{10,11... | collective-permute-start | bytes 122888 | tf_op jit(solution)/shard_map/ppermute | solution.py:585
  7.0 1.6 %compose_y.1 = (f32[75,8,128]{2,1,0:T(8,128)S(1)}, f32[5,5,128,128]{3,2,1,0:T(8,128)S(1)}) custom-call(f32[25,16,8,128]{3,2,1,0:T(8,128)S(1)} %get-tuple-element.76.lower.refs_8_, f32[25,16,8,128]{3,2,1,0:T(8,128)S(1)} %get-tuple-element.77.upper.refs_9_, f32[5,5,128,128]{3,2,1,0:T(8,128)} %bitcast.7), custom_call_target="tpu_custom_call" | custom-call | tf_op jit(solution)/shard_map/compose_y/pallas_call | solution.py:30
  8.6 4.0 %collective-permute-start.2 = (f32[75,8,128]{2,1,0:T(8,128)S(1)}, f32[75,8,128]{2,1,0:T(8,128)S(1)}, u32[]{:S(2)}, u32[]{:S(2)}) collective-permute-start(f32[75,8,128]{2,1,0:T(8,128)S(1)} %get-tuple-element.78._.refs_0_), channel_id=1, source_target_pairs={{0,3},{1,2},{2,1},{3,0},{4,7},{5,6},{6,5},{7,4},{8,11},{9,10},{10,... | collective-permute-start | bytes 921608 | tf_op jit(solution)/shard_map/ppermute | solution.py:585
  12.5 0.4 %collective-permute-start.1 = (f32[75,8,128]{2,1,0:T(8,128)S(1)}, f32[75,8,128]{2,1,0:T(8,128)S(1)}, u32[]{:S(2)}, u32[]{:S(2)}) collective-permute-start(f32[75,8,128]{2,1,0:T(8,128)S(1)} %get-tuple-element.78._.refs_0_), channel_id=1, source_target_pairs={{0,2},{1,3},{2,0},{3,1},{4,6},{5,7},{6,4},{7,5},{8,10},{9,11},{10,... | collective-permute-start | bytes 921608 | tf_op jit(solution)/shard_map/ppermute | solution.py:585
  13.2 1.6 %collective-permute-start.5 = (f32[5,2,16,128]{3,2,1,0:T(8,128)S(1)}, f32[5,2,16,128]{3,2,1,0:T(8,128)S(1)}, u32[]{:S(2)}, u32[]{:S(2)}) collective-permute-start(f32[5,2,16,128]{3,2,1,0:T(8,128)S(1)} %get-tuple-element.82), channel_id=1, source_target_pairs={{8,16},{24,0},{16,8},{0,24},{9,17},{25,1},{17,9},{1,25},{10,18},{2... | collective-permute-start | bytes 245768 | tf_op jit(solution)/shard_map/ppermute | solution.py:591
  14.8 1.2 %collective-permute-start.9 = (f32[25,16,128]{2,1,0:T(8,128)S(1)}, f32[25,16,128]{2,1,0:T(8,128)S(1)}, u32[]{:S(2)}, u32[]{:S(2)}) collective-permute-start(f32[25,16,128]{2,1,0:T(8,128)S(1)} %join_matrices.2), channel_id=1, source_target_pairs={{0,16},{8,24},{16,0},{24,8},{1,17},{9,25},{17,1},{25,9},{2,18},{10... | collective-permute-start | bytes 614408 | tf_op jit(solution)/shard_map/ppermute | solution.py:585
  15.9 1.6 %collective-permute-done.5.x_cross = f32[5,2,16,128]{3,2,1,0:T(8,128)S(1)} collective-permute-done((f32[5,2,16,128]{3,2,1,0:T(8,128)S(1)}, f32[5,2,16,128]{3,2,1,0:T(8,128)S(1)}, u32[]{:S(2)}, u32[]{:S(2)}) %collective-permute-start.5) | collective-permute-done | bytes 81952 | tf_op jit(solution)/shard_map/ppermute | solution.py:591
  17.6 0.8 %local_x.1 = (f32[2,5,16,128]{3,2,1,0:T(8,128)S(1)}, f32[5,8,16,128]{3,2,1,0:T(8,128)S(1)}) custom-call(f32[5,8,16,128]{3,2,1,0:T(8,128)S(1)} %bitcast.6, f32[5,8,16,128]{3,2,1,0:T(8,128)S(1)} %copy-done.1, f32[5,2,16,128]{3,2,1,0:T(8,128)S(1)} %collective-permute-done.4.x_pair, f32[5,2,16,128]{3,2,1,0:T(8,128)S(1)} %collective-permute-done.5.x_cross, ...), custom_call_target="tpu_custom_call" | custom-call | tf_op jit(solution)/shard_map/local_x/pallas_call | solution.py:30
  18.4 1.1 %collective-permute-start.8 = (f32[2,5,16,128]{3,2,1,0:T(8,128)S(1)}, f32[2,5,16,128]{3,2,1,0:T(8,128)S(1)}, u32[]{:S(2)}, u32[]{:S(2)}) collective-permute-start(f32[2,5,16,128]{3,2,1,0:T(8,128)S(1)} %get-tuple-element.87.refs_2_), channel_id=1, source_target_pairs={{0,8},{8,0},{16,24},{24,16},{1,9},{9,1},{17,25},{25,17},{2,10},{10... | collective-permute-start | bytes 245768 | tf_op jit(solution)/shard_map/ppermute | solution.py:585
  19.5 0.9 %collective-permute-done.8.refs_3_ = f32[2,5,16,128]{3,2,1,0:T(8,128)S(1)} collective-permute-done((f32[2,5,16,128]{3,2,1,0:T(8,128)S(1)}, f32[2,5,16,128]{3,2,1,0:T(8,128)S(1)}, u32[]{:S(2)}, u32[]{:S(2)}) %collective-permute-start.8) | collective-permute-done | bytes 81952 | tf_op jit(solution)/shard_map/ppermute | solution.py:585
  20.5 1.6 %collective-permute-start.10 = (f32[5,16,128]{2,1,0:T(8,128)S(1)}, f32[5,16,128]{2,1,0:T(8,128)S(1)}, u32[]{:S(2)}, u32[]{:S(2)}) collective-permute-start(f32[5,16,128]{2,1,0:T(8,128)S(1)} %join_vectors.2.refs_5_), channel_id=1, source_target_pairs={{0,16},{8,24},{16,0},{24,8},{1,17},{9,25},{17,1},{25,9},{2,18},{10... | collective-permute-start | bytes 122888 | tf_op jit(solution)/shard_map/ppermute | solution.py:585
  22.1 2.5 %collective-permute-done.10.refs_6_ = f32[5,16,128]{2,1,0:T(8,128)S(1)} collective-permute-done((f32[5,16,128]{2,1,0:T(8,128)S(1)}, f32[5,16,128]{2,1,0:T(8,128)S(1)}, u32[]{:S(2)}, u32[]{:S(2)}) %collective-permute-start.10) | collective-permute-done | bytes 40992 | tf_op jit(solution)/shard_map/ppermute | solution.py:585
  24.5 0.8 %middle.1 = (f32[2,5,8,128]{3,2,1,0:T(8,128)S(1)}, f32[5,128,128]{2,1,0:T(8,128)S(1)}) custom-call(f32[75,16,128]{2,1,0:T(8,128)S(1)} %get-tuple-element.100.rest_0_, f32[75,16,128]{2,1,0:T(8,128)S(1)} %get-tuple-element.101.rest_1_, f32[2,5,16,128]{3,2,1,0:T(8,128)S(1)} %get-tuple-element.102.rest_2_, f32[2,5,16,128]{3,2,1,0:T(8,128)S(1)} %get-tuple-element.103.rest_3_, ...), custom_call_target="tpu_custom_call" | custom-call | tf_op jit(solution)/shard_map/middle/pallas_call | solution.py:30
  25.3 2.9 %collective-permute-start.13 = (f32[2,5,8,128]{3,2,1,0:T(8,128)S(1)}, f32[2,5,8,128]{3,2,1,0:T(8,128)S(1)}, u32[]{:S(2)}, u32[]{:S(2)}) collective-permute-start(f32[2,5,8,128]{3,2,1,0:T(8,128)S(1)} %get-tuple-element.113.refs_4_), channel_id=1, source_target_pairs={{0,3},{1,2},{2,1},{3,0},{4,7},{5,6},{6,5},{7,4},{8,11},{9,10},{10,... | collective-permute-start | bytes 122888 | tf_op jit(solution)/shard_map/ppermute | solution.py:585
  28.2 0.4 %collective-permute-start.12 = (f32[2,5,8,128]{3,2,1,0:T(8,128)S(1)}, f32[2,5,8,128]{3,2,1,0:T(8,128)S(1)}, u32[]{:S(2)}, u32[]{:S(2)}) collective-permute-start(f32[2,5,8,128]{3,2,1,0:T(8,128)S(1)} %get-tuple-element.113.refs_4_), channel_id=1, source_target_pairs={{0,2},{1,3},{2,0},{3,1},{4,6},{5,7},{6,4},{7,5},{8,10},{9,11},{10,... | collective-permute-start | bytes 122888 | tf_op jit(solution)/shard_map/ppermute | solution.py:585
  28.9 2.8 %collective-permute-start.14 = (f32[13,8,128]{2,1,0:T(8,128)S(1)}, f32[13,8,128]{2,1,0:T(8,128)S(1)}, u32[]{:S(2)}, u32[]{:S(2)}) collective-permute-start(f32[13,8,128]{2,1,0:T(8,128)S(1)} %get-tuple-element.127), channel_id=1, source_target_pairs={{0,4},{1,5},{2,6},{3,7},{4,0},{5,1},{6,2},{7,3},{8,12},{9,13},{10,... | collective-permute-start | bytes 159752 | tf_op jit(solution)/shard_map/ppermute | solution.py:585
  31.9 0.5 %collective-permute-done.12.refs_6_ = f32[2,5,8,128]{3,2,1,0:T(8,128)S(1)} collective-permute-done((f32[2,5,8,128]{3,2,1,0:T(8,128)S(1)}, f32[2,5,8,128]{3,2,1,0:T(8,128)S(1)}, u32[]{:S(2)}, u32[]{:S(2)}) %collective-permute-start.12) | collective-permute-done | bytes 40992 | tf_op jit(solution)/shard_map/ppermute | solution.py:585
  32.4 0.2 collective-permute-done.11.refs_5_
  32.7 2.7 %collective-permute-start.16 = (f32[5,8,128]{2,1,0:T(8,128)S(1)}, f32[5,8,128]{2,1,0:T(8,128)S(1)}, u32[]{:S(2)}, u32[]{:S(2)}) collective-permute-start(f32[5,8,128]{2,1,0:T(8,128)S(1)} %join_vectors.3.refs_10_), channel_id=1, source_target_pairs={{0,4},{1,5},{2,6},{3,7},{4,0},{5,1},{6,2},{7,3},{8,12},{9,13},{10,... | collective-permute-start | bytes 61448 | tf_op jit(solution)/shard_map/ppermute | solution.py:585
  35.4 1.8 %collective-permute-done.15.refs_9_ = f32[12,8,128]{2,1,0:T(8,128)S(1)} collective-permute-done((f32[12,8,128]{2,1,0:T(8,128)S(1)}, f32[12,8,128]{2,1,0:T(8,128)S(1)}, u32[]{:S(2)}, u32[]{:S(2)}) %collective-permute-start.15) | collective-permute-done | bytes 49184 | tf_op jit(solution)/shard_map/ppermute | solution.py:585
  37.2 0.2 collective-permute-done.16.refs_11_
  37.5 1.3 %end.1 = f32[5,128,128]{2,1,0:T(8,128)} custom-call(f32[75,8,128]{2,1,0:T(8,128)S(1)} %get-tuple-element.132.rest_0_, f32[75,8,128]{2,1,0:T(8,128)S(1)} %get-tuple-element.133.rest_1_, f32[75,8,128]{2,1,0:T(8,128)S(1)} %get-tuple-element.134.rest_2_, f32[75,8,128]{2,1,0:T(8,128)S(1)} %get-tuple-element.135.rest_3_, ...), custom_call_target="tpu_custom_call" | custom-call | tf_op jit(solution)/shard_map/end/pallas_call | solution.py:30
  (28 shorter events, 0.9 us)
Async XLA Ops:
  3.7 9.5 %collective-permute-start.3 = (f32[75,16,128]{2,1,0:T(8,128)S(1)}, f32[75,16,128]{2,1,0:T(8,128)S(1)}, u32[]{:S(2)}, u32[]{:S(2)}) collective-permute-start(f32[75,16,128]{2,1,0:T(8,128)S(1)} %get-tuple-element.79.refs_0_), channel_id=1, source_target_pairs={{0,8},{8,0},{16,24},{24,16},{1,9},{9,1},{17,25},{25,17},{2,10},{10... | collective-permute-start | bytes 1843208 | tf_op jit(solution)/shard_map/ppermute | solution.py:585
  4.2 8.7 %collective-permute-start.6 = (f32[5,2,8,128]{3,2,1,0:T(8,128)S(1)}, f32[5,2,8,128]{3,2,1,0:T(8,128)S(1)}, u32[]{:S(2)}, u32[]{:S(2)}) collective-permute-start(f32[5,2,8,128]{3,2,1,0:T(8,128)S(1)} %get-tuple-element.83), channel_id=1, source_target_pairs={{0,1},{1,0},{2,3},{3,2},{4,5},{5,4},{6,7},{7,6},{8,9},{9,8},{10,11... | collective-permute-start | bytes 122888 | tf_op jit(solution)/shard_map/ppermute | solution.py:585
  6.8 6.4 %collective-permute-start.7 = (f32[5,2,8,128]{3,2,1,0:T(8,128)S(1)}, f32[5,2,8,128]{3,2,1,0:T(8,128)S(1)}, u32[]{:S(2)}, u32[]{:S(2)}) collective-permute-start(f32[5,2,8,128]{3,2,1,0:T(8,128)S(1)} %get-tuple-element.84), channel_id=1, source_target_pairs={{1,2},{3,4},{5,6},{2,1},{4,3},{6,5},{0,8},{7,15},{9,10},{11,12},{1... | collective-permute-start | bytes 122888 | tf_op jit(solution)/shard_map/ppermute | solution.py:597
  7.0 10.6 %copy-start = (f32[5,5,8,16,128]{4,3,2,1,0:T(8,128)S(1)}, f32[5,5,8,16,128]{4,3,2,1,0:T(8,128)}, u32[]{:S(2)}) copy-start(f32[5,5,8,16,128]{4,3,2,1,0:T(8,128)} %inverse.1) | copy-start | bytes 4915204
  8.5 9.0 %copy-start.1 = (f32[5,8,16,128]{3,2,1,0:T(8,128)S(1)}, f32[5,8,16,128]{3,2,1,0:T(8,128)}, u32[]{:S(2)}) copy-start(f32[5,8,16,128]{3,2,1,0:T(8,128)} %forcing.1) | copy-start | bytes 983044
  8.6 20.1 %collective-permute-start.2 = (f32[75,8,128]{2,1,0:T(8,128)S(1)}, f32[75,8,128]{2,1,0:T(8,128)S(1)}, u32[]{:S(2)}, u32[]{:S(2)}) collective-permute-start(f32[75,8,128]{2,1,0:T(8,128)S(1)} %get-tuple-element.78._.refs_0_), channel_id=1, source_target_pairs={{0,3},{1,2},{2,1},{3,0},{4,7},{5,6},{6,5},{7,4},{8,11},{9,10},{10,... | collective-permute-start | bytes 921608 | tf_op jit(solution)/shard_map/ppermute | solution.py:585
  12.5 16.4 %collective-permute-start.1 = (f32[75,8,128]{2,1,0:T(8,128)S(1)}, f32[75,8,128]{2,1,0:T(8,128)S(1)}, u32[]{:S(2)}, u32[]{:S(2)}) collective-permute-start(f32[75,8,128]{2,1,0:T(8,128)S(1)} %get-tuple-element.78._.refs_0_), channel_id=1, source_target_pairs={{0,2},{1,3},{2,0},{3,1},{4,6},{5,7},{6,4},{7,5},{8,10},{9,11},{10,... | collective-permute-start | bytes 921608 | tf_op jit(solution)/shard_map/ppermute | solution.py:585
  13.0 15.9 %collective-permute-start = (f32[75,8,128]{2,1,0:T(8,128)S(1)}, f32[75,8,128]{2,1,0:T(8,128)S(1)}, u32[]{:S(2)}, u32[]{:S(2)}) collective-permute-start(f32[75,8,128]{2,1,0:T(8,128)S(1)} %get-tuple-element.78._.refs_0_), channel_id=1, source_target_pairs={{0,1},{1,0},{2,3},{3,2},{4,5},{5,4},{6,7},{7,6},{8,9},{9,8},{10,11... | collective-permute-start | bytes 921608 | tf_op jit(solution)/shard_map/ppermute | solution.py:585
  13.2 1.6 %collective-permute-start.4 = (f32[5,2,16,128]{3,2,1,0:T(8,128)S(1)}, f32[5,2,16,128]{3,2,1,0:T(8,128)S(1)}, u32[]{:S(2)}, u32[]{:S(2)}) collective-permute-start(f32[5,2,16,128]{3,2,1,0:T(8,128)S(1)} %get-tuple-element.81), channel_id=1, source_target_pairs={{0,8},{8,0},{16,24},{24,16},{1,9},{9,1},{17,25},{25,17},{2,10},{10... | collective-permute-start | bytes 245768 | tf_op jit(solution)/shard_map/ppermute | solution.py:585
  13.2 4.4 %collective-permute-start.5 = (f32[5,2,16,128]{3,2,1,0:T(8,128)S(1)}, f32[5,2,16,128]{3,2,1,0:T(8,128)S(1)}, u32[]{:S(2)}, u32[]{:S(2)}) collective-permute-start(f32[5,2,16,128]{3,2,1,0:T(8,128)S(1)} %get-tuple-element.82), channel_id=1, source_target_pairs={{8,16},{24,0},{16,8},{0,24},{9,17},{25,1},{17,9},{1,25},{10,18},{2... | collective-permute-start | bytes 245768 | tf_op jit(solution)/shard_map/ppermute | solution.py:591
  14.8 9.8 %collective-permute-start.9 = (f32[25,16,128]{2,1,0:T(8,128)S(1)}, f32[25,16,128]{2,1,0:T(8,128)S(1)}, u32[]{:S(2)}, u32[]{:S(2)}) collective-permute-start(f32[25,16,128]{2,1,0:T(8,128)S(1)} %join_matrices.2), channel_id=1, source_target_pairs={{0,16},{8,24},{16,0},{24,8},{1,17},{9,25},{17,1},{25,9},{2,18},{10... | collective-permute-start | bytes 614408 | tf_op jit(solution)/shard_map/ppermute | solution.py:585
  18.4 2.1 %collective-permute-start.8 = (f32[2,5,16,128]{3,2,1,0:T(8,128)S(1)}, f32[2,5,16,128]{3,2,1,0:T(8,128)S(1)}, u32[]{:S(2)}, u32[]{:S(2)}) collective-permute-start(f32[2,5,16,128]{3,2,1,0:T(8,128)S(1)} %get-tuple-element.87.refs_2_), channel_id=1, source_target_pairs={{0,8},{8,0},{16,24},{24,16},{1,9},{9,1},{17,25},{25,17},{2,10},{10... | collective-permute-start | bytes 245768 | tf_op jit(solution)/shard_map/ppermute | solution.py:585
  20.5 4.1 %collective-permute-start.10 = (f32[5,16,128]{2,1,0:T(8,128)S(1)}, f32[5,16,128]{2,1,0:T(8,128)S(1)}, u32[]{:S(2)}, u32[]{:S(2)}) collective-permute-start(f32[5,16,128]{2,1,0:T(8,128)S(1)} %join_vectors.2.refs_5_), channel_id=1, source_target_pairs={{0,16},{8,24},{16,0},{24,8},{1,17},{9,25},{17,1},{25,9},{2,18},{10... | collective-permute-start | bytes 122888 | tf_op jit(solution)/shard_map/ppermute | solution.py:585
  25.3 6.6 %collective-permute-start.13 = (f32[2,5,8,128]{3,2,1,0:T(8,128)S(1)}, f32[2,5,8,128]{3,2,1,0:T(8,128)S(1)}, u32[]{:S(2)}, u32[]{:S(2)}) collective-permute-start(f32[2,5,8,128]{3,2,1,0:T(8,128)S(1)} %get-tuple-element.113.refs_4_), channel_id=1, source_target_pairs={{0,3},{1,2},{2,1},{3,0},{4,7},{5,6},{6,5},{7,4},{8,11},{9,10},{10,... | collective-permute-start | bytes 122888 | tf_op jit(solution)/shard_map/ppermute | solution.py:585
  28.2 4.2 %collective-permute-start.12 = (f32[2,5,8,128]{3,2,1,0:T(8,128)S(1)}, f32[2,5,8,128]{3,2,1,0:T(8,128)S(1)}, u32[]{:S(2)}, u32[]{:S(2)}) collective-permute-start(f32[2,5,8,128]{3,2,1,0:T(8,128)S(1)} %get-tuple-element.113.refs_4_), channel_id=1, source_target_pairs={{0,2},{1,3},{2,0},{3,1},{4,6},{5,7},{6,4},{7,5},{8,10},{9,11},{10,... | collective-permute-start | bytes 122888 | tf_op jit(solution)/shard_map/ppermute | solution.py:585
  28.7 4.0 %collective-permute-start.11 = (f32[2,5,8,128]{3,2,1,0:T(8,128)S(1)}, f32[2,5,8,128]{3,2,1,0:T(8,128)S(1)}, u32[]{:S(2)}, u32[]{:S(2)}) collective-permute-start(f32[2,5,8,128]{3,2,1,0:T(8,128)S(1)} %get-tuple-element.113.refs_4_), channel_id=1, source_target_pairs={{0,1},{1,0},{2,3},{3,2},{4,5},{5,4},{6,7},{7,6},{8,9},{9,8},{10,11... | collective-permute-start | bytes 122888 | tf_op jit(solution)/shard_map/ppermute | solution.py:585
  28.9 8.3 %collective-permute-start.14 = (f32[13,8,128]{2,1,0:T(8,128)S(1)}, f32[13,8,128]{2,1,0:T(8,128)S(1)}, u32[]{:S(2)}, u32[]{:S(2)}) collective-permute-start(f32[13,8,128]{2,1,0:T(8,128)S(1)} %get-tuple-element.127), channel_id=1, source_target_pairs={{0,4},{1,5},{2,6},{3,7},{4,0},{5,1},{6,2},{7,3},{8,12},{9,13},{10,... | collective-permute-start | bytes 159752 | tf_op jit(solution)/shard_map/ppermute | solution.py:585
  31.7 5.5 %collective-permute-start.15 = (f32[12,8,128]{2,1,0:T(8,128)S(1)}, f32[12,8,128]{2,1,0:T(8,128)S(1)}, u32[]{:S(2)}, u32[]{:S(2)}) collective-permute-start(f32[12,8,128]{2,1,0:T(8,128)S(1)} %get-tuple-element.128), channel_id=1, source_target_pairs={{0,4},{1,5},{2,6},{3,7},{4,0},{5,1},{6,2},{7,3},{8,12},{9,13},{10,... | collective-permute-start | bytes 147464 | tf_op jit(solution)/shard_map/ppermute | solution.py:585
  32.7 4.7 %collective-permute-start.16 = (f32[5,8,128]{2,1,0:T(8,128)S(1)}, f32[5,8,128]{2,1,0:T(8,128)S(1)}, u32[]{:S(2)}, u32[]{:S(2)}) collective-permute-start(f32[5,8,128]{2,1,0:T(8,128)S(1)} %join_vectors.3.refs_10_), channel_id=1, source_target_pairs={{0,4},{1,5},{2,6},{3,7},{4,0},{5,1},{6,2},{7,3},{8,12},{9,13},{10,... | collective-permute-start | bytes 61448 | tf_op jit(solution)/shard_map/ppermute | solution.py:585

commit v5 on v4

--- a/solution.py
+++ b/solution.py
@@ -88,10 +88,12 @@
     return [p - q for p, q in zip(left, right, strict=True)]
 
 
-def compose_lines(length, lower_at, upper_at, store_p, load_p, emit):
-    entries = [(a, b) for a in range(NVAR) for b in range(NVAR)]
-    signed = lambda m: [-q for q in m] if length % 2 else list(m)
-    first = [lower_at(0, a, b) for a, b in entries]
+def signed(matrix, length):
+    return [-q for q in matrix] if length % 2 else list(matrix)
+
+
+def compose_forward(length, lower_at, store_p, emit):
+    first = whole(lambda a, b: lower_at(0, a, b))
     store_p(0, first)
 
     def forward(i, p):
@@ -100,47 +102,54 @@
         return tuple(p)
 
     last = lax.fori_loop(1, length, forward, tuple(first), unroll=UNROLL)
-    emit(0, signed(last))
-
+    emit(0, signed(last, length))
+
+
+def compose_backward(length, upper_at, load_p, emit):
     def backward(k, carried):
         w, r = carried
         i = length - 1 - k
-        here = [upper_at(i, a, b) for a, b in entries]
+        here = whole(lambda a, b: upper_at(i, a, b))
         at = lambda a, b: here[NVAR * a + b]
         return tuple(plus(load_p(i), matmat(at, w))), tuple(matmat(at, r))
 
-    r = tuple(upper_at(length - 1, a, b) for a, b in entries)
-    w, r = lax.fori_loop(1, length, backward, (last, r), unroll=UNROLL)
-    emit(1, signed(r))
+    w = tuple(load_p(length - 1))
+    r = tuple(whole(lambda a, b: upper_at(length - 1, a, b)))
+    w, r = lax.fori_loop(1, length, backward, (w, r), unroll=UNROLL)
+    emit(1, signed(r, length))
     emit(2, [-q for q in w])
 
 
-def compose_x(lower, upper, out, held):
+def compose_x(lower, upper, out, held, turn):
     cells, rows = lower.shape[2:4]
 
-    def group(g, _):
+    def register(g):
         here = pl.ds(pl.multiple_of(g * ROWS, ROWS), ROWS)
 
         def emit(which, matrix):
-            for a in range(NVAR):
-                for b in range(NVAR):
-                    out[entry(which, a, b), here] = matrix[NVAR * a + b]
+            for k, value in enumerate(matrix):
+                out[which * NVAR * NVAR + k, here] = value
 
         def store_p(i, p):
             for k in range(NVAR * NVAR):
-                held[i, k] = p[k]
-
-        compose_lines(
-            cells,
-            lambda i, a, b: lower[a, b, i, here],
-            lambda i, a, b: upper[a, b, i, here],
-            store_p,
-            lambda i: [held[i, k] for k in range(NVAR * NVAR)],
-            emit,
-        )
+                held[i, k, here] = p[k]
+
+        load_p = lambda i: [held[i, k, here] for k in range(NVAR * NVAR)]
+        return here, emit, store_p, load_p
+
+    def forward(g, _):
+        here, emit, store_p, _ = register(g)
+        compose_forward(cells, lambda i, a, b: lower[a, b, i, here], store_p, emit)
         return 0
 
-    lax.fori_loop(0, rows // ROWS, group, 0)
+    def backward(g, _):
+        here, emit, _, load_p = register(g)
+        compose_backward(cells, lambda i, a, b: upper[a, b, i, here], load_p, emit)
+        return 0
+
+    lax.fori_loop(0, rows // ROWS, forward, 0)
+    turn()
+    lax.fori_loop(0, rows // ROWS, backward, 0)
 
 
 def compose_y_kernel(lower, upper, y_inverse_hbm, out, y_inverse, held, semaphores):
@@ -157,13 +166,10 @@
         for k in range(NVAR * NVAR):
             held[i, k] = p[k]
 
-    compose_lines(
-        cells_y,
-        lambda j, a, b: lower[NVAR * a + b, j],
-        lambda j, a, b: upper[NVAR * a + b, j],
-        store_p,
-        lambda i: [held[i, k] for k in range(NVAR * NVAR)],
-        emit,
+    at = lambda ref: lambda j, a, b: ref[NVAR * a + b, j]
+    compose_forward(cells_y, at(lower), store_p, emit)
+    compose_backward(
+        cells_y, at(upper), lambda i: [held[i, k] for k in range(NVAR * NVAR)], emit
     )
     load.wait()
 
@@ -337,8 +343,7 @@
         x_layers(x_cross, cells - 2)
 
     copies[1].wait()
-    copies[2].wait()
-    compose_x(x_lower, x_upper, x_out, held)
+    compose_x(x_lower, x_upper, x_out, held, copies[2].wait)
     for copy in copies[3:]:
         copy.wait()
 
@@ -602,10 +607,10 @@
     every = NVAR * NVAR
     y_pair, y_cross, x_pair, x_cross, x_m, field, x_lower, x_upper, y_lower, y_upper = call(
         functools.partial(begin_kernel, cells, rows), "begin",
-        [(NVAR, 2, cells, lanes)] * 2 + [(NVAR, 2, rows, lanes)] * 2
+        [(NVAR, 2, cells, lanes)] * 2 + [(NVAR, 2, rows, lanes), (NVAR, 6, rows, lanes)]
         + [(MATRICES, rows, lanes), (NVAR, cells * rows, lanes)] + [x_lower.shape] * 2
         + [(every, rows, cells, lanes)] * 2,
-        [], [(cells, every, ROWS, lanes)],
+        [], [(cells, every, rows, lanes)],
         from_hbm=[flat(field), x_lower, x_upper]
         + [m.reshape(every, cells * rows, lanes) for m in (y_lower, y_upper)],
         copies=3 + 2 * cells,

time: 39 us -> 38 us (0.974)
  starting transfers between devices: 22.6 us -> 20.8 us
  waiting for transfers between devices: 7.88 us -> 9.12 us
  Pallas kernels: 8.25 us -> 7.84 us
    ppermute x15, waiting for transfers between devices: 6.26 us -> 9.11 us  [swap(): return lax.ppermute(value, axis, pairs)]
    ppermute x15, starting transfers between devices: 20.8 us -> 18.2 us  [swap(): return lax.ppermute(value, axis, pairs)]
    ppermute x1, waiting for transfers between devices: 1.62 us -> 0.01 us  [across(): return lax.ppermute(value, axis, pairs + [(j, i) for i, j in pairs])]
    ppermute x1, starting transfers between devices: 1.6 us -> 2.61 us  [across(): return lax.ppermute(value, axis, pairs + [(j, i) for i, j in pairs])]
    pallas_call x9, Pallas kernels: 8.25 us -> 7.83 us  [call(): pl.pallas_call(kernel, name=name, out_shape=shapes[0] if single else shap...]
  transfers between devices with their start and end apart: 17 -> 17, of which waited for: 7 -> 7; matrix products, arithmetic and copies ran while one was open for 0% -> 0% of each run, Pallas kernels for 8% -> 9%
where the time goes in v5:
time: 38 us; the launch traced here: 37.9 us
  starting transfers between devices  20.8 us (55%)
  waiting for transfers between devices  9.12 us (24%)
  Pallas kernels  7.84 us (21%)
    ppermute x15, starting transfers between devices, swap(): return lax.ppermute(value, axis, pairs)  18.2 us
    ppermute x15, waiting for transfers between devices, swap(): return lax.ppermute(value, axis, pairs)  9.11 us
    pallas_call x9, Pallas kernels, call(): pl.pallas_call(kernel, name=name, out_shape=shapes[0] if single else shap...  7.83 us
    ppermute x1, starting transfers between devices, across(): return lax.ppermute(value, axis, pairs + [(j, i) for i, j in pairs])  2.61 us
  transfers between devices with their start and end apart: 17, of which 7 were waited for; matrix products, arithmetic and copies ran while one was open for 0% of the time, Pallas kernels for 9%

profile of v5, /device:TPU:0, one launch (start us, length us, event | category | flops | bytes accessed | tf_op | source)
XLA Modules:
  0.0 37.9 jit_solution(14189159217246412860)
XLA Ops:
  0.0 3.2 %begin.1 = (f32[5,2,8,128]{3,2,1,0:T(8,128)S(1)}, f32[5,2,8,128]{3,2,1,0:T(8,128)S(1)}, f32[5,2,16,128]{3,2,1,0:T(8,128)S(1)}, f32[5,6,16,128]{3,2,1,0:T(8,128)S...) custom-call(f32[5,128,128]{2,1,0:T(8,128)} %bitcast.10, ...), custom_call_target="tpu_custom_call" | custom-call | tf_op jit(solution)/shard_map/begin/pallas_call | solution.py:30
  3.3 0.5 %collective-permute-start.3 = (f32[75,16,128]{2,1,0:T(8,128)S(1)}, f32[75,16,128]{2,1,0:T(8,128)S(1)}, u32[]{:S(2)}, u32[]{:S(2)}) collective-permute-start(f32[75,16,128]{2,1,0:T(8,128)S(1)} %get-tuple-element.79.refs_0_), channel_id=1, source_target_pairs={{0,8},{8,0},{16,24},{24,16},{1,9},{9,1},{17,25},{25,17},{2,10},{10... | collective-permute-start | bytes 1843208 | tf_op jit(solution)/shard_map/ppermute | solution.py:590
  3.8 2.6 %collective-permute-start.5 = (f32[5,6,16,128]{3,2,1,0:T(8,128)S(1)}, f32[5,6,16,128]{3,2,1,0:T(8,128)S(1)}, u32[]{:S(2)}, u32[]{:S(2)}) collective-permute-start(f32[5,6,16,128]{3,2,1,0:T(8,128)S(1)} %get-tuple-element.82), channel_id=1, source_target_pairs={{8,16},{24,0},{16,8},{0,24},{9,17},{25,1},{17,9},{1,25},{10,18},{2... | collective-permute-start | bytes 737288 | tf_op jit(solution)/shard_map/ppermute | solution.py:596
  6.4 1.5 %collective-permute-start.6 = (f32[5,2,8,128]{3,2,1,0:T(8,128)S(1)}, f32[5,2,8,128]{3,2,1,0:T(8,128)S(1)}, u32[]{:S(2)}, u32[]{:S(2)}) collective-permute-start(f32[5,2,8,128]{3,2,1,0:T(8,128)S(1)} %get-tuple-element.83), channel_id=1, source_target_pairs={{0,1},{1,0},{2,3},{3,2},{4,5},{5,4},{6,7},{7,6},{8,9},{9,8},{10,11... | collective-permute-start | bytes 122888 | tf_op jit(solution)/shard_map/ppermute | solution.py:590
  7.9 1.6 %compose_y.1 = (f32[75,8,128]{2,1,0:T(8,128)S(1)}, f32[5,5,128,128]{3,2,1,0:T(8,128)S(1)}) custom-call(f32[25,16,8,128]{3,2,1,0:T(8,128)S(1)} %get-tuple-element.76.lower.refs_8_, f32[25,16,8,128]{3,2,1,0:T(8,128)S(1)} %get-tuple-element.77.upper.refs_9_, f32[5,5,128,128]{3,2,1,0:T(8,128)} %bitcast.7), custom_call_target="tpu_custom_call" | custom-call | tf_op jit(solution)/shard_map/compose_y/pallas_call | solution.py:30
  9.5 4.1 %collective-permute-start.2 = (f32[75,8,128]{2,1,0:T(8,128)S(1)}, f32[75,8,128]{2,1,0:T(8,128)S(1)}, u32[]{:S(2)}, u32[]{:S(2)}) collective-permute-start(f32[75,8,128]{2,1,0:T(8,128)S(1)} %get-tuple-element.78._.refs_0_), channel_id=1, source_target_pairs={{0,3},{1,2},{2,1},{3,0},{4,7},{5,6},{6,5},{7,4},{8,11},{9,10},{10,... | collective-permute-start | bytes 921608 | tf_op jit(solution)/shard_map/ppermute | solution.py:590
  13.6 0.5 %collective-permute-start.1 = (f32[75,8,128]{2,1,0:T(8,128)S(1)}, f32[75,8,128]{2,1,0:T(8,128)S(1)}, u32[]{:S(2)}, u32[]{:S(2)}) collective-permute-start(f32[75,8,128]{2,1,0:T(8,128)S(1)} %get-tuple-element.78._.refs_0_), channel_id=1, source_target_pairs={{0,2},{1,3},{2,0},{3,1},{4,6},{5,7},{6,4},{7,5},{8,10},{9,11},{10,... | collective-permute-start | bytes 921608 | tf_op jit(solution)/shard_map/ppermute | solution.py:590
  14.1 0.2 collective-permute-start
  14.3 1.3 %collective-permute-done.4.x_pair = f32[5,2,16,128]{3,2,1,0:T(8,128)S(1)} collective-permute-done((f32[5,2,16,128]{3,2,1,0:T(8,128)S(1)}, f32[5,2,16,128]{3,2,1,0:T(8,128)S(1)}, u32[]{:S(2)}, u32[]{:S(2)}) %collective-permute-start.4) | collective-permute-done | bytes 81952 | tf_op jit(solution)/shard_map/ppermute | solution.py:590
  15.5 0.5 %collective-permute-start.9 = (f32[25,16,128]{2,1,0:T(8,128)S(1)}, f32[25,16,128]{2,1,0:T(8,128)S(1)}, u32[]{:S(2)}, u32[]{:S(2)}) collective-permute-start(f32[25,16,128]{2,1,0:T(8,128)S(1)} %join_matrices.2), channel_id=1, source_target_pairs={{0,16},{8,24},{16,0},{24,8},{1,17},{9,25},{17,1},{25,9},{2,18},{10... | collective-permute-start | bytes 614408 | tf_op jit(solution)/shard_map/ppermute | solution.py:590
  16.1 0.8 %local_x.1 = (f32[2,5,16,128]{3,2,1,0:T(8,128)S(1)}, f32[5,8,16,128]{3,2,1,0:T(8,128)S(1)}) custom-call(f32[5,8,16,128]{3,2,1,0:T(8,128)S(1)} %bitcast.6, f32[5,8,16,128]{3,2,1,0:T(8,128)S(1)} %copy-done.1, f32[5,2,16,128]{3,2,1,0:T(8,128)S(1)} %collective-permute-done.4.x_pair, f32[5,6,16,128]{3,2,1,0:T(8,128)S(1)} %collective-permute-done.5.x_cross, ...), custom_call_target="tpu_custom_call" | custom-call | tf_op jit(solution)/shard_map/local_x/pallas_call | solution.py:30
  17.0 1.3 %collective-permute-done.8.refs_3_ = f32[2,5,16,128]{3,2,1,0:T(8,128)S(1)} collective-permute-done((f32[2,5,16,128]{3,2,1,0:T(8,128)S(1)}, f32[2,5,16,128]{3,2,1,0:T(8,128)S(1)}, u32[]{:S(2)}, u32[]{:S(2)}) %collective-permute-start.8) | collective-permute-done | bytes 81952 | tf_op jit(solution)/shard_map/ppermute | solution.py:590
  18.3 1.6 %collective-permute-start.10 = (f32[5,16,128]{2,1,0:T(8,128)S(1)}, f32[5,16,128]{2,1,0:T(8,128)S(1)}, u32[]{:S(2)}, u32[]{:S(2)}) collective-permute-start(f32[5,16,128]{2,1,0:T(8,128)S(1)} %join_vectors.2.refs_5_), channel_id=1, source_target_pairs={{0,16},{8,24},{16,0},{24,8},{1,17},{9,25},{17,1},{25,9},{2,18},{10... | collective-permute-start | bytes 122888 | tf_op jit(solution)/shard_map/ppermute | solution.py:590
  19.9 3.7 %collective-permute-done.10.refs_6_ = f32[5,16,128]{2,1,0:T(8,128)S(1)} collective-permute-done((f32[5,16,128]{2,1,0:T(8,128)S(1)}, f32[5,16,128]{2,1,0:T(8,128)S(1)}, u32[]{:S(2)}, u32[]{:S(2)}) %collective-permute-start.10) | collective-permute-done | bytes 40992 | tf_op jit(solution)/shard_map/ppermute | solution.py:590
  23.6 0.8 %middle.1 = (f32[2,5,8,128]{3,2,1,0:T(8,128)S(1)}, f32[5,128,128]{2,1,0:T(8,128)S(1)}) custom-call(f32[75,16,128]{2,1,0:T(8,128)S(1)} %get-tuple-element.100.rest_0_, f32[75,16,128]{2,1,0:T(8,128)S(1)} %get-tuple-element.101.rest_1_, f32[2,5,16,128]{3,2,1,0:T(8,128)S(1)} %get-tuple-element.102.rest_2_, f32[2,5,16,128]{3,2,1,0:T(8,128)S(1)} %get-tuple-element.103.rest_3_, ...), custom_call_target="tpu_custom_call" | custom-call | tf_op jit(solution)/shard_map/middle/pallas_call | solution.py:30
  24.4 2.9 %collective-permute-start.13 = (f32[2,5,8,128]{3,2,1,0:T(8,128)S(1)}, f32[2,5,8,128]{3,2,1,0:T(8,128)S(1)}, u32[]{:S(2)}, u32[]{:S(2)}) collective-permute-start(f32[2,5,8,128]{3,2,1,0:T(8,128)S(1)} %get-tuple-element.113.refs_4_), channel_id=1, source_target_pairs={{0,3},{1,2},{2,1},{3,0},{4,7},{5,6},{6,5},{7,4},{8,11},{9,10},{10,... | collective-permute-start | bytes 122888 | tf_op jit(solution)/shard_map/ppermute | solution.py:590
  27.3 0.4 %collective-permute-start.12 = (f32[2,5,8,128]{3,2,1,0:T(8,128)S(1)}, f32[2,5,8,128]{3,2,1,0:T(8,128)S(1)}, u32[]{:S(2)}, u32[]{:S(2)}) collective-permute-start(f32[2,5,8,128]{3,2,1,0:T(8,128)S(1)} %get-tuple-element.113.refs_4_), channel_id=1, source_target_pairs={{0,2},{1,3},{2,0},{3,1},{4,6},{5,7},{6,4},{7,5},{8,10},{9,11},{10,... | collective-permute-start | bytes 122888 | tf_op jit(solution)/shard_map/ppermute | solution.py:590
  27.7 0.2 collective-permute-start.11
  27.9 2.8 %collective-permute-start.14 = (f32[13,8,128]{2,1,0:T(8,128)S(1)}, f32[13,8,128]{2,1,0:T(8,128)S(1)}, u32[]{:S(2)}, u32[]{:S(2)}) collective-permute-start(f32[13,8,128]{2,1,0:T(8,128)S(1)} %get-tuple-element.127), channel_id=1, source_target_pairs={{0,4},{1,5},{2,6},{3,7},{4,0},{5,1},{6,2},{7,3},{8,12},{9,13},{10,... | collective-permute-start | bytes 159752 | tf_op jit(solution)/shard_map/ppermute | solution.py:590
  30.9 0.7 %collective-permute-done.12.refs_6_ = f32[2,5,8,128]{3,2,1,0:T(8,128)S(1)} collective-permute-done((f32[2,5,8,128]{3,2,1,0:T(8,128)S(1)}, f32[2,5,8,128]{3,2,1,0:T(8,128)S(1)}, u32[]{:S(2)}, u32[]{:S(2)}) %collective-permute-start.12) | collective-permute-done | bytes 40992 | tf_op jit(solution)/shard_map/ppermute | solution.py:590
  31.8 2.7 %collective-permute-start.16 = (f32[5,8,128]{2,1,0:T(8,128)S(1)}, f32[5,8,128]{2,1,0:T(8,128)S(1)}, u32[]{:S(2)}, u32[]{:S(2)}) collective-permute-start(f32[5,8,128]{2,1,0:T(8,128)S(1)} %join_vectors.3.refs_10_), channel_id=1, source_target_pairs={{0,4},{1,5},{2,6},{3,7},{4,0},{5,1},{6,2},{7,3},{8,12},{9,13},{10,... | collective-permute-start | bytes 61448 | tf_op jit(solution)/shard_map/ppermute | solution.py:590
  34.5 1.8 %collective-permute-done.15.refs_9_ = f32[12,8,128]{2,1,0:T(8,128)S(1)} collective-permute-done((f32[12,8,128]{2,1,0:T(8,128)S(1)}, f32[12,8,128]{2,1,0:T(8,128)S(1)}, u32[]{:S(2)}, u32[]{:S(2)}) %collective-permute-start.15) | collective-permute-done | bytes 49184 | tf_op jit(solution)/shard_map/ppermute | solution.py:590
  36.3 0.3 collective-permute-done.16.refs_11_
  36.5 1.3 %end.1 = f32[5,128,128]{2,1,0:T(8,128)} custom-call(f32[75,8,128]{2,1,0:T(8,128)S(1)} %get-tuple-element.132.rest_0_, f32[75,8,128]{2,1,0:T(8,128)S(1)} %get-tuple-element.133.rest_1_, f32[75,8,128]{2,1,0:T(8,128)S(1)} %get-tuple-element.134.rest_2_, f32[75,8,128]{2,1,0:T(8,128)S(1)} %get-tuple-element.135.rest_3_, ...), custom_call_target="tpu_custom_call" | custom-call | tf_op jit(solution)/shard_map/end/pallas_call | solution.py:30
  (28 shorter events, 0.4 us)
Async XLA Ops:
  3.3 11.0 %collective-permute-start.3 = (f32[75,16,128]{2,1,0:T(8,128)S(1)}, f32[75,16,128]{2,1,0:T(8,128)S(1)}, u32[]{:S(2)}, u32[]{:S(2)}) collective-permute-start(f32[75,16,128]{2,1,0:T(8,128)S(1)} %get-tuple-element.79.refs_0_), channel_id=1, source_target_pairs={{0,8},{8,0},{16,24},{24,16},{1,9},{9,1},{17,25},{25,17},{2,10},{10... | collective-permute-start | bytes 1843208 | tf_op jit(solution)/shard_map/ppermute | solution.py:590
  3.8 12.3 %collective-permute-start.5 = (f32[5,6,16,128]{3,2,1,0:T(8,128)S(1)}, f32[5,6,16,128]{3,2,1,0:T(8,128)S(1)}, u32[]{:S(2)}, u32[]{:S(2)}) collective-permute-start(f32[5,6,16,128]{3,2,1,0:T(8,128)S(1)} %get-tuple-element.82), channel_id=1, source_target_pairs={{8,16},{24,0},{16,8},{0,24},{9,17},{25,1},{17,9},{1,25},{10,18},{2... | collective-permute-start | bytes 737288 | tf_op jit(solution)/shard_map/ppermute | solution.py:596
  6.4 7.2 %collective-permute-start.6 = (f32[5,2,8,128]{3,2,1,0:T(8,128)S(1)}, f32[5,2,8,128]{3,2,1,0:T(8,128)S(1)}, u32[]{:S(2)}, u32[]{:S(2)}) collective-permute-start(f32[5,2,8,128]{3,2,1,0:T(8,128)S(1)} %get-tuple-element.83), channel_id=1, source_target_pairs={{0,1},{1,0},{2,3},{3,2},{4,5},{5,4},{6,7},{7,6},{8,9},{9,8},{10,11... | collective-permute-start | bytes 122888 | tf_op jit(solution)/shard_map/ppermute | solution.py:590
  7.9 6.2 %collective-permute-start.7 = (f32[5,2,8,128]{3,2,1,0:T(8,128)S(1)}, f32[5,2,8,128]{3,2,1,0:T(8,128)S(1)}, u32[]{:S(2)}, u32[]{:S(2)}) collective-permute-start(f32[5,2,8,128]{3,2,1,0:T(8,128)S(1)} %get-tuple-element.84), channel_id=1, source_target_pairs={{1,2},{3,4},{5,6},{2,1},{4,3},{6,5},{0,8},{7,15},{9,10},{11,12},{1... | collective-permute-start | bytes 122888 | tf_op jit(solution)/shard_map/ppermute | solution.py:602
  7.9 8.2 %copy-start = (f32[5,5,8,16,128]{4,3,2,1,0:T(8,128)S(1)}, f32[5,5,8,16,128]{4,3,2,1,0:T(8,128)}, u32[]{:S(2)}) copy-start(f32[5,5,8,16,128]{4,3,2,1,0:T(8,128)} %inverse.1) | copy-start | bytes 4915204
  9.5 6.6 %copy-start.1 = (f32[5,8,16,128]{3,2,1,0:T(8,128)S(1)}, f32[5,8,16,128]{3,2,1,0:T(8,128)}, u32[]{:S(2)}) copy-start(f32[5,8,16,128]{3,2,1,0:T(8,128)} %forcing.1) | copy-start | bytes 983044
  9.5 18.2 %collective-permute-start.2 = (f32[75,8,128]{2,1,0:T(8,128)S(1)}, f32[75,8,128]{2,1,0:T(8,128)S(1)}, u32[]{:S(2)}, u32[]{:S(2)}) collective-permute-start(f32[75,8,128]{2,1,0:T(8,128)S(1)} %get-tuple-element.78._.refs_0_), channel_id=1, source_target_pairs={{0,3},{1,2},{2,1},{3,0},{4,7},{5,6},{6,5},{7,4},{8,11},{9,10},{10,... | collective-permute-start | bytes 921608 | tf_op jit(solution)/shard_map/ppermute | solution.py:590
  13.6 14.3 %collective-permute-start.1 = (f32[75,8,128]{2,1,0:T(8,128)S(1)}, f32[75,8,128]{2,1,0:T(8,128)S(1)}, u32[]{:S(2)}, u32[]{:S(2)}) collective-permute-start(f32[75,8,128]{2,1,0:T(8,128)S(1)} %get-tuple-element.78._.refs_0_), channel_id=1, source_target_pairs={{0,2},{1,3},{2,0},{3,1},{4,6},{5,7},{6,4},{7,5},{8,10},{9,11},{10,... | collective-permute-start | bytes 921608 | tf_op jit(solution)/shard_map/ppermute | solution.py:590
  14.1 13.9 %collective-permute-start = (f32[75,8,128]{2,1,0:T(8,128)S(1)}, f32[75,8,128]{2,1,0:T(8,128)S(1)}, u32[]{:S(2)}, u32[]{:S(2)}) collective-permute-start(f32[75,8,128]{2,1,0:T(8,128)S(1)} %get-tuple-element.78._.refs_0_), channel_id=1, source_target_pairs={{0,1},{1,0},{2,3},{3,2},{4,5},{5,4},{6,7},{7,6},{8,9},{9,8},{10,11... | collective-permute-start | bytes 921608 | tf_op jit(solution)/shard_map/ppermute | solution.py:590
  14.3 1.3 %collective-permute-start.4 = (f32[5,2,16,128]{3,2,1,0:T(8,128)S(1)}, f32[5,2,16,128]{3,2,1,0:T(8,128)S(1)}, u32[]{:S(2)}, u32[]{:S(2)}) collective-permute-start(f32[5,2,16,128]{3,2,1,0:T(8,128)S(1)} %get-tuple-element.81), channel_id=1, source_target_pairs={{0,8},{8,0},{16,24},{24,16},{1,9},{9,1},{17,25},{25,17},{2,10},{10... | collective-permute-start | bytes 245768 | tf_op jit(solution)/shard_map/ppermute | solution.py:590
  15.5 8.0 %collective-permute-start.9 = (f32[25,16,128]{2,1,0:T(8,128)S(1)}, f32[25,16,128]{2,1,0:T(8,128)S(1)}, u32[]{:S(2)}, u32[]{:S(2)}) collective-permute-start(f32[25,16,128]{2,1,0:T(8,128)S(1)} %join_matrices.2), channel_id=1, source_target_pairs={{0,16},{8,24},{16,0},{24,8},{1,17},{9,25},{17,1},{25,9},{2,18},{10... | collective-permute-start | bytes 614408 | tf_op jit(solution)/shard_map/ppermute | solution.py:590
  16.9 1.3 %collective-permute-start.8 = (f32[2,5,16,128]{3,2,1,0:T(8,128)S(1)}, f32[2,5,16,128]{3,2,1,0:T(8,128)S(1)}, u32[]{:S(2)}, u32[]{:S(2)}) collective-permute-start(f32[2,5,16,128]{3,2,1,0:T(8,128)S(1)} %get-tuple-element.87.refs_2_), channel_id=1, source_target_pairs={{0,8},{8,0},{16,24},{24,16},{1,9},{9,1},{17,25},{25,17},{2,10},{10... | collective-permute-start | bytes 245768 | tf_op jit(solution)/shard_map/ppermute | solution.py:590
  18.3 5.3 %collective-permute-start.10 = (f32[5,16,128]{2,1,0:T(8,128)S(1)}, f32[5,16,128]{2,1,0:T(8,128)S(1)}, u32[]{:S(2)}, u32[]{:S(2)}) collective-permute-start(f32[5,16,128]{2,1,0:T(8,128)S(1)} %join_vectors.2.refs_5_), channel_id=1, source_target_pairs={{0,16},{8,24},{16,0},{24,8},{1,17},{9,25},{17,1},{25,9},{2,18},{10... | collective-permute-start | bytes 122888 | tf_op jit(solution)/shard_map/ppermute | solution.py:590
  24.4 6.6 %collective-permute-start.13 = (f32[2,5,8,128]{3,2,1,0:T(8,128)S(1)}, f32[2,5,8,128]{3,2,1,0:T(8,128)S(1)}, u32[]{:S(2)}, u32[]{:S(2)}) collective-permute-start(f32[2,5,8,128]{3,2,1,0:T(8,128)S(1)} %get-tuple-element.113.refs_4_), channel_id=1, source_target_pairs={{0,3},{1,2},{2,1},{3,0},{4,7},{5,6},{6,5},{7,4},{8,11},{9,10},{10,... | collective-permute-start | bytes 122888 | tf_op jit(solution)/shard_map/ppermute | solution.py:590
  27.3 4.4 %collective-permute-start.12 = (f32[2,5,8,128]{3,2,1,0:T(8,128)S(1)}, f32[2,5,8,128]{3,2,1,0:T(8,128)S(1)}, u32[]{:S(2)}, u32[]{:S(2)}) collective-permute-start(f32[2,5,8,128]{3,2,1,0:T(8,128)S(1)} %get-tuple-element.113.refs_4_), channel_id=1, source_target_pairs={{0,2},{1,3},{2,0},{3,1},{4,6},{5,7},{6,4},{7,5},{8,10},{9,11},{10,... | collective-permute-start | bytes 122888 | tf_op jit(solution)/shard_map/ppermute | solution.py:590
  27.7 4.0 %collective-permute-start.11 = (f32[2,5,8,128]{3,2,1,0:T(8,128)S(1)}, f32[2,5,8,128]{3,2,1,0:T(8,128)S(1)}, u32[]{:S(2)}, u32[]{:S(2)}) collective-permute-start(f32[2,5,8,128]{3,2,1,0:T(8,128)S(1)} %get-tuple-element.113.refs_4_), channel_id=1, source_target_pairs={{0,1},{1,0},{2,3},{3,2},{4,5},{5,4},{6,7},{7,6},{8,9},{9,8},{10,11... | collective-permute-start | bytes 122888 | tf_op jit(solution)/shard_map/ppermute | solution.py:590
  27.9 8.3 %collective-permute-start.14 = (f32[13,8,128]{2,1,0:T(8,128)S(1)}, f32[13,8,128]{2,1,0:T(8,128)S(1)}, u32[]{:S(2)}, u32[]{:S(2)}) collective-permute-start(f32[13,8,128]{2,1,0:T(8,128)S(1)} %get-tuple-element.127), channel_id=1, source_target_pairs={{0,4},{1,5},{2,6},{3,7},{4,0},{5,1},{6,2},{7,3},{8,12},{9,13},{10,... | collective-permute-start | bytes 159752 | tf_op jit(solution)/shard_map/ppermute | solution.py:590
  30.8 5.5 %collective-permute-start.15 = (f32[12,8,128]{2,1,0:T(8,128)S(1)}, f32[12,8,128]{2,1,0:T(8,128)S(1)}, u32[]{:S(2)}, u32[]{:S(2)}) collective-permute-start(f32[12,8,128]{2,1,0:T(8,128)S(1)} %get-tuple-element.128), channel_id=1, source_target_pairs={{0,4},{1,5},{2,6},{3,7},{4,0},{5,1},{6,2},{7,3},{8,12},{9,13},{10,... | collective-permute-start | bytes 147464 | tf_op jit(solution)/shard_map/ppermute | solution.py:590
  31.8 4.7 %collective-permute-start.16 = (f32[5,8,128]{2,1,0:T(8,128)S(1)}, f32[5,8,128]{2,1,0:T(8,128)S(1)}, u32[]{:S(2)}, u32[]{:S(2)}) collective-permute-start(f32[5,8,128]{2,1,0:T(8,128)S(1)} %join_vectors.3.refs_10_), channel_id=1, source_target_pairs={{0,4},{1,5},{2,6},{3,7},{4,0},{5,1},{6,2},{7,3},{8,12},{9,13},{10,... | collective-permute-start | bytes 61448 | tf_op jit(solution)/shard_map/ppermute | solution.py:590

commit v6 on v5

--- a/solution.py
+++ b/solution.py
@@ -14,7 +14,8 @@
 UNROLL = 3
 MATRICES = 3 * NVAR * NVAR
 VX = 2
-PIECES = {"px": (25,), "py": (13, 12)}
+SCALED = ("py",)
+PIECES = {"px": (25,), "py": (13, 13)}
 VMEM_BYTES = 12 * 1024 * 1024
 
 
@@ -407,6 +408,32 @@
         k -= size
 
 
+def rescaled(matrix, log):
+    largest = jnp.maximum(functools.reduce(jnp.maximum, [jnp.abs(q) for q in matrix]), 1.0)
+    factor = 1.0 / largest
+    return [q * factor for q in matrix], log + jnp.log(largest)
+
+
+def scaled_union(group, at):
+    f = [None, rescaled(whole(at(group[0], 0)), 0.0)]
+    for m in group[1:-1]:
+        matrix, log = f[-1]
+        f.append(rescaled(matmat(at(m, 0), matrix), log))
+    matrix, log = f[-1]
+    c, log = rescaled(matmat(at(group[-1], 2), matrix), log)
+    for k in reversed(range(len(group) - 1)):
+        through = matmat(at(group[k], 1), c)
+        if k:
+            own, own_log = f[k]
+            own = matmat(at(group[k], 2), own)
+        else:
+            own, own_log = whole(at(group[0], 2)), jnp.zeros_like(log)
+        top = jnp.maximum(log, own_log)
+        left, right = jnp.exp(log - top), jnp.exp(own_log - top)
+        c, log = rescaled([p * left + q * right for p, q in zip(through, own)], top)
+    return c, log
+
+
 def join_matrices_kernel(axis, level, radix, last, *refs):
     bundles, outs = refs[:radix], refs[radix:]
     lines = outs[0].shape[-2]
@@ -424,6 +451,10 @@
                     else:
                         outs[0][which * NVAR * NVAR + k, here] = value
 
+            if last and axis in SCALED:
+                c, log = scaled_union(group, at)
+                emit(2, c + [log])
+                return 0
             f = [None, whole(at(group[0], 0))]
             for m in group[1:-1]:
                 f.append(matmat(at(m, 0), f[-1]))
@@ -461,6 +492,10 @@
     @pl.when(bit(axis, levels[-1]) == 0)
     def _():
         through = matvec(got_c, [own[k] for k in range(NVAR)])
+        if axis in SCALED:
+            piece, at_k = piece_of(axis, NVAR * NVAR)
+            third = jnp.exp(c_pieces[piece][at_k] * (1.0 / 3.0))
+            through = [t * third * third * third for t in through]
         for k in range(NVAR):
             f_ref[k] = jnp.zeros(shape, F32)
             b_ref[k] = through[k] + got[k]

time: 38 us -> 38.2 us (level)
  no operation moved by 1% of the time
where the time goes in v6:
time: 38.2 us; the launch traced here: 38 us
  starting transfers between devices  20.8 us (54%)
  waiting for transfers between devices  9.25 us (24%)
  Pallas kernels  7.84 us (21%)
    ppermute x15, starting transfers between devices, swap(): return lax.ppermute(value, axis, pairs)  18.2 us
    ppermute x15, waiting for transfers between devices, swap(): return lax.ppermute(value, axis, pairs)  9.25 us
    pallas_call x9, Pallas kernels, call(): pl.pallas_call(kernel, name=name, out_shape=shapes[0] if single else shap...  7.84 us
    ppermute x1, starting transfers between devices, across(): return lax.ppermute(value, axis, pairs + [(j, i) for i, j in pairs])  2.61 us
  transfers between devices with their start and end apart: 17, of which 7 were waited for; matrix products, arithmetic and copies ran while one was open for 0% of the time, Pallas kernels for 9%

profile of v6, /device:TPU:0, one launch (start us, length us, event | category | flops | bytes accessed | tf_op | source)
XLA Modules:
  0.0 38.0 jit_solution(12060651940448669859)
XLA Ops:
  0.0 3.2 %begin.1 = (f32[5,2,8,128]{3,2,1,0:T(8,128)S(1)}, f32[5,2,8,128]{3,2,1,0:T(8,128)S(1)}, f32[5,2,16,128]{3,2,1,0:T(8,128)S(1)}, f32[5,6,16,128]{3,2,1,0:T(8,128)S...) custom-call(f32[5,128,128]{2,1,0:T(8,128)} %bitcast.10, ...), custom_call_target="tpu_custom_call" | custom-call | tf_op jit(solution)/shard_map/begin/pallas_call | solution.py:31
  3.3 0.5 %collective-permute-start.3 = (f32[75,16,128]{2,1,0:T(8,128)S(1)}, f32[75,16,128]{2,1,0:T(8,128)S(1)}, u32[]{:S(2)}, u32[]{:S(2)}) collective-permute-start(f32[75,16,128]{2,1,0:T(8,128)S(1)} %get-tuple-element.79.refs_0_), channel_id=1, source_target_pairs={{0,8},{8,0},{16,24},{24,16},{1,9},{9,1},{17,25},{25,17},{2,10},{10... | collective-permute-start | bytes 1843208 | tf_op jit(solution)/shard_map/ppermute | solution.py:625
  3.8 2.6 %collective-permute-start.5 = (f32[5,6,16,128]{3,2,1,0:T(8,128)S(1)}, f32[5,6,16,128]{3,2,1,0:T(8,128)S(1)}, u32[]{:S(2)}, u32[]{:S(2)}) collective-permute-start(f32[5,6,16,128]{3,2,1,0:T(8,128)S(1)} %get-tuple-element.82), channel_id=1, source_target_pairs={{8,16},{24,0},{16,8},{0,24},{9,17},{25,1},{17,9},{1,25},{10,18},{2... | collective-permute-start | bytes 737288 | tf_op jit(solution)/shard_map/ppermute | solution.py:631
  6.4 1.5 %collective-permute-start.6 = (f32[5,2,8,128]{3,2,1,0:T(8,128)S(1)}, f32[5,2,8,128]{3,2,1,0:T(8,128)S(1)}, u32[]{:S(2)}, u32[]{:S(2)}) collective-permute-start(f32[5,2,8,128]{3,2,1,0:T(8,128)S(1)} %get-tuple-element.83), channel_id=1, source_target_pairs={{0,1},{1,0},{2,3},{3,2},{4,5},{5,4},{6,7},{7,6},{8,9},{9,8},{10,11... | collective-permute-start | bytes 122888 | tf_op jit(solution)/shard_map/ppermute | solution.py:625
  7.9 1.6 %compose_y.1 = (f32[75,8,128]{2,1,0:T(8,128)S(1)}, f32[5,5,128,128]{3,2,1,0:T(8,128)S(1)}) custom-call(f32[25,16,8,128]{3,2,1,0:T(8,128)S(1)} %get-tuple-element.76.lower.refs_8_, f32[25,16,8,128]{3,2,1,0:T(8,128)S(1)} %get-tuple-element.77.upper.refs_9_, f32[5,5,128,128]{3,2,1,0:T(8,128)} %bitcast.7), custom_call_target="tpu_custom_call" | custom-call | tf_op jit(solution)/shard_map/compose_y/pallas_call | solution.py:31
  9.5 4.1 %collective-permute-start.2 = (f32[75,8,128]{2,1,0:T(8,128)S(1)}, f32[75,8,128]{2,1,0:T(8,128)S(1)}, u32[]{:S(2)}, u32[]{:S(2)}) collective-permute-start(f32[75,8,128]{2,1,0:T(8,128)S(1)} %get-tuple-element.78._.refs_0_), channel_id=1, source_target_pairs={{0,3},{1,2},{2,1},{3,0},{4,7},{5,6},{6,5},{7,4},{8,11},{9,10},{10,... | collective-permute-start | bytes 921608 | tf_op jit(solution)/shard_map/ppermute | solution.py:625
  13.6 0.5 %collective-permute-start.1 = (f32[75,8,128]{2,1,0:T(8,128)S(1)}, f32[75,8,128]{2,1,0:T(8,128)S(1)}, u32[]{:S(2)}, u32[]{:S(2)}) collective-permute-start(f32[75,8,128]{2,1,0:T(8,128)S(1)} %get-tuple-element.78._.refs_0_), channel_id=1, source_target_pairs={{0,2},{1,3},{2,0},{3,1},{4,6},{5,7},{6,4},{7,5},{8,10},{9,11},{10,... | collective-permute-start | bytes 921608 | tf_op jit(solution)/shard_map/ppermute | solution.py:625
  14.1 0.2 collective-permute-start
  14.3 1.3 %collective-permute-done.4.x_pair = f32[5,2,16,128]{3,2,1,0:T(8,128)S(1)} collective-permute-done((f32[5,2,16,128]{3,2,1,0:T(8,128)S(1)}, f32[5,2,16,128]{3,2,1,0:T(8,128)S(1)}, u32[]{:S(2)}, u32[]{:S(2)}) %collective-permute-start.4) | collective-permute-done | bytes 81952 | tf_op jit(solution)/shard_map/ppermute | solution.py:625
  15.5 0.5 %collective-permute-start.9 = (f32[25,16,128]{2,1,0:T(8,128)S(1)}, f32[25,16,128]{2,1,0:T(8,128)S(1)}, u32[]{:S(2)}, u32[]{:S(2)}) collective-permute-start(f32[25,16,128]{2,1,0:T(8,128)S(1)} %join_matrices.2), channel_id=1, source_target_pairs={{0,16},{8,24},{16,0},{24,8},{1,17},{9,25},{17,1},{25,9},{2,18},{10... | collective-permute-start | bytes 614408 | tf_op jit(solution)/shard_map/ppermute | solution.py:625
  16.1 0.8 %local_x.1 = (f32[2,5,16,128]{3,2,1,0:T(8,128)S(1)}, f32[5,8,16,128]{3,2,1,0:T(8,128)S(1)}) custom-call(f32[5,8,16,128]{3,2,1,0:T(8,128)S(1)} %bitcast.6, f32[5,8,16,128]{3,2,1,0:T(8,128)S(1)} %copy-done.1, f32[5,2,16,128]{3,2,1,0:T(8,128)S(1)} %collective-permute-done.4.x_pair, f32[5,6,16,128]{3,2,1,0:T(8,128)S(1)} %collective-permute-done.5.x_cross, ...), custom_call_target="tpu_custom_call" | custom-call | tf_op jit(solution)/shard_map/local_x/pallas_call | solution.py:31
  17.0 1.3 %collective-permute-done.8.refs_3_ = f32[2,5,16,128]{3,2,1,0:T(8,128)S(1)} collective-permute-done((f32[2,5,16,128]{3,2,1,0:T(8,128)S(1)}, f32[2,5,16,128]{3,2,1,0:T(8,128)S(1)}, u32[]{:S(2)}, u32[]{:S(2)}) %collective-permute-start.8) | collective-permute-done | bytes 81952 | tf_op jit(solution)/shard_map/ppermute | solution.py:625
  18.3 1.6 %collective-permute-start.10 = (f32[5,16,128]{2,1,0:T(8,128)S(1)}, f32[5,16,128]{2,1,0:T(8,128)S(1)}, u32[]{:S(2)}, u32[]{:S(2)}) collective-permute-start(f32[5,16,128]{2,1,0:T(8,128)S(1)} %join_vectors.2.refs_5_), channel_id=1, source_target_pairs={{0,16},{8,24},{16,0},{24,8},{1,17},{9,25},{17,1},{25,9},{2,18},{10... | collective-permute-start | bytes 122888 | tf_op jit(solution)/shard_map/ppermute | solution.py:625
  19.9 3.7 %collective-permute-done.10.refs_6_ = f32[5,16,128]{2,1,0:T(8,128)S(1)} collective-permute-done((f32[5,16,128]{2,1,0:T(8,128)S(1)}, f32[5,16,128]{2,1,0:T(8,128)S(1)}, u32[]{:S(2)}, u32[]{:S(2)}) %collective-permute-start.10) | collective-permute-done | bytes 40992 | tf_op jit(solution)/shard_map/ppermute | solution.py:625
  23.6 0.8 %middle.1 = (f32[2,5,8,128]{3,2,1,0:T(8,128)S(1)}, f32[5,128,128]{2,1,0:T(8,128)S(1)}) custom-call(f32[75,16,128]{2,1,0:T(8,128)S(1)} %get-tuple-element.100.rest_0_, f32[75,16,128]{2,1,0:T(8,128)S(1)} %get-tuple-element.101.rest_1_, f32[2,5,16,128]{3,2,1,0:T(8,128)S(1)} %get-tuple-element.102.rest_2_, f32[2,5,16,128]{3,2,1,0:T(8,128)S(1)} %get-tuple-element.103.rest_3_, ...), custom_call_target="tpu_custom_call" | custom-call | tf_op jit(solution)/shard_map/middle/pallas_call | solution.py:31
  24.4 2.9 %collective-permute-start.13 = (f32[2,5,8,128]{3,2,1,0:T(8,128)S(1)}, f32[2,5,8,128]{3,2,1,0:T(8,128)S(1)}, u32[]{:S(2)}, u32[]{:S(2)}) collective-permute-start(f32[2,5,8,128]{3,2,1,0:T(8,128)S(1)} %get-tuple-element.113.refs_4_), channel_id=1, source_target_pairs={{0,3},{1,2},{2,1},{3,0},{4,7},{5,6},{6,5},{7,4},{8,11},{9,10},{10,... | collective-permute-start | bytes 122888 | tf_op jit(solution)/shard_map/ppermute | solution.py:625
  27.3 0.4 %collective-permute-start.12 = (f32[2,5,8,128]{3,2,1,0:T(8,128)S(1)}, f32[2,5,8,128]{3,2,1,0:T(8,128)S(1)}, u32[]{:S(2)}, u32[]{:S(2)}) collective-permute-start(f32[2,5,8,128]{3,2,1,0:T(8,128)S(1)} %get-tuple-element.113.refs_4_), channel_id=1, source_target_pairs={{0,2},{1,3},{2,0},{3,1},{4,6},{5,7},{6,4},{7,5},{8,10},{9,11},{10,... | collective-permute-start | bytes 122888 | tf_op jit(solution)/shard_map/ppermute | solution.py:625
  27.7 0.2 collective-permute-start.11
  27.9 2.9 %collective-permute-start.14 = (f32[13,8,128]{2,1,0:T(8,128)S(1)}, f32[13,8,128]{2,1,0:T(8,128)S(1)}, u32[]{:S(2)}, u32[]{:S(2)}) collective-permute-start(f32[13,8,128]{2,1,0:T(8,128)S(1)} %get-tuple-element.127), channel_id=1, source_target_pairs={{0,4},{1,5},{2,6},{3,7},{4,0},{5,1},{6,2},{7,3},{8,12},{9,13},{10,... | collective-permute-start | bytes 159752 | tf_op jit(solution)/shard_map/ppermute | solution.py:625
  30.9 0.7 %collective-permute-done.12.refs_6_ = f32[2,5,8,128]{3,2,1,0:T(8,128)S(1)} collective-permute-done((f32[2,5,8,128]{3,2,1,0:T(8,128)S(1)}, f32[2,5,8,128]{3,2,1,0:T(8,128)S(1)}, u32[]{:S(2)}, u32[]{:S(2)}) %collective-permute-start.12) | collective-permute-done | bytes 40992 | tf_op jit(solution)/shard_map/ppermute | solution.py:625
  31.8 2.7 %collective-permute-start.16 = (f32[5,8,128]{2,1,0:T(8,128)S(1)}, f32[5,8,128]{2,1,0:T(8,128)S(1)}, u32[]{:S(2)}, u32[]{:S(2)}) collective-permute-start(f32[5,8,128]{2,1,0:T(8,128)S(1)} %join_vectors.3.refs_10_), channel_id=1, source_target_pairs={{0,4},{1,5},{2,6},{3,7},{4,0},{5,1},{6,2},{7,3},{8,12},{9,13},{10,... | collective-permute-start | bytes 61448 | tf_op jit(solution)/shard_map/ppermute | solution.py:625
  34.5 2.0 %collective-permute-done.15.refs_9_ = f32[13,8,128]{2,1,0:T(8,128)S(1)} collective-permute-done((f32[13,8,128]{2,1,0:T(8,128)S(1)}, f32[13,8,128]{2,1,0:T(8,128)S(1)}, u32[]{:S(2)}, u32[]{:S(2)}) %collective-permute-start.15) | collective-permute-done | bytes 53280 | tf_op jit(solution)/shard_map/ppermute | solution.py:625
  36.5 0.2 collective-permute-done.16.refs_11_
  36.7 1.3 %end.1 = f32[5,128,128]{2,1,0:T(8,128)} custom-call(f32[75,8,128]{2,1,0:T(8,128)S(1)} %get-tuple-element.132.rest_0_, f32[75,8,128]{2,1,0:T(8,128)S(1)} %get-tuple-element.133.rest_1_, f32[75,8,128]{2,1,0:T(8,128)S(1)} %get-tuple-element.134.rest_2_, f32[75,8,128]{2,1,0:T(8,128)S(1)} %get-tuple-element.135.rest_3_, ...), custom_call_target="tpu_custom_call" | custom-call | tf_op jit(solution)/shard_map/end/pallas_call | solution.py:31
  (28 shorter events, 0.3 us)
Async XLA Ops:
  3.3 11.0 %collective-permute-start.3 = (f32[75,16,128]{2,1,0:T(8,128)S(1)}, f32[75,16,128]{2,1,0:T(8,128)S(1)}, u32[]{:S(2)}, u32[]{:S(2)}) collective-permute-start(f32[75,16,128]{2,1,0:T(8,128)S(1)} %get-tuple-element.79.refs_0_), channel_id=1, source_target_pairs={{0,8},{8,0},{16,24},{24,16},{1,9},{9,1},{17,25},{25,17},{2,10},{10... | collective-permute-start | bytes 1843208 | tf_op jit(solution)/shard_map/ppermute | solution.py:625
  3.8 12.3 %collective-permute-start.5 = (f32[5,6,16,128]{3,2,1,0:T(8,128)S(1)}, f32[5,6,16,128]{3,2,1,0:T(8,128)S(1)}, u32[]{:S(2)}, u32[]{:S(2)}) collective-permute-start(f32[5,6,16,128]{3,2,1,0:T(8,128)S(1)} %get-tuple-element.82), channel_id=1, source_target_pairs={{8,16},{24,0},{16,8},{0,24},{9,17},{25,1},{17,9},{1,25},{10,18},{2... | collective-permute-start | bytes 737288 | tf_op jit(solution)/shard_map/ppermute | solution.py:631
  6.4 7.2 %collective-permute-start.6 = (f32[5,2,8,128]{3,2,1,0:T(8,128)S(1)}, f32[5,2,8,128]{3,2,1,0:T(8,128)S(1)}, u32[]{:S(2)}, u32[]{:S(2)}) collective-permute-start(f32[5,2,8,128]{3,2,1,0:T(8,128)S(1)} %get-tuple-element.83), channel_id=1, source_target_pairs={{0,1},{1,0},{2,3},{3,2},{4,5},{5,4},{6,7},{7,6},{8,9},{9,8},{10,11... | collective-permute-start | bytes 122888 | tf_op jit(solution)/shard_map/ppermute | solution.py:625
  7.9 6.2 %collective-permute-start.7 = (f32[5,2,8,128]{3,2,1,0:T(8,128)S(1)}, f32[5,2,8,128]{3,2,1,0:T(8,128)S(1)}, u32[]{:S(2)}, u32[]{:S(2)}) collective-permute-start(f32[5,2,8,128]{3,2,1,0:T(8,128)S(1)} %get-tuple-element.84), channel_id=1, source_target_pairs={{1,2},{3,4},{5,6},{2,1},{4,3},{6,5},{0,8},{7,15},{9,10},{11,12},{1... | collective-permute-start | bytes 122888 | tf_op jit(solution)/shard_map/ppermute | solution.py:637
  7.9 8.2 %copy-start = (f32[5,5,8,16,128]{4,3,2,1,0:T(8,128)S(1)}, f32[5,5,8,16,128]{4,3,2,1,0:T(8,128)}, u32[]{:S(2)}) copy-start(f32[5,5,8,16,128]{4,3,2,1,0:T(8,128)} %inverse.1) | copy-start | bytes 4915204
  9.5 6.6 %copy-start.1 = (f32[5,8,16,128]{3,2,1,0:T(8,128)S(1)}, f32[5,8,16,128]{3,2,1,0:T(8,128)}, u32[]{:S(2)}) copy-start(f32[5,8,16,128]{3,2,1,0:T(8,128)} %forcing.1) | copy-start | bytes 983044
  9.5 18.2 %collective-permute-start.2 = (f32[75,8,128]{2,1,0:T(8,128)S(1)}, f32[75,8,128]{2,1,0:T(8,128)S(1)}, u32[]{:S(2)}, u32[]{:S(2)}) collective-permute-start(f32[75,8,128]{2,1,0:T(8,128)S(1)} %get-tuple-element.78._.refs_0_), channel_id=1, source_target_pairs={{0,3},{1,2},{2,1},{3,0},{4,7},{5,6},{6,5},{7,4},{8,11},{9,10},{10,... | collective-permute-start | bytes 921608 | tf_op jit(solution)/shard_map/ppermute | solution.py:625
  13.6 14.3 %collective-permute-start.1 = (f32[75,8,128]{2,1,0:T(8,128)S(1)}, f32[75,8,128]{2,1,0:T(8,128)S(1)}, u32[]{:S(2)}, u32[]{:S(2)}) collective-permute-start(f32[75,8,128]{2,1,0:T(8,128)S(1)} %get-tuple-element.78._.refs_0_), channel_id=1, source_target_pairs={{0,2},{1,3},{2,0},{3,1},{4,6},{5,7},{6,4},{7,5},{8,10},{9,11},{10,... | collective-permute-start | bytes 921608 | tf_op jit(solution)/shard_map/ppermute | solution.py:625
  14.1 13.9 %collective-permute-start = (f32[75,8,128]{2,1,0:T(8,128)S(1)}, f32[75,8,128]{2,1,0:T(8,128)S(1)}, u32[]{:S(2)}, u32[]{:S(2)}) collective-permute-start(f32[75,8,128]{2,1,0:T(8,128)S(1)} %get-tuple-element.78._.refs_0_), channel_id=1, source_target_pairs={{0,1},{1,0},{2,3},{3,2},{4,5},{5,4},{6,7},{7,6},{8,9},{9,8},{10,11... | collective-permute-start | bytes 921608 | tf_op jit(solution)/shard_map/ppermute | solution.py:625
  14.3 1.3 %collective-permute-start.4 = (f32[5,2,16,128]{3,2,1,0:T(8,128)S(1)}, f32[5,2,16,128]{3,2,1,0:T(8,128)S(1)}, u32[]{:S(2)}, u32[]{:S(2)}) collective-permute-start(f32[5,2,16,128]{3,2,1,0:T(8,128)S(1)} %get-tuple-element.81), channel_id=1, source_target_pairs={{0,8},{8,0},{16,24},{24,16},{1,9},{9,1},{17,25},{25,17},{2,10},{10... | collective-permute-start | bytes 245768 | tf_op jit(solution)/shard_map/ppermute | solution.py:625
  15.5 8.0 %collective-permute-start.9 = (f32[25,16,128]{2,1,0:T(8,128)S(1)}, f32[25,16,128]{2,1,0:T(8,128)S(1)}, u32[]{:S(2)}, u32[]{:S(2)}) collective-permute-start(f32[25,16,128]{2,1,0:T(8,128)S(1)} %join_matrices.2), channel_id=1, source_target_pairs={{0,16},{8,24},{16,0},{24,8},{1,17},{9,25},{17,1},{25,9},{2,18},{10... | collective-permute-start | bytes 614408 | tf_op jit(solution)/shard_map/ppermute | solution.py:625
  16.9 1.3 %collective-permute-start.8 = (f32[2,5,16,128]{3,2,1,0:T(8,128)S(1)}, f32[2,5,16,128]{3,2,1,0:T(8,128)S(1)}, u32[]{:S(2)}, u32[]{:S(2)}) collective-permute-start(f32[2,5,16,128]{3,2,1,0:T(8,128)S(1)} %get-tuple-element.87.refs_2_), channel_id=1, source_target_pairs={{0,8},{8,0},{16,24},{24,16},{1,9},{9,1},{17,25},{25,17},{2,10},{10... | collective-permute-start | bytes 245768 | tf_op jit(solution)/shard_map/ppermute | solution.py:625
  18.3 5.3 %collective-permute-start.10 = (f32[5,16,128]{2,1,0:T(8,128)S(1)}, f32[5,16,128]{2,1,0:T(8,128)S(1)}, u32[]{:S(2)}, u32[]{:S(2)}) collective-permute-start(f32[5,16,128]{2,1,0:T(8,128)S(1)} %join_vectors.2.refs_5_), channel_id=1, source_target_pairs={{0,16},{8,24},{16,0},{24,8},{1,17},{9,25},{17,1},{25,9},{2,18},{10... | collective-permute-start | bytes 122888 | tf_op jit(solution)/shard_map/ppermute | solution.py:625
  24.4 6.6 %collective-permute-start.13 = (f32[2,5,8,128]{3,2,1,0:T(8,128)S(1)}, f32[2,5,8,128]{3,2,1,0:T(8,128)S(1)}, u32[]{:S(2)}, u32[]{:S(2)}) collective-permute-start(f32[2,5,8,128]{3,2,1,0:T(8,128)S(1)} %get-tuple-element.113.refs_4_), channel_id=1, source_target_pairs={{0,3},{1,2},{2,1},{3,0},{4,7},{5,6},{6,5},{7,4},{8,11},{9,10},{10,... | collective-permute-start | bytes 122888 | tf_op jit(solution)/shard_map/ppermute | solution.py:625
  27.3 4.4 %collective-permute-start.12 = (f32[2,5,8,128]{3,2,1,0:T(8,128)S(1)}, f32[2,5,8,128]{3,2,1,0:T(8,128)S(1)}, u32[]{:S(2)}, u32[]{:S(2)}) collective-permute-start(f32[2,5,8,128]{3,2,1,0:T(8,128)S(1)} %get-tuple-element.113.refs_4_), channel_id=1, source_target_pairs={{0,2},{1,3},{2,0},{3,1},{4,6},{5,7},{6,4},{7,5},{8,10},{9,11},{10,... | collective-permute-start | bytes 122888 | tf_op jit(solution)/shard_map/ppermute | solution.py:625
  27.7 4.0 %collective-permute-start.11 = (f32[2,5,8,128]{3,2,1,0:T(8,128)S(1)}, f32[2,5,8,128]{3,2,1,0:T(8,128)S(1)}, u32[]{:S(2)}, u32[]{:S(2)}) collective-permute-start(f32[2,5,8,128]{3,2,1,0:T(8,128)S(1)} %get-tuple-element.113.refs_4_), channel_id=1, source_target_pairs={{0,1},{1,0},{2,3},{3,2},{4,5},{5,4},{6,7},{7,6},{8,9},{9,8},{10,11... | collective-permute-start | bytes 122888 | tf_op jit(solution)/shard_map/ppermute | solution.py:625
  27.9 6.5 %collective-permute-start.14 = (f32[13,8,128]{2,1,0:T(8,128)S(1)}, f32[13,8,128]{2,1,0:T(8,128)S(1)}, u32[]{:S(2)}, u32[]{:S(2)}) collective-permute-start(f32[13,8,128]{2,1,0:T(8,128)S(1)} %get-tuple-element.127), channel_id=1, source_target_pairs={{0,4},{1,5},{2,6},{3,7},{4,0},{5,1},{6,2},{7,3},{8,12},{9,13},{10,... | collective-permute-start | bytes 159752 | tf_op jit(solution)/shard_map/ppermute | solution.py:625
  30.9 5.6 %collective-permute-start.15 = (f32[13,8,128]{2,1,0:T(8,128)S(1)}, f32[13,8,128]{2,1,0:T(8,128)S(1)}, u32[]{:S(2)}, u32[]{:S(2)}) collective-permute-start(f32[13,8,128]{2,1,0:T(8,128)S(1)} %get-tuple-element.128), channel_id=1, source_target_pairs={{0,4},{1,5},{2,6},{3,7},{4,0},{5,1},{6,2},{7,3},{8,12},{9,13},{10,... | collective-permute-start | bytes 159752 | tf_op jit(solution)/shard_map/ppermute | solution.py:625
  31.8 4.9 %collective-permute-start.16 = (f32[5,8,128]{2,1,0:T(8,128)S(1)}, f32[5,8,128]{2,1,0:T(8,128)S(1)}, u32[]{:S(2)}, u32[]{:S(2)}) collective-permute-start(f32[5,8,128]{2,1,0:T(8,128)S(1)} %join_vectors.3.refs_10_), channel_id=1, source_target_pairs={{0,4},{1,5},{2,6},{3,7},{4,0},{5,1},{6,2},{7,3},{8,12},{9,13},{10,... | collective-permute-start | bytes 61448 | tf_op jit(solution)/shard_map/ppermute | solution.py:625

commit v7 on v6

--- a/solution.py
+++ b/solution.py
@@ -106,16 +106,19 @@
     emit(0, signed(last, length))
 
 
-def compose_backward(length, upper_at, load_p, emit):
+def compose_backward(length, upper_at, load_p, emit, keep=lambda i, w, r: None):
     def backward(k, carried):
         w, r = carried
         i = length - 1 - k
         here = whole(lambda a, b: upper_at(i, a, b))
         at = lambda a, b: here[NVAR * a + b]
-        return tuple(plus(load_p(i), matmat(at, w))), tuple(matmat(at, r))
+        w, r = tuple(plus(load_p(i), matmat(at, w))), tuple(matmat(at, r))
+        keep(i, w, r)
+        return w, r
 
     w = tuple(load_p(length - 1))
     r = tuple(whole(lambda a, b: upper_at(length - 1, a, b)))
+    keep(length - 1, w, r)
     w, r = lax.fori_loop(1, length, backward, (w, r), unroll=UNROLL)
     emit(1, signed(r, length))
     emit(2, [-q for q in w])
@@ -173,6 +176,23 @@
         cells_y, at(upper), lambda i: [held[i, k] for k in range(NVAR * NVAR)], emit
     )
     load.wait()
+
+
+def responses_kernel(lower, upper, _, from_f, from_b, held):
+    def store_p(i, p):
+        for k in range(NVAR * NVAR):
+            held[i, k] = p[k]
+
+    def keep(j, w, r):
+        for k in range(NVAR * NVAR):
+            from_f[j, k] = w[k]
+            from_b[j, k] = r[k]
+
+    at = lambda ref: lambda j, a, b: ref[NVAR * a + b, j]
+    load_p = lambda i: [held[i, k] for k in range(NVAR * NVAR)]
+    nothing = lambda which, matrix: None
+    compose_forward(lower.shape[1], at(lower), store_p, nothing)
+    compose_backward(lower.shape[1], at(upper), load_p, nothing, keep)
 
 
 def local_x_kernel(
@@ -528,7 +548,7 @@
 
 def middle_kernel(radices, *rest):
     (source, x_lower, x_upper, y_inverse, y_lower, y_upper,
-     reduced, y_source, f_ref, b_ref, held) = rest[descend_count("px", radices) :]
+     reduced, y_cells, f_ref, b_ref, held, y_source) = rest[descend_count("px", radices) :]
     cells, rows = source.shape[1:3]
     descend("px", radices, rest, f_ref, b_ref)
 
@@ -571,7 +591,10 @@
         j = rows - 1 - k
         product = matvec(lambda a, b: y_upper[NVAR * a + b, j], list(w))
         here = pl.ds(pl.multiple_of(j * cells, cells), cells)
-        return tuple(held[c, here] - product[c] for c in range(NVAR))
+        w = [held[c, here] - product[c] for c in range(NVAR)]
+        for c in range(NVAR):
+            y_cells[c, here] = w[c]
+        return tuple(w)
 
     w = lax.fori_loop(0, rows, y_backward, (zero,) * NVAR, unroll=True)
     for c in range(NVAR):
@@ -581,31 +604,18 @@
 
 def end_kernel(radices, cells, rows, *rest):
     first = descend_count("py", radices)
-    y_source, y_lower, y_upper, out, f_ref, b_ref, held = rest[first:]
+    y_cells, from_f, from_b, out, f_ref, b_ref = rest[first:]
     descend("py", radices, rest, f_ref, b_ref)
-
-    def line(j):
-        return pl.ds(j, cells, stride=rows)
-
-    def forward(j, v):
-        product = matvec(lambda a, b: y_lower[NVAR * a + b, j], list(v))
-        v = [y_source[c, line(j), :] - product[c] for c in range(NVAR)]
-        for c in range(NVAR):
-            held[c, pl.ds(pl.multiple_of(j * cells, cells), cells)] = v[c]
-        return tuple(v)
-
-    lax.fori_loop(0, rows, forward, tuple(f_ref[k] for k in range(NVAR)), unroll=True)
-
-    def backward(k, w):
-        j = rows - 1 - k
-        here = pl.ds(pl.multiple_of(j * cells, cells), cells)
-        product = matvec(lambda a, b: y_upper[NVAR * a + b, j], list(w))
-        w = [held[c, here] - product[c] for c in range(NVAR)]
-        for c in range(NVAR):
-            out[c, line(j), :] = w[c]
-        return tuple(w)
-
-    lax.fori_loop(0, rows, backward, tuple(b_ref[k] for k in range(NVAR)), unroll=True)
+    f = [f_ref[k] for k in range(NVAR)]
+    b = [b_ref[k] for k in range(NVAR)]
+    for j in range(rows):
+        forward = matvec(lambda a, c: from_f[j, NVAR * a + c], f)
+        backward = matvec(lambda a, c: from_b[j, NVAR * a + c], b)
+        for c in range(NVAR):
+            value = y_cells[c, j * cells : (j + 1) * cells]
+            value = value + forward[c] if j % 2 else value - forward[c]
+            value = value - backward[c] if (rows - j) % 2 else value + backward[c]
+            out[c, pl.ds(j, cells, stride=rows), :] = value
 
 
 def radices_of(count):
@@ -655,7 +665,7 @@
     y_pair, x_pair = swap(y_pair, "py", 1), swap(x_pair, "px", 1)
     halos = (x_pair, x_cross, y_pair, y_cross)
 
-    def exchange(axis, radices, own_m, got_m, own_v, rest):
+    def exchange(axis, radices, own_m, got_m, own_v, rest, late=None):
         operands, level = [], 0
         for t, radix in enumerate(radices[:-1]):
             last = t == len(radices) - 2
@@ -679,6 +689,7 @@
                 next_got = hold(next_got, own_v)
             own_m, got_m, level = next_m[0], next_got, next_level
         operands += [*got_m, own_v, swap(own_v, axis, 1 << level)]
+        rest = late(own_v, rest) if late else rest
         held = hold(operands + rest)
         return held[: len(operands)], held[len(operands) :]
 
@@ -696,21 +707,27 @@
     x_got = [swap(x_m, "px", k) for k in range(1, x_radices[0])]
     rest = [source, x_lower, x_upper, y_inverse, y_lower, y_upper]
     operands, rest = exchange("px", x_radices, x_m, x_got, reduced, rest)
-    reduced, source = call(
+    reduced, y_cells = call(
         functools.partial(middle_kernel, x_radices), "middle",
         [(2, NVAR, cells, lanes), (NVAR, cells * rows, lanes)],
         operands + rest,
-        [(NVAR, rows, lanes), (NVAR, rows, lanes), (NVAR, cells * rows, lanes)],
+        [(NVAR, rows, lanes), (NVAR, rows, lanes), (NVAR, cells * rows, lanes),
+         (NVAR, cells * rows, lanes)],
     )
+    def responses(own_v, rest):
+        kept = call(responses_kernel, "responses", [(rows, every, cells, lanes)] * 2,
+                    [*rest[1:], own_v], [(rows, every, cells, lanes)])
+        return [rest[0], *kept]
+
     y_m, *y_got = hold([y_m, *y_got], reduced)
     operands, rest = exchange(
-        "py", y_radices, y_m, y_got, reduced, [source, *rest[-2:]]
+        "py", y_radices, y_m, y_got, reduced, [y_cells, *rest[-2:]], responses
     )
     out = call(
         functools.partial(end_kernel, y_radices, cells, rows), "end",
         [(NVAR, cells * rows, lanes)],
         operands + rest,
-        [(NVAR, cells, lanes), (NVAR, cells, lanes), (NVAR, cells * rows, lanes)],
+        [(NVAR, cells, lanes), (NVAR, cells, lanes)],
         result_in_hbm=True,
     )
     return out.reshape(NVAR, cells, rows, lanes)

time: 38.2 us -> 37.9 us (level)
  waiting for transfers between devices: 9.25 us -> 7.42 us
  Pallas kernels: 7.84 us -> 9.44 us
    ppermute x15, waiting for transfers between devices: 9.25 us -> 7.41 us  [swap(): return lax.ppermute(value, axis, pairs)]
    pallas_call x9 -> x10, Pallas kernels: 7.84 us -> 9.44 us  [call(): pl.pallas_call(kernel, name=name, out_shape=shapes[0] if single else shap...]
  transfers between devices with their start and end apart: 17 -> 17, of which waited for: 7 -> 7; matrix products, arithmetic and copies ran while one was open for 0% -> 0% of each run, Pallas kernels for 9% -> 13%
where the time goes in v7:
time: 37.9 us; the launch traced here: 37.8 us
  starting transfers between devices  20.8 us (55%)
  Pallas kernels  9.44 us (25%)
  waiting for transfers between devices  7.42 us (20%)
    ppermute x15, starting transfers between devices, swap(): return lax.ppermute(value, axis, pairs)  18.2 us
    pallas_call x10, Pallas kernels, call(): pl.pallas_call(kernel, name=name, out_shape=shapes[0] if single else shap...  9.44 us
    ppermute x15, waiting for transfers between devices, swap(): return lax.ppermute(value, axis, pairs)  7.41 us
    ppermute x1, starting transfers between devices, across(): return lax.ppermute(value, axis, pairs + [(j, i) for i, j in pairs])  2.61 us
  transfers between devices with their start and end apart: 17, of which 7 were waited for; matrix products, arithmetic and copies ran while one was open for 0% of the time, Pallas kernels for 13%

profile of v7, /device:TPU:0, one launch (start us, length us, event | category | flops | bytes accessed | tf_op | source)
XLA Modules:
  0.0 37.8 jit_solution(1291216360641396834)
XLA Ops:
  0.0 3.2 %begin.1 = (f32[5,2,8,128]{3,2,1,0:T(8,128)S(1)}, f32[5,2,8,128]{3,2,1,0:T(8,128)S(1)}, f32[5,2,16,128]{3,2,1,0:T(8,128)S(1)}, f32[5,6,16,128]{3,2,1,0:T(8,128)S...) custom-call(f32[5,128,128]{2,1,0:T(8,128)} %bitcast.10, ...), custom_call_target="tpu_custom_call" | custom-call | tf_op jit(solution)/shard_map/begin/pallas_call | solution.py:31
  3.3 0.5 %collective-permute-start.3 = (f32[75,16,128]{2,1,0:T(8,128)S(1)}, f32[75,16,128]{2,1,0:T(8,128)S(1)}, u32[]{:S(2)}, u32[]{:S(2)}) collective-permute-start(f32[75,16,128]{2,1,0:T(8,128)S(1)} %get-tuple-element.81.refs_0_), channel_id=1, source_target_pairs={{0,8},{8,0},{16,24},{24,16},{1,9},{9,1},{17,25},{25,17},{2,10},{10... | collective-permute-start | bytes 1843208 | tf_op jit(solution)/shard_map/ppermute | solution.py:635
  3.8 2.6 %collective-permute-start.5 = (f32[5,6,16,128]{3,2,1,0:T(8,128)S(1)}, f32[5,6,16,128]{3,2,1,0:T(8,128)S(1)}, u32[]{:S(2)}, u32[]{:S(2)}) collective-permute-start(f32[5,6,16,128]{3,2,1,0:T(8,128)S(1)} %get-tuple-element.84), channel_id=1, source_target_pairs={{8,16},{24,0},{16,8},{0,24},{9,17},{25,1},{17,9},{1,25},{10,18},{2... | collective-permute-start | bytes 737288 | tf_op jit(solution)/shard_map/ppermute | solution.py:641
  6.4 1.5 %collective-permute-start.6 = (f32[5,2,8,128]{3,2,1,0:T(8,128)S(1)}, f32[5,2,8,128]{3,2,1,0:T(8,128)S(1)}, u32[]{:S(2)}, u32[]{:S(2)}) collective-permute-start(f32[5,2,8,128]{3,2,1,0:T(8,128)S(1)} %get-tuple-element.85), channel_id=1, source_target_pairs={{0,1},{1,0},{2,3},{3,2},{4,5},{5,4},{6,7},{7,6},{8,9},{9,8},{10,11... | collective-permute-start | bytes 122888 | tf_op jit(solution)/shard_map/ppermute | solution.py:635
  7.9 1.6 %compose_y.1 = (f32[75,8,128]{2,1,0:T(8,128)S(1)}, f32[5,5,128,128]{3,2,1,0:T(8,128)S(1)}) custom-call(f32[25,16,8,128]{3,2,1,0:T(8,128)S(1)} %get-tuple-element.78.lower.refs_8_, f32[25,16,8,128]{3,2,1,0:T(8,128)S(1)} %get-tuple-element.79.upper.refs_9_, f32[5,5,128,128]{3,2,1,0:T(8,128)} %bitcast.7), custom_call_target="tpu_custom_call" | custom-call | tf_op jit(solution)/shard_map/compose_y/pallas_call | solution.py:31
  9.5 4.1 %collective-permute-start.2 = (f32[75,8,128]{2,1,0:T(8,128)S(1)}, f32[75,8,128]{2,1,0:T(8,128)S(1)}, u32[]{:S(2)}, u32[]{:S(2)}) collective-permute-start(f32[75,8,128]{2,1,0:T(8,128)S(1)} %get-tuple-element.80._.refs_0_), channel_id=1, source_target_pairs={{0,3},{1,2},{2,1},{3,0},{4,7},{5,6},{6,5},{7,4},{8,11},{9,10},{10,... | collective-permute-start | bytes 921608 | tf_op jit(solution)/shard_map/ppermute | solution.py:635
  13.6 0.5 %collective-permute-start.1 = (f32[75,8,128]{2,1,0:T(8,128)S(1)}, f32[75,8,128]{2,1,0:T(8,128)S(1)}, u32[]{:S(2)}, u32[]{:S(2)}) collective-permute-start(f32[75,8,128]{2,1,0:T(8,128)S(1)} %get-tuple-element.80._.refs_0_), channel_id=1, source_target_pairs={{0,2},{1,3},{2,0},{3,1},{4,6},{5,7},{6,4},{7,5},{8,10},{9,11},{10,... | collective-permute-start | bytes 921608 | tf_op jit(solution)/shard_map/ppermute | solution.py:635
  14.1 0.2 collective-permute-start
  14.3 1.3 %collective-permute-done.4.x_pair = f32[5,2,16,128]{3,2,1,0:T(8,128)S(1)} collective-permute-done((f32[5,2,16,128]{3,2,1,0:T(8,128)S(1)}, f32[5,2,16,128]{3,2,1,0:T(8,128)S(1)}, u32[]{:S(2)}, u32[]{:S(2)}) %collective-permute-start.4) | collective-permute-done | bytes 81952 | tf_op jit(solution)/shard_map/ppermute | solution.py:635
  15.5 0.5 %collective-permute-start.9 = (f32[25,16,128]{2,1,0:T(8,128)S(1)}, f32[25,16,128]{2,1,0:T(8,128)S(1)}, u32[]{:S(2)}, u32[]{:S(2)}) collective-permute-start(f32[25,16,128]{2,1,0:T(8,128)S(1)} %join_matrices.2), channel_id=1, source_target_pairs={{0,16},{8,24},{16,0},{24,8},{1,17},{9,25},{17,1},{25,9},{2,18},{10... | collective-permute-start | bytes 614408 | tf_op jit(solution)/shard_map/ppermute | solution.py:635
  16.1 0.8 %local_x.1 = (f32[2,5,16,128]{3,2,1,0:T(8,128)S(1)}, f32[5,8,16,128]{3,2,1,0:T(8,128)S(1)}) custom-call(f32[5,8,16,128]{3,2,1,0:T(8,128)S(1)} %bitcast.6, f32[5,8,16,128]{3,2,1,0:T(8,128)S(1)} %copy-done.1, f32[5,2,16,128]{3,2,1,0:T(8,128)S(1)} %collective-permute-done.4.x_pair, f32[5,6,16,128]{3,2,1,0:T(8,128)S(1)} %collective-permute-done.5.x_cross, ...), custom_call_target="tpu_custom_call" | custom-call | tf_op jit(solution)/shard_map/local_x/pallas_call | solution.py:31
  17.0 1.3 %collective-permute-done.8.refs_3_ = f32[2,5,16,128]{3,2,1,0:T(8,128)S(1)} collective-permute-done((f32[2,5,16,128]{3,2,1,0:T(8,128)S(1)}, f32[2,5,16,128]{3,2,1,0:T(8,128)S(1)}, u32[]{:S(2)}, u32[]{:S(2)}) %collective-permute-start.8) | collective-permute-done | bytes 81952 | tf_op jit(solution)/shard_map/ppermute | solution.py:635
  18.3 1.6 %collective-permute-start.10 = (f32[5,16,128]{2,1,0:T(8,128)S(1)}, f32[5,16,128]{2,1,0:T(8,128)S(1)}, u32[]{:S(2)}, u32[]{:S(2)}) collective-permute-start(f32[5,16,128]{2,1,0:T(8,128)S(1)} %join_vectors.2.refs_5_), channel_id=1, source_target_pairs={{0,16},{8,24},{16,0},{24,8},{1,17},{9,25},{17,1},{25,9},{2,18},{10... | collective-permute-start | bytes 122888 | tf_op jit(solution)/shard_map/ppermute | solution.py:635
  19.9 3.7 %collective-permute-done.10.refs_6_ = f32[5,16,128]{2,1,0:T(8,128)S(1)} collective-permute-done((f32[5,16,128]{2,1,0:T(8,128)S(1)}, f32[5,16,128]{2,1,0:T(8,128)S(1)}, u32[]{:S(2)}, u32[]{:S(2)}) %collective-permute-start.10) | collective-permute-done | bytes 40992 | tf_op jit(solution)/shard_map/ppermute | solution.py:635
  23.6 0.8 %middle.1 = (f32[2,5,8,128]{3,2,1,0:T(8,128)S(1)}, f32[5,128,128]{2,1,0:T(8,128)S(1)}) custom-call(f32[75,16,128]{2,1,0:T(8,128)S(1)} %get-tuple-element.102.rest_0_, f32[75,16,128]{2,1,0:T(8,128)S(1)} %get-tuple-element.103.rest_1_, f32[2,5,16,128]{3,2,1,0:T(8,128)S(1)} %get-tuple-element.104.rest_2_, f32[2,5,16,128]{3,2,1,0:T(8,128)S(1)} %get-tuple-element.105.rest_3_, ...), custom_call_target="tpu_custom_call" | custom-call | tf_op jit(solution)/shard_map/middle/pallas_call | solution.py:31
  24.4 2.9 %collective-permute-start.13 = (f32[2,5,8,128]{3,2,1,0:T(8,128)S(1)}, f32[2,5,8,128]{3,2,1,0:T(8,128)S(1)}, u32[]{:S(2)}, u32[]{:S(2)}) collective-permute-start(f32[2,5,8,128]{3,2,1,0:T(8,128)S(1)} %get-tuple-element.115.refs_4_), channel_id=1, source_target_pairs={{0,3},{1,2},{2,1},{3,0},{4,7},{5,6},{6,5},{7,4},{8,11},{9,10},{10,... | collective-permute-start | bytes 122888 | tf_op jit(solution)/shard_map/ppermute | solution.py:635
  27.3 0.4 %collective-permute-start.12 = (f32[2,5,8,128]{3,2,1,0:T(8,128)S(1)}, f32[2,5,8,128]{3,2,1,0:T(8,128)S(1)}, u32[]{:S(2)}, u32[]{:S(2)}) collective-permute-start(f32[2,5,8,128]{3,2,1,0:T(8,128)S(1)} %get-tuple-element.115.refs_4_), channel_id=1, source_target_pairs={{0,2},{1,3},{2,0},{3,1},{4,6},{5,7},{6,4},{7,5},{8,10},{9,11},{10,... | collective-permute-start | bytes 122888 | tf_op jit(solution)/shard_map/ppermute | solution.py:635
  27.7 0.2 collective-permute-start.11
  27.9 2.9 %collective-permute-start.14 = (f32[13,8,128]{2,1,0:T(8,128)S(1)}, f32[13,8,128]{2,1,0:T(8,128)S(1)}, u32[]{:S(2)}, u32[]{:S(2)}) collective-permute-start(f32[13,8,128]{2,1,0:T(8,128)S(1)} %get-tuple-element.129), channel_id=1, source_target_pairs={{0,4},{1,5},{2,6},{3,7},{4,0},{5,1},{6,2},{7,3},{8,12},{9,13},{10,... | collective-permute-start | bytes 159752 | tf_op jit(solution)/shard_map/ppermute | solution.py:635
  30.9 0.7 %collective-permute-done.12.refs_6_ = f32[2,5,8,128]{3,2,1,0:T(8,128)S(1)} collective-permute-done((f32[2,5,8,128]{3,2,1,0:T(8,128)S(1)}, f32[2,5,8,128]{3,2,1,0:T(8,128)S(1)}, u32[]{:S(2)}, u32[]{:S(2)}) %collective-permute-start.12) | collective-permute-done | bytes 40992 | tf_op jit(solution)/shard_map/ppermute | solution.py:635
  31.8 2.7 %collective-permute-start.16 = (f32[5,8,128]{2,1,0:T(8,128)S(1)}, f32[5,8,128]{2,1,0:T(8,128)S(1)}, u32[]{:S(2)}, u32[]{:S(2)}) collective-permute-start(f32[5,8,128]{2,1,0:T(8,128)S(1)} %join_vectors.3._.refs_10_), channel_id=1, source_target_pairs={{0,4},{1,5},{2,6},{3,7},{4,0},{5,1},{6,2},{7,3},{8,12},{9,13},{10,... | collective-permute-start | bytes 61448 | tf_op jit(solution)/shard_map/ppermute | solution.py:635
  34.5 1.8 %responses.1 = (f32[16,25,8,128]{3,2,1,0:T(8,128)S(1)}, f32[16,25,8,128]{3,2,1,0:T(8,128)S(1)}) custom-call(f32[25,16,8,128]{3,2,1,0:T(8,128)S(1)} %get-tuple-element.132.lower, f32[25,16,8,128]{3,2,1,0:T(8,128)S(1)} %get-tuple-element.133.upper, f32[5,8,128]{2,1,0:T(8,128)S(1)} %join_vectors.3._.refs_10_), custom_call_target="tpu_custom_call" | custom-call | tf_op jit(solution)/shard_map/responses/pallas_call | solution.py:31
  36.4 0.2 collective-permute-done.16.refs_11_
  36.7 1.1 %end.1 = f32[5,128,128]{2,1,0:T(8,128)} custom-call(f32[75,8,128]{2,1,0:T(8,128)S(1)} %get-tuple-element.136.rest_0_, f32[75,8,128]{2,1,0:T(8,128)S(1)} %get-tuple-element.137.rest_1_, f32[75,8,128]{2,1,0:T(8,128)S(1)} %get-tuple-element.138.rest_2_, f32[75,8,128]{2,1,0:T(8,128)S(1)} %get-tuple-element.139.rest_3_, ...), custom_call_target="tpu_custom_call" | custom-call | tf_op jit(solution)/shard_map/end/pallas_call | solution.py:31
  (29 shorter events, 0.5 us)
Async XLA Ops:
  3.3 11.0 %collective-permute-start.3 = (f32[75,16,128]{2,1,0:T(8,128)S(1)}, f32[75,16,128]{2,1,0:T(8,128)S(1)}, u32[]{:S(2)}, u32[]{:S(2)}) collective-permute-start(f32[75,16,128]{2,1,0:T(8,128)S(1)} %get-tuple-element.81.refs_0_), channel_id=1, source_target_pairs={{0,8},{8,0},{16,24},{24,16},{1,9},{9,1},{17,25},{25,17},{2,10},{10... | collective-permute-start | bytes 1843208 | tf_op jit(solution)/shard_map/ppermute | solution.py:635
  3.8 12.3 %collective-permute-start.5 = (f32[5,6,16,128]{3,2,1,0:T(8,128)S(1)}, f32[5,6,16,128]{3,2,1,0:T(8,128)S(1)}, u32[]{:S(2)}, u32[]{:S(2)}) collective-permute-start(f32[5,6,16,128]{3,2,1,0:T(8,128)S(1)} %get-tuple-element.84), channel_id=1, source_target_pairs={{8,16},{24,0},{16,8},{0,24},{9,17},{25,1},{17,9},{1,25},{10,18},{2... | collective-permute-start | bytes 737288 | tf_op jit(solution)/shard_map/ppermute | solution.py:641
  6.4 7.2 %collective-permute-start.6 = (f32[5,2,8,128]{3,2,1,0:T(8,128)S(1)}, f32[5,2,8,128]{3,2,1,0:T(8,128)S(1)}, u32[]{:S(2)}, u32[]{:S(2)}) collective-permute-start(f32[5,2,8,128]{3,2,1,0:T(8,128)S(1)} %get-tuple-element.85), channel_id=1, source_target_pairs={{0,1},{1,0},{2,3},{3,2},{4,5},{5,4},{6,7},{7,6},{8,9},{9,8},{10,11... | collective-permute-start | bytes 122888 | tf_op jit(solution)/shard_map/ppermute | solution.py:635
  7.9 6.2 %collective-permute-start.7 = (f32[5,2,8,128]{3,2,1,0:T(8,128)S(1)}, f32[5,2,8,128]{3,2,1,0:T(8,128)S(1)}, u32[]{:S(2)}, u32[]{:S(2)}) collective-permute-start(f32[5,2,8,128]{3,2,1,0:T(8,128)S(1)} %get-tuple-element.86), channel_id=1, source_target_pairs={{1,2},{3,4},{5,6},{2,1},{4,3},{6,5},{0,8},{7,15},{9,10},{11,12},{1... | collective-permute-start | bytes 122888 | tf_op jit(solution)/shard_map/ppermute | solution.py:647
  7.9 8.2 %copy-start = (f32[5,5,8,16,128]{4,3,2,1,0:T(8,128)S(1)}, f32[5,5,8,16,128]{4,3,2,1,0:T(8,128)}, u32[]{:S(2)}) copy-start(f32[5,5,8,16,128]{4,3,2,1,0:T(8,128)} %inverse.1) | copy-start | bytes 4915204
  9.5 6.6 %copy-start.1 = (f32[5,8,16,128]{3,2,1,0:T(8,128)S(1)}, f32[5,8,16,128]{3,2,1,0:T(8,128)}, u32[]{:S(2)}) copy-start(f32[5,8,16,128]{3,2,1,0:T(8,128)} %forcing.1) | copy-start | bytes 983044
  9.5 18.2 %collective-permute-start.2 = (f32[75,8,128]{2,1,0:T(8,128)S(1)}, f32[75,8,128]{2,1,0:T(8,128)S(1)}, u32[]{:S(2)}, u32[]{:S(2)}) collective-permute-start(f32[75,8,128]{2,1,0:T(8,128)S(1)} %get-tuple-element.80._.refs_0_), channel_id=1, source_target_pairs={{0,3},{1,2},{2,1},{3,0},{4,7},{5,6},{6,5},{7,4},{8,11},{9,10},{10,... | collective-permute-start | bytes 921608 | tf_op jit(solution)/shard_map/ppermute | solution.py:635
  13.6 14.3 %collective-permute-start.1 = (f32[75,8,128]{2,1,0:T(8,128)S(1)}, f32[75,8,128]{2,1,0:T(8,128)S(1)}, u32[]{:S(2)}, u32[]{:S(2)}) collective-permute-start(f32[75,8,128]{2,1,0:T(8,128)S(1)} %get-tuple-element.80._.refs_0_), channel_id=1, source_target_pairs={{0,2},{1,3},{2,0},{3,1},{4,6},{5,7},{6,4},{7,5},{8,10},{9,11},{10,... | collective-permute-start | bytes 921608 | tf_op jit(solution)/shard_map/ppermute | solution.py:635
  14.1 13.9 %collective-permute-start = (f32[75,8,128]{2,1,0:T(8,128)S(1)}, f32[75,8,128]{2,1,0:T(8,128)S(1)}, u32[]{:S(2)}, u32[]{:S(2)}) collective-permute-start(f32[75,8,128]{2,1,0:T(8,128)S(1)} %get-tuple-element.80._.refs_0_), channel_id=1, source_target_pairs={{0,1},{1,0},{2,3},{3,2},{4,5},{5,4},{6,7},{7,6},{8,9},{9,8},{10,11... | collective-permute-start | bytes 921608 | tf_op jit(solution)/shard_map/ppermute | solution.py:635
  14.3 1.3 %collective-permute-start.4 = (f32[5,2,16,128]{3,2,1,0:T(8,128)S(1)}, f32[5,2,16,128]{3,2,1,0:T(8,128)S(1)}, u32[]{:S(2)}, u32[]{:S(2)}) collective-permute-start(f32[5,2,16,128]{3,2,1,0:T(8,128)S(1)} %get-tuple-element.83), channel_id=1, source_target_pairs={{0,8},{8,0},{16,24},{24,16},{1,9},{9,1},{17,25},{25,17},{2,10},{10... | collective-permute-start | bytes 245768 | tf_op jit(solution)/shard_map/ppermute | solution.py:635
  15.5 8.0 %collective-permute-start.9 = (f32[25,16,128]{2,1,0:T(8,128)S(1)}, f32[25,16,128]{2,1,0:T(8,128)S(1)}, u32[]{:S(2)}, u32[]{:S(2)}) collective-permute-start(f32[25,16,128]{2,1,0:T(8,128)S(1)} %join_matrices.2), channel_id=1, source_target_pairs={{0,16},{8,24},{16,0},{24,8},{1,17},{9,25},{17,1},{25,9},{2,18},{10... | collective-permute-start | bytes 614408 | tf_op jit(solution)/shard_map/ppermute | solution.py:635
  16.9 1.3 %collective-permute-start.8 = (f32[2,5,16,128]{3,2,1,0:T(8,128)S(1)}, f32[2,5,16,128]{3,2,1,0:T(8,128)S(1)}, u32[]{:S(2)}, u32[]{:S(2)}) collective-permute-start(f32[2,5,16,128]{3,2,1,0:T(8,128)S(1)} %get-tuple-element.89.refs_2_), channel_id=1, source_target_pairs={{0,8},{8,0},{16,24},{24,16},{1,9},{9,1},{17,25},{25,17},{2,10},{10... | collective-permute-start | bytes 245768 | tf_op jit(solution)/shard_map/ppermute | solution.py:635
  18.3 5.3 %collective-permute-start.10 = (f32[5,16,128]{2,1,0:T(8,128)S(1)}, f32[5,16,128]{2,1,0:T(8,128)S(1)}, u32[]{:S(2)}, u32[]{:S(2)}) collective-permute-start(f32[5,16,128]{2,1,0:T(8,128)S(1)} %join_vectors.2.refs_5_), channel_id=1, source_target_pairs={{0,16},{8,24},{16,0},{24,8},{1,17},{9,25},{17,1},{25,9},{2,18},{10... | collective-permute-start | bytes 122888 | tf_op jit(solution)/shard_map/ppermute | solution.py:635
  24.4 6.6 %collective-permute-start.13 = (f32[2,5,8,128]{3,2,1,0:T(8,128)S(1)}, f32[2,5,8,128]{3,2,1,0:T(8,128)S(1)}, u32[]{:S(2)}, u32[]{:S(2)}) collective-permute-start(f32[2,5,8,128]{3,2,1,0:T(8,128)S(1)} %get-tuple-element.115.refs_4_), channel_id=1, source_target_pairs={{0,3},{1,2},{2,1},{3,0},{4,7},{5,6},{6,5},{7,4},{8,11},{9,10},{10,... | collective-permute-start | bytes 122888 | tf_op jit(solution)/shard_map/ppermute | solution.py:635
  27.3 4.4 %collective-permute-start.12 = (f32[2,5,8,128]{3,2,1,0:T(8,128)S(1)}, f32[2,5,8,128]{3,2,1,0:T(8,128)S(1)}, u32[]{:S(2)}, u32[]{:S(2)}) collective-permute-start(f32[2,5,8,128]{3,2,1,0:T(8,128)S(1)} %get-tuple-element.115.refs_4_), channel_id=1, source_target_pairs={{0,2},{1,3},{2,0},{3,1},{4,6},{5,7},{6,4},{7,5},{8,10},{9,11},{10,... | collective-permute-start | bytes 122888 | tf_op jit(solution)/shard_map/ppermute | solution.py:635
  27.7 4.0 %collective-permute-start.11 = (f32[2,5,8,128]{3,2,1,0:T(8,128)S(1)}, f32[2,5,8,128]{3,2,1,0:T(8,128)S(1)}, u32[]{:S(2)}, u32[]{:S(2)}) collective-permute-start(f32[2,5,8,128]{3,2,1,0:T(8,128)S(1)} %get-tuple-element.115.refs_4_), channel_id=1, source_target_pairs={{0,1},{1,0},{2,3},{3,2},{4,5},{5,4},{6,7},{7,6},{8,9},{9,8},{10,11... | collective-permute-start | bytes 122888 | tf_op jit(solution)/shard_map/ppermute | solution.py:635
  27.9 8.3 %collective-permute-start.14 = (f32[13,8,128]{2,1,0:T(8,128)S(1)}, f32[13,8,128]{2,1,0:T(8,128)S(1)}, u32[]{:S(2)}, u32[]{:S(2)}) collective-permute-start(f32[13,8,128]{2,1,0:T(8,128)S(1)} %get-tuple-element.129), channel_id=1, source_target_pairs={{0,4},{1,5},{2,6},{3,7},{4,0},{5,1},{6,2},{7,3},{8,12},{9,13},{10,... | collective-permute-start | bytes 159752 | tf_op jit(solution)/shard_map/ppermute | solution.py:635
  30.8 5.6 %collective-permute-start.15 = (f32[13,8,128]{2,1,0:T(8,128)S(1)}, f32[13,8,128]{2,1,0:T(8,128)S(1)}, u32[]{:S(2)}, u32[]{:S(2)}) collective-permute-start(f32[13,8,128]{2,1,0:T(8,128)S(1)} %get-tuple-element.130), channel_id=1, source_target_pairs={{0,4},{1,5},{2,6},{3,7},{4,0},{5,1},{6,2},{7,3},{8,12},{9,13},{10,... | collective-permute-start | bytes 159752 | tf_op jit(solution)/shard_map/ppermute | solution.py:635
  31.8 4.9 %collective-permute-start.16 = (f32[5,8,128]{2,1,0:T(8,128)S(1)}, f32[5,8,128]{2,1,0:T(8,128)S(1)}, u32[]{:S(2)}, u32[]{:S(2)}) collective-permute-start(f32[5,8,128]{2,1,0:T(8,128)S(1)} %join_vectors.3._.refs_10_), channel_id=1, source_target_pairs={{0,4},{1,5},{2,6},{3,7},{4,0},{5,1},{6,2},{7,3},{8,12},{9,13},{10,... | collective-permute-start | bytes 61448 | tf_op jit(solution)/shard_map/ppermute | solution.py:635
